TPU v7x, 32 devices: a whole 2x2x4 slice. The times are simulated.
32 devices in a mesh: groups: 2 (over y), wide: 4 (over z), narrow: 4 (over x, core).
Axes of the slice: x: 2, y: 2, z: 4, core: 2. Of those that a mesh axis runs over, the one named last changes fastest.
Arguments:
- activations: bfloat16 [2048, 8192], P(('groups', 'wide'), 'narrow'), parts along dimension 0, may hold values from -6 to 6
- request_tenants: int32 [2048, 1], P(('groups', 'wide')), parts along dimension 0, may hold values from 0 to 63; in each aligned block of 256 rows (0 to 255, 256 to 511, ...) at most 16 rows name the same one
- adapter_slot: int32 [64], replicated, may hold values from 0 to 63, each once
- shared_weight: bfloat16 [8192, 2048], P(None, 'narrow'), may hold values from -0.0625 to 0.0625
- adapter_down_weight: bfloat16 [64, 8192, 128], P('wide', 'narrow'), may hold values from -0.0625 to 0.0625
- adapter_up_weight: bfloat16 [64, 64, 2048], P('wide', None, 'narrow'), may hold values from -0.75 to 0.75
Outputs:
- projected: bfloat16 [2048, 2048], P(('groups', 'wide'), 'narrow'), parts along dimension 0
There are 2 independent parts, one for each index of `groups`. A program takes and returns all parts, laid end to end along the dimension named above; an argument that names none is the same for every part. Nothing has to cross between parts.
Inputs may be any that keep to these rules, and one draw needn't show every extreme that they name: `request_tenants`: in each aligned block of 256 rows (the rows of one device) no tenant is named by more than 16 rows, a bound that some block reaches; every tenant is named by some row. `adapter_slot`: A permutation of the tenants.
All inputs are finite; a program needn't handle non-finite values.
Results may differ from a plain program's by a relative error of at most 0.007.
Values may be sent and summed in bfloat16 or wider, within the bound.
No kernel may reach another device: no remote copies, remote signals or barrier semaphores. Data moves between devices by JAX's collectives and lax.ppermute only.
A program may use at most 128 MiB of HBM per device.

v0:
```python
import functools

import jax
import jax.numpy as jnp
from jax import lax
from jax.experimental import pallas as pl
from jax.experimental.pallas import tpu as pltpu
from jax.sharding import PartitionSpec as P

KEY_VALUE_COLS = 1024
LANES = 128
MOST = 16
OWN_ROWS = 112
AWAY_ROWS = 96
LATER_ROWS = 32
VMEM = pltpu.VMEM
MIB = 1 << 20

f32, bf16, i32 = jnp.float32, jnp.bfloat16, jnp.int32


def first_turn(wide_size, local_count):
    most = -(-(local_count * MOST + 1) // 32) * 32
    return [(k, 0, min(AWAY_ROWS if k else OWN_ROWS, most)) for k in reversed(range(wide_size))]


def ends(blocks, wide_size):
    return [max(start + count - 1 for j, start, count in blocks if j == k) for k in range(wide_size)]


def swap(x, axis, k):
    size = lax.axis_size(axis)
    return lax.ppermute(x, axis, [(i, i ^ k) for i in range(size)])


def after(x, *others):
    return lax.optimization_barrier((x, *others))[0]


def after_all(xs, *others):
    return lax.optimization_barrier((xs, others))[0]


def cost(flops, bytes_accessed, scale=0.001):
    return pl.CostEstimate(
        flops=int(flops * scale), bytes_accessed=int(bytes_accessed * scale), transcendentals=0
    )


def params(mib):
    return pltpu.CompilerParams(vmem_limit_bytes=mib * MIB)


def in_hbm(x):
    return pltpu.with_memory_space_constraint(x, pltpu.HBM)


def pack_kernel(
    local_count, wide_size, layout, span, per_turn, where_ref, tenant_ref, slot_ref, act_ref, *refs
):
    picked = range(*span)
    begun_ref, refs = refs[0], refs[1:]
    last_span = span[1] == len(layout)
    place_ref, refs = (refs[0], refs[1:]) if last_span else (None, refs)
    blocks = dict(zip(picked, refs[:-2]))
    act_held, in_sem = refs[-2:]
    rows, features = act_held.shape
    chunks = 4
    width = features // chunks
    loads = in_sem.shape[0]

    def load(n):
        part = pl.ds(n * (rows // loads), rows // loads)
        return pltpu.make_async_copy(act_ref.at[part, :], act_held.at[part, :], in_sem.at[n])

    for n in range(loads):
        load(n).start()
    begun_ref[0, 0] = jnp.int32(1)

    tenants = slot_ref.shape[1]
    tenant = tenant_ref[...]
    named = tenant == lax.broadcasted_iota(i32, (tenants, rows), 0)
    slots = jnp.broadcast_to(slot_ref[...].astype(f32), (8, tenants)).astype(bf16)
    slot = jnp.dot(slots, named.astype(f32).astype(bf16), preferred_element_type=f32)[:1]
    dest = jnp.floor((slot + 0.5) * (1.0 / local_count))
    adapter = slot - dest * local_count + 1.0
    leap = jnp.bitwise_xor(dest.astype(i32), where_ref[0])
    padded = max(8, wide_size)
    goes = (leap == lax.broadcasted_iota(i32, (padded, rows), 0)).astype(f32)
    earlier = lax.broadcasted_iota(i32, (rows, rows), 0) < lax.broadcasted_iota(
        i32, (rows, rows), 1
    )
    before = jnp.dot(
        goes.astype(bf16), earlier.astype(f32).astype(bf16), preferred_element_type=f32
    )
    position = jnp.sum(goes * before, axis=0, keepdims=True).astype(i32)
    adapters = jnp.broadcast_to(adapter, (8, rows)).astype(bf16)
    place = jnp.full((1, rows), -1, i32)
    more = jnp.zeros((1, rows), f32)
    position = position - where_ref[2] * per_turn
    for k, end in enumerate(ends(layout, wide_size)):
        more = jnp.where((leap == k) & (position >= end), 1.0, more)
    offset, here = 0, []
    for k, start, count in layout:
        mine = position - start
        mine = jnp.where((leap == k) & (mine >= 0) & (mine < count - 1), mine, -1)
        place = jnp.where(mine >= 0, mine + offset, place)
        offset += count
        here.append(mine)
    any_more = jnp.max(more, axis=1, keepdims=True)

    perm = jnp.concatenate(
        [
            (lax.broadcasted_iota(i32, (LANES, rows), 0) == here[n]).astype(f32).astype(bf16)
            for n in picked
        ],
        axis=0,
    )
    all_ids = lax.dot_general(
        adapters, perm, (((1,), (1,)), ((), ())), preferred_element_type=f32
    )
    lane = lax.broadcasted_iota(i32, (1, LANES), 1)
    for n in range(loads):
        load(n).wait()
    for c in range(chunks):
        cols = pl.ds(c * width, width)
        body = jnp.dot(perm, act_held[:, cols], preferred_element_type=f32)
        for m, n in enumerate(picked):
            count = layout[n][2]
            part = body[m * LANES : m * LANES + count]
            if c == 0:
                ids = all_ids[:1, m * LANES : (m + 1) * LANES]
                ids = jnp.where(lane == LANES - 1, any_more, ids)
                last = lax.broadcasted_iota(i32, (count, LANES), 0) == count - 1
                first = jnp.where(last, ids, part[:, :LANES])
                part = jnp.concatenate([first, part[:, LANES:]], axis=1)
            blocks[n][:, cols] = part.astype(bf16)
    if last_span:
        place_ref[...] = jnp.broadcast_to(place.astype(f32), (LANES, rows)).T


def pack(where, tenant, slot, activations, local_count, wide_size, layout, span, per_turn):
    rows, features = activations.shape
    counts = [count for _, _, count in layout[slice(*span)]]
    places = [jax.ShapeDtypeStruct((rows, LANES), f32)] if span[1] == len(layout) else []
    loads = 4
    whole = pl.BlockSpec(memory_space=VMEM)
    scalar = pl.BlockSpec(memory_space=pltpu.SMEM)
    return pl.pallas_call(
        functools.partial(pack_kernel, local_count, wide_size, layout, span, per_turn),
        out_shape=[
            jax.ShapeDtypeStruct((1, 1), i32),
            *places,
        ]
        + [pltpu.VMEM((c, features), bf16) for c in counts],
        in_specs=[scalar, whole, whole, pl.BlockSpec(memory_space=pltpu.HBM)],
        out_specs=[scalar] + [whole for _ in [*places, *counts]],
        scratch_shapes=[VMEM((rows, features), bf16), pltpu.SemaphoreType.DMA((loads,))],
        compiler_params=params(12),
        cost_estimate=cost(2 * sum(counts) * rows * features, 2 * features * (rows + sum(counts))),
        name="pack_rows",
    )(where, tenant, slot, in_hbm(activations))


def stage_kernel(down_ref, up_ref, down_out, up_out, sem):
    adapters, _, width = down_ref.shape
    copies = [
        pltpu.make_async_copy(
            down_ref.at[j], down_out.at[:, pl.ds(j * width, width)], sem.at[j]
        )
        for j in range(adapters)
    ]
    copies.append(pltpu.make_async_copy(up_ref, up_out, sem.at[adapters]))
    for copy in copies:
        copy.start()
    for copy in copies:
        copy.wait()


def stage(down_weight, up_weight):
    adapters, features, width = down_weight.shape
    whole = pl.BlockSpec(memory_space=VMEM)
    return pl.pallas_call(
        stage_kernel,
        out_shape=[
            pltpu.VMEM((features, adapters * width), down_weight.dtype),
            pltpu.VMEM(up_weight.shape, up_weight.dtype),
        ],
        in_specs=[pl.BlockSpec(memory_space=pltpu.HBM)] * 2,
        out_specs=[whole, whole],
        scratch_shapes=[pltpu.SemaphoreType.DMA((adapters + 1,))],
        compiler_params=params(12),
        cost_estimate=cost(10, 10),
        name="stage_maps",
    )(in_hbm(down_weight), in_hbm(up_weight))


def down_kernel(count, cols, narrow_size, per_step, where_ref, weight_ref, *refs):
    xs, refs = refs[:count], refs[count:]
    before, refs = (refs[:3], refs[3:]) if narrow_size else ((), refs)
    flag_ref, ids_ref, *outs, held_ref = refs
    steps = weight_ref.shape[1] // (per_step * LANES)

    flag = jnp.zeros((1, LANES), f32)
    ids = []
    offset = 0
    for x in xs:
        rows = x.shape[0]
        held_ref[pl.ds(offset, rows), :] = x[...]
        last = x[pl.ds(rows - 16, 16), :LANES].astype(f32)[15:]
        flag = jnp.maximum(flag, last)
        turned = jnp.broadcast_to(last, (LANES, LANES)).T[:rows]
        keep = lax.broadcasted_iota(i32, (rows, LANES), 0) < rows - 1
        ids.append(jnp.where(keep, turned, 0.0))
        offset += rows
    ids = jnp.concatenate(ids, axis=0)
    lane = lax.broadcasted_iota(i32, (1, LANES), 1)
    flag = jnp.max(jnp.where(lane == LANES - 1, flag, 0.0)).astype(i32)

    total = jnp.zeros(ids.shape, f32)
    for c in range(steps):
        weights = weight_ref[:, c * per_step * LANES : (c + 1) * per_step * LANES]
        found = jnp.dot(held_ref[...], weights, preferred_element_type=f32)
        for j in range(per_step):
            name = c * per_step + j + 1.0
            total = jnp.where(ids == name, found[:, j * LANES : (j + 1) * LANES], total)

    if not narrow_size:
        flag_ref[0, 0] = flag
        ids_ref[...] = ids
        outs[0][...] = total
        return
    if before:
        flag = jnp.maximum(flag, before[0][0, 0])
        ids = jnp.concatenate([before[1][...], ids], axis=0)
        total = jnp.concatenate([before[2][...], total], axis=0)
    flag_ref[0, 0] = flag
    padding = jnp.zeros((ids_ref.shape[0] - ids.shape[0], LANES), f32)
    if padding.shape[0]:
        ids = jnp.concatenate([ids, padding], axis=0)
        total = jnp.concatenate([total, padding], axis=0)
    ids_ref[...] = ids
    half = total.shape[0] // 2
    rank = LANES // 2
    top, bottom = total[:half], total[half:]
    low = lax.broadcasted_iota(i32, (half, LANES), 1) < rank
    keys = jnp.where(low, top, pltpu.roll(bottom, rank, 1))
    values = jnp.where(low, pltpu.roll(top, rank, 1), bottom)
    for j in range(narrow_size):
        start = jnp.bitwise_xor(where_ref[1], j) * cols
        outs[j][...] = jnp.where(start >= KEY_VALUE_COLS, values, keys).astype(outs[j].dtype)


def down(where, blocks, weight, cols, before, narrow_size, scale):
    features, width = weight.shape
    new_rows = sum(b.shape[0] for b in blocks)
    per_step = min(4, width // LANES)
    whole = pl.BlockSpec(memory_space=VMEM)
    scalar = pl.BlockSpec(memory_space=pltpu.SMEM)
    if narrow_size:
        rows = -(-(new_rows + before[1].shape[0]) // 32) * 32
        sums = [((rows // 2, LANES), bf16 if j else f32) for j in range(narrow_size)]
    else:
        rows = new_rows
        sums = [((rows, LANES), f32)]
    return pl.pallas_call(
        functools.partial(down_kernel, len(blocks), cols, narrow_size, per_step),
        out_shape=[
            jax.ShapeDtypeStruct((1, 1), i32),
            jax.ShapeDtypeStruct((rows, LANES), f32),
        ]
        + [jax.ShapeDtypeStruct(*s) for s in sums],
        in_specs=[scalar, whole]
        + [whole for _ in blocks]
        + ([scalar, whole, whole] if narrow_size else []),
        out_specs=[scalar, whole] + [whole for _ in sums],
        scratch_shapes=[VMEM((new_rows, features), bf16)],
        compiler_params=params(18),
        cost_estimate=cost(
            2 * new_rows * features * width, 2 * features * (new_rows + width), scale
        ),
        name="down_maps",
    )(where, weight, *blocks, *(before if narrow_size else []))


def up_kernel(narrow_size, ids_ref, *refs):
    parts, weight_ref, outs = refs[:narrow_size], refs[narrow_size], refs[narrow_size + 1 :]
    total = parts[0][...]
    for part in parts[1:]:
        total = total + part[...].astype(f32)
    low_rank = total.astype(bf16).astype(f32)
    rank = LANES // 2
    turned = pltpu.roll(low_rank, rank, 1)
    low = lax.broadcasted_iota(i32, low_rank.shape, 1) < rank
    twice = jnp.concatenate(
        [jnp.where(low, low_rank, turned), jnp.where(low, turned, low_rank)], axis=0
    )
    ids = ids_ref[...]
    second = (lax.broadcasted_iota(i32, ids.shape, 1) >= rank).astype(f32)
    adapters = weight_ref.shape[0] // rank
    left = [
        jnp.where(ids - second == 2.0 * pair + 1.0, twice, 0.0).astype(bf16)
        for pair in range(adapters // 2)
    ]
    found = jnp.dot(jnp.concatenate(left, axis=1), weight_ref[...], preferred_element_type=f32)
    offset = 0
    for out in outs:
        rows = out.shape[0]
        out[...] = found[offset : offset + rows].astype(bf16)
        offset += rows


def up(ids, parts, weight, counts):
    cols = weight.shape[1]
    return pl.pallas_call(
        functools.partial(up_kernel, len(parts)),
        out_shape=[jax.ShapeDtypeStruct((c, cols), bf16) for c in counts],
        compiler_params=params(10),
        cost_estimate=cost(2 * sum(counts) * weight.size, 2 * weight.size + 2 * sum(counts) * (cols + 512)),
        name="up_maps",
    )(ids, *parts, weight)


def base_kernel(count, where_ref, *refs):
    acts, weight_ref, so_far, out_ref = refs[:count], refs[count], refs[count + 1 : -1], refs[-1]
    step = pl.program_id(0)
    for j in range(count):

        @pl.when(step == j)
        def _(j=j):
            found = jnp.dot(acts[j][...], weight_ref[...], preferred_element_type=f32)
            if j:
                found = out_ref[...] + found
            elif so_far:
                found = so_far[0][...] + found
            out_ref[...] = found


def base(where, acts, first, weight, so_far):
    rows, features = acts[0].shape
    cols = weight.shape[1]
    count = len(acts)
    given = [] if so_far is None else [so_far]
    return pl.pallas_call(
        functools.partial(base_kernel, count),
        grid_spec=pltpu.PrefetchScalarGridSpec(
            num_scalar_prefetch=1,
            grid=(count,),
            in_specs=[pl.BlockSpec((rows, features), lambda i, where: (0, 0)) for _ in acts]
            + [
                pl.BlockSpec(
                    (features, cols),
                    lambda i, where: (jnp.bitwise_xor(where[1], first + i), 0),
                )
            ]
            + [pl.BlockSpec((rows, cols), lambda i, where: (0, 0)) for _ in given],
            out_specs=pl.BlockSpec((rows, cols), lambda i, where: (0, 0)),
        ),
        out_shape=jax.ShapeDtypeStruct((rows, cols), f32),
        compiler_params=params(14),
        cost_estimate=cost(2 * rows * features * count * cols, 2 * features * count * (cols + rows)),
        name="shared_projection",
    )(where, *acts, in_hbm(weight), *given)


def join_kernel(base_ref, place_ref, *refs):
    corrections, out_ref, held_ref, sem = refs[:-3], *refs[-3:]
    stacked = jnp.concatenate([c[...] for c in corrections], axis=0)
    rows, count = base_ref.shape[0], stacked.shape[0]
    parts = sem.shape[0]
    copies = []
    for n in range(parts):
        part = pl.ds(n * (rows // parts), rows // parts)
        place = place_ref[part, :1].astype(i32)
        perm = lax.broadcasted_iota(i32, (rows // parts, count), 1) == place
        found = jnp.dot(perm.astype(f32).astype(bf16), stacked, preferred_element_type=f32)
        held_ref[part, :] = (base_ref[part, :] + found).astype(out_ref.dtype)
        copy = pltpu.make_async_copy(held_ref.at[part, :], out_ref.at[part, :], sem.at[n])
        copy.start()
        copies.append(copy)
    for copy in copies:
        copy.wait()


def join(base_out, place, corrections, dtype):
    rows, cols = base_out.shape
    count = sum(c.shape[0] for c in corrections)
    parts = 2
    return pl.pallas_call(
        join_kernel,
        out_shape=pltpu.HBM((rows, cols), dtype),
        in_specs=[pl.BlockSpec(memory_space=VMEM)] * (2 + len(corrections)),
        out_specs=pl.BlockSpec(memory_space=pltpu.HBM),
        scratch_shapes=[VMEM((rows, cols), dtype), pltpu.SemaphoreType.DMA((parts,))],
        compiler_params=params(10),
        cost_estimate=cost(2 * rows * cols * count, 2 * cols * (count + 3 * rows)),
        name="join_corrections",
    )(base_out, place, *corrections)


def raise_sums(ids, sums, up_weight, counts):
    sums = [swap(part, "narrow", j) if j else part for j, part in enumerate(sums)]
    return up(ids, sums, up_weight, counts)


def later_turn(turn, axes, total, done, tenant, slot, activations, down_weight, up_weight):
    wide_size, narrow_size = lax.axis_size("wide"), lax.axis_size("narrow")
    where = jnp.stack([*axes, turn])
    layout = [(k, end, LATER_ROWS) for k, end in enumerate(done)]
    _, place, *sent = pack(
        where,
        tenant,
        slot,
        activations,
        down_weight.shape[0],
        wide_size,
        layout,
        (0, wide_size),
        LATER_ROWS - 1,
    )
    got = [swap(b, "wide", k) if k else b for k, b in enumerate(sent)]
    cols = up_weight.shape[1]
    down_weight, up_weight = stage(down_weight, up_weight)
    before = down(where, got[:1], down_weight, cols, None, 0, 0.001)
    more, ids, *sums = down(where, got[1:], down_weight, cols, before, narrow_size, 0.001)
    outs = raise_sums(ids, sums, up_weight, [b.shape[0] for b in got])
    answers = [swap(b, "wide", k) if k else b for k, b in enumerate(outs)]
    return join(total, place, answers, f32), more[0, 0]


def on_device(
    activations,
    request_tenants,
    adapter_slot,
    shared_weight,
    adapter_down_weight,
    adapter_up_weight,
):
    rows = activations.shape[0]
    wide_size, narrow_size = lax.axis_size("wide"), lax.axis_size("narrow")
    local_count = adapter_down_weight.shape[0]
    axes = (lax.axis_index("wide").astype(i32), lax.axis_index("narrow").astype(i32))
    where = jnp.stack([*axes, jnp.int32(0)])
    tenant = request_tenants.reshape(1, rows)
    slot = adapter_slot.reshape(1, -1)
    up_weight = adapter_up_weight.reshape(-1, adapter_up_weight.shape[-1])

    cols = up_weight.shape[1]
    layout = first_turn(wide_size, local_count)
    own = len(layout) - 1
    routed = (local_count, wide_size, layout)
    begun, *sent = pack(where, tenant, slot, activations, *routed, (0, 1), 0)
    if own > 1:
        sent += pack(where, tenant, slot, after(activations, *sent), *routed, (1, own), 0)[1:]
    got = [swap(b, "wide", k) for (k, _, _), b in zip(layout, sent)]
    half = narrow_size // 2

    def step(work, *operands):
        def never(*operands):
            return jax.tree.map(
                lambda s: jnp.zeros(s.shape, s.dtype), jax.eval_shape(work, *operands)
            )

        return lax.cond(begun[0, 0] > 0, work, never, *operands)

    def spread(act):
        acts, bit = {0: act}, half // 2
        while bit:
            acts.update({j ^ bit: swap(x, "narrow", bit) for j, x in list(acts.items())})
            bit //= 2
        return [acts[j] for j in sorted(acts)]

    def pack_own(tenant, slot, activations):
        return pack(where, tenant, slot, activations, *routed, (own, own + 1), 0)[1:]

    def work_before(activations, shared_weight, maps):
        return base(where, spread(activations), 0, shared_weight, None), stage(*maps)

    def work_after(across, shared_weight, base_out):
        for n, act in enumerate(spread(across)):
            base_out = base(where, [act], half + n, shared_weight, base_out)
        return base_out

    shared_weight, maps = after_all((shared_weight, (adapter_down_weight, up_weight)), *sent)
    place, own_block = step(pack_own, tenant, slot, after(activations, *sent))
    across = swap(after(activations, own_block), "narrow", half) if half else None
    base_out, (down_beside, up_beside) = step(
        work_before, *after_all((activations, shared_weight, maps), own_block)
    )
    before = down(where, [got[0], after(own_block, base_out)], down_beside, cols, None, 0, 0.001)
    more, ids, *sums = down(
        where, after_all(got[1:], *before), down_beside, cols, before, narrow_size, 20
    )
    counts = [layout[n][2] for n in (0, own, *range(1, own))]
    outs = raise_sums(ids, sums, up_beside, counts)
    outs = [outs[0], *outs[2:], outs[1]]
    answers = [swap(b, "wide", k) if k else b for (k, _, _), b in zip(layout, outs)]
    if half:
        base_out = step(work_after, *after_all((across, shared_weight, base_out), *outs))
    more = more[0, 0]

    def done(base_out):
        return join(base_out, place, answers, bf16)

    def go_on(base_out):
        def turn_of(state):
            turn, _, total = state
            total, more = later_turn(
                turn, axes, total, ends(layout, wide_size), tenant, slot, activations, adapter_down_weight, up_weight
            )
            return turn + 1, more, total

        state = (jnp.int32(0), jnp.int32(1), join(base_out, place, answers, f32))
        return lax.while_loop(lambda s: s[1] > 0, turn_of, state)[2].astype(bf16)

    return lax.cond(more > 0, go_on, done, base_out)


def solution(mesh):
    in_specs = (
        P(("groups", "wide"), "narrow"),
        P(("groups", "wide"), None),
        P(),
        P(None, "narrow"),
        P("wide", "narrow", None),
        P("wide", None, "narrow"),
    )
    out_specs = P(("groups", "wide"), "narrow")
    return jax.shard_map(
        on_device, mesh=mesh, in_specs=in_specs, out_specs=out_specs, check_vma=False
    )
```

profile of v0, /device:TPU:0, one launch (start us, length us, event | category | flops | bytes accessed | tf_op | source)
XLA Modules:
  0.0 64.3 jit_solution(16304074643193342680)
XLA Ops:
  0.1 3.0 %pack_rows.9 = (s32[1,1]{1,0:T(1,128)}, bf16[96,2048]{1,0:T(8,128)(2,1)}) custom-call(s32[3]{0:T(128)S(1)} %pad_add_fusion.1.where_ref, s32[1,256]{1,0:T(1,128)} %bitcast.21, s32[1,64]{1,0:T(1,128)} %bitcast.25, bf16[256,2048]{1,0:T(8,128)(2,1)} %act_ref.2), custom_call_target="tpu_custom_call" | custom-call | flops 100663 | bytes 1441 | tf_op jit(solution)/shard_map/pack_rows/pallas_call | solution.py:149
  3.1 5.1 %collective-permute-start.13 = (bf16[96,2048]{1,0:T(8,128)(2,1)}, bf16[96,2048]{1,0:T(8,128)(2,1)S(1)}, u32[]{:S(2)}, u32[]{:S(2)}) collective-permute-start(bf16[96,2048]{1,0:T(8,128)(2,1)} %get-tuple-element.388), channel_id=1, source_target_pairs={{0,12},{4,8},{8,4},{12,0},{1,13},{5,9},{9,5},{13,1},{2,14},{6,10},... | collective-permute-start | bytes 1179656 | tf_op jit(solution)/shard_map/ppermute | solution.py:33
  8.2 2.4 %pack_rows.10 = (s32[1,1]{1,0:T(1,128)}, bf16[96,2048]{1,0:T(8,128)(2,1)S(1)}, bf16[96,2048]{1,0:T(8,128)(2,1)S(1)}) custom-call(s32[3]{0:T(128)S(1)} %pad_add_fusion.1.where_ref, s32[1,256]{1,0:T(1,128)} %bitcast.22, s32[1,64]{1,0:T(1,128)} %bitcast.26, bf16[256,2048]{1,0:T(8,128)(2,1)} %act_ref.2), custom_call_target="tpu_custom_call" | custom-call | flops 201326 | bytes 1835 | tf_op jit(solution)/shard_map/pack_rows/pallas_call | solution.py:149
  10.7 0.6 collective-permute-start.12
  11.9 2.9 %conditional.4 = (f32[256,128]{1,0:T(8,128)}, bf16[112,2048]{1,0:T(8,128)(2,1)S(1)}) conditional(s32[]{:T(128)} %bitcast.8, () %tuple.66, (s32[3]{0:T(128)S(1)}, s32[1,256]{1,0:T(1,128)}, s32[1,64]{1,0:T(1,128)}, bf16[256,2048]{1,0:T(8,128)(2,1)}) %tuple.107), branch_computations={%region_0.0_spmd, %region_1.0_spmd} | conditional | flops 117440 | bytes 589846 | solution.py:464
  11.9 2.8 %pack_rows.8 = (s32[1,1]{1,0:T(1,128)}, f32[256,128]{1,0:T(8,128)}, bf16[112,2048]{1,0:T(8,128)(2,1)S(1)}) custom-call(s32[3]{0:T(128)S(1)} %get-tuple-element.282.where_ref, s32[1,256]{1,0:T(1,128)} %get-tuple-element.283.tenant_ref, s32[1,64]{1,0:T(1,128)} %get-tuple-element.284.slot_ref, bf16[256,2048]{1,0:T(8,128)(2,1)} %get-tuple-element.285.act_ref), custom_call_target="tpu_custom_call" | custom-call | flops 117440 | bytes 1507 | tf_op jit(solution)/shard_map/cond/branch_1_fun/pack_rows/pallas_call | solution.py:149
  14.8 1.8 %collective-permute-start.14 = (bf16[256,2048]{1,0:T(8,128)(2,1)}, bf16[256,2048]{1,0:T(8,128)(2,1)}, u32[]{:S(2)}, u32[]{:S(2)}) collective-permute-start(bf16[256,2048]{1,0:T(8,128)(2,1)} %act_ref.2), channel_id=1, source_target_pairs={{0,2},{1,3},{2,0},{3,1},{4,6},{5,7},{6,4},{7,5},{8,10},{9,11},{10,... | collective-permute-start | bytes 3145736 | tf_op jit(solution)/shard_map/ppermute | solution.py:33
  16.5 7.8 %conditional.5 = (f32[256,512]{1,0:T(8,128)S(1)}, bf16[2048,2048]{1,0:T(8,128)(2,1)S(1)}, bf16[1024,512]{1,0:T(8,128)(2,1)S(1)}) conditional(s32[]{:T(128)} %bitcast.8, () %tuple.63, (bf16[256,2048]{1,0:T(8,128)(2,1)}, s32[3]{0:T(128)S(1)}, bf16[8192,512]{1,0:T(8,128)(2,1)}, bf16[16,2048,128]{2,1,0:T(8,128)(2,1)}, bf16[1024,512]{1,0:T(8,128)(2,1)}) %tuple.101), branch_computations={%region_2.0_spmd, %region_3.0_spmd} | conditional | flops 1073741 | bytes 9961504 | solution.py:464
  16.5 3.9 %stage_maps.4 = (bf16[2048,2048]{1,0:T(8,128)(2,1)S(1)}, bf16[1024,512]{1,0:T(8,128)(2,1)S(1)}) custom-call(bf16[16,2048,128]{2,1,0:T(8,128)(2,1)} %get-tuple-element.291.down_ref, bf16[1024,512]{1,0:T(8,128)(2,1)} %get-tuple-element.292.up_ref), custom_call_target="tpu_custom_call" | custom-call | tf_op jit(solution)/shard_map/cond/branch_1_fun/stage_maps/pallas_call | solution.py:183
  20.4 3.9 %shared_projection.3 = f32[256,512]{1,0:T(8,128)S(1)} custom-call(s32[3]{0:T(128)S(1)} %get-tuple-element.288.where_ref, bf16[256,2048]{1,0:T(8,128)(2,1)} %get-tuple-element.289.refs_0_, bf16[256,2048]{1,0:T(8,128)(2,1)S(1)} %collective-permute-done.refs_1_, bf16[8192,512]{1,0:T(8,128)(2,1)} %get-tuple-element.290.refs_2_), custom_call_target="tpu_custom_call" | custom-call | flops 1073741 | bytes 6291 | tf_op jit(solution)/shard_map/cond/branch_1_fun/shared_projection/pallas_call | solution.py:344
  24.3 2.9 %down_maps.12 = (s32[1,1]{1,0:T(1,128)}, f32[208,128]{1,0:T(8,128)S(1)}, f32[208,128]{1,0:T(8,128)S(1)}) custom-call(s32[3]{0:T(128)S(1)} %pad_add_fusion.1.where_ref, bf16[2048,2048]{1,0:T(8,128)(2,1)S(1)} %get-tuple-element.401.weight_ref, bf16[96,2048]{1,0:T(8,128)(2,1)S(1)} %collective-permute-done.13.refs_0_, ...), custom_call_target="tpu_custom_call" | custom-call | flops 1744830 | bytes 9240 | tf_op jit(solution)/shard_map/down_maps/pallas_call | solution.py:266
  27.2 14.7 %collective-permute-done.11.refs_0_ = bf16[96,2048]{1,0:T(8,128)(2,1)S(1)} collective-permute-done((bf16[96,2048]{1,0:T(8,128)(2,1)S(1)}, bf16[96,2048]{1,0:T(8,128)(2,1)S(1)}, u32[]{:S(2)}, u32[]{:S(2)}) %collective-permute-start.11) | collective-permute-done | bytes 393248 | tf_op jit(solution)/shard_map/ppermute | solution.py:33
  41.9 3.5 %down_maps.13 = (s32[1,1]{1,0:T(1,128)}, f32[416,128]{1,0:T(8,128)S(1)}, f32[208,128]{1,0:T(8,128)S(1)}, bf16[208,128]{1,0:T(8,128)(2,1)S(1)}, bf16[208,128]{1,0...) custom-call(s32[3]{0:T(128)S(1)} %pad_add_fusion.1.where_ref, bf16[2048,2048]{1,0:T(8,128)(2,1)S(1)} %get-tuple-element.401.weight_ref, ...), custom_call_target="tpu_custom_call" | custom-call | flops 32212254720 | bytes 183500800 | tf_op jit(solution)/shard_map/down_maps/pallas_call | solution.py:266
  45.5 1.5 %collective-permute-start.16 = (bf16[208,128]{1,0:T(8,128)(2,1)S(1)}, bf16[208,128]{1,0:T(8,128)(2,1)S(1)}, u32[]{:S(2)}, u32[]{:S(2)}) collective-permute-start(bf16[208,128]{1,0:T(8,128)(2,1)S(1)} %get-tuple-element.414), channel_id=1, source_target_pairs={{0,2},{1,3},{2,0},{3,1},{4,6},{5,7},{6,4},{7,5},{8,10},{9,11},{10,... | collective-permute-start | bytes 159752 | tf_op jit(solution)/shard_map/ppermute | solution.py:33
  47.4 2.4 %collective-permute-done.16.refs_2_ = bf16[208,128]{1,0:T(8,128)(2,1)S(1)} collective-permute-done((bf16[208,128]{1,0:T(8,128)(2,1)S(1)}, bf16[208,128]{1,0:T(8,128)(2,1)S(1)}, u32[]{:S(2)}, u32[]{:S(2)}) %collective-permute-start.16) | collective-permute-done | bytes 53280 | tf_op jit(solution)/shard_map/ppermute | solution.py:33
  49.8 1.1 %collective-permute-done.17.refs_3_ = bf16[208,128]{1,0:T(8,128)(2,1)S(1)} collective-permute-done((bf16[208,128]{1,0:T(8,128)(2,1)S(1)}, bf16[208,128]{1,0:T(8,128)(2,1)S(1)}, u32[]{:S(2)}, u32[]{:S(2)}) %collective-permute-start.17) | collective-permute-done | bytes 53280 | tf_op jit(solution)/shard_map/ppermute | solution.py:33
  50.9 0.6 %up_maps.6 = (bf16[96,512]{1,0:T(8,128)(2,1)S(1)}, bf16[112,512]{1,0:T(8,128)(2,1)S(1)}, bf16[96,512]{1,0:T(8,128)(2,1)S(1)}, bf16[96,512]{1,0:T(8,128)(2,1)S(1)}) custom-call(f32[416,128]{1,0:T(8,128)S(1)} %get-tuple-element.411.ids_ref, f32[208,128]{1,0:T(8,128)S(1)} %get-tuple-element.412.refs_0_, bf16[208,128]{1,0:T(8,128)(2,1)S(1)} %collective-permute-done.15.refs_1_, ...), custom_call_target="tpu_custom_call" | custom-call | flops 419430 | bytes 1867 | tf_op jit(solution)/shard_map/up_maps/pallas_call | solution.py:315
  51.5 2.5 %collective-permute-start.18 = (bf16[96,512]{1,0:T(8,128)(2,1)S(1)}, bf16[96,512]{1,0:T(8,128)(2,1)S(1)}, u32[]{:S(2)}, u32[]{:S(2)}) collective-permute-start(bf16[96,512]{1,0:T(8,128)(2,1)S(1)} %get-tuple-element.417), channel_id=1, source_target_pairs={{0,12},{4,8},{8,4},{12,0},{1,13},{5,9},{9,5},{13,1},{2,14},{6,10},... | collective-permute-start | bytes 294920 | tf_op jit(solution)/shard_map/ppermute | solution.py:33
  54.1 1.9 %collective-permute-start.20 = (bf16[96,512]{1,0:T(8,128)(2,1)S(1)}, bf16[96,512]{1,0:T(8,128)(2,1)S(1)}, u32[]{:S(2)}, u32[]{:S(2)}) collective-permute-start(bf16[96,512]{1,0:T(8,128)(2,1)S(1)} %get-tuple-element.419), channel_id=1, source_target_pairs={{0,4},{4,0},{8,12},{12,8},{1,5},{5,1},{9,13},{13,9},{2,6},{6,2},{1... | collective-permute-start | bytes 294920 | tf_op jit(solution)/shard_map/ppermute | solution.py:33
  56.7 6.1 %conditional.6 = (f32[256,512]{1,0:T(8,128)S(1)}) conditional(s32[]{:T(128)} %bitcast.8, () %tuple.73, (bf16[256,2048]{1,0:T(8,128)(2,1)}, s32[3]{0:T(128)S(1)}, bf16[8192,512]{1,0:T(8,128)(2,1)}, f32[256,512]{1,0:T(8,128)S(1)}) %tuple.76), branch_computations={%region_4.0_spmd, %region_5.0_spmd} | conditional | flops 1073740 | bytes 4200642 | solution.py:464
  56.8 3.2 %shared_projection.4.refs_2_ = f32[256,512]{1,0:T(8,128)S(1)} custom-call(s32[3]{0:T(128)S(1)} %get-tuple-element.295.where_ref, bf16[256,2048]{1,0:T(8,128)(2,1)} %get-tuple-element.296.refs_0_, bf16[8192,512]{1,0:T(8,128)(2,1)} %get-tuple-element.297.refs_1_, f32[256,512]{1,0:T(8,128)S(1)} %get-tuple-element.298.refs_2_), custom_call_target="tpu_custom_call" | custom-call | flops 536870 | bytes 3145 | tf_op jit(solution)/shard_map/cond/branch_1_fun/shared_projection/pallas_call | solution.py:344
  60.0 2.8 %shared_projection.5 = f32[256,512]{1,0:T(8,128)S(1)} custom-call(s32[3]{0:T(128)S(1)} %get-tuple-element.295.where_ref, bf16[256,2048]{1,0:T(8,128)(2,1)S(1)} %collective-permute-done.1.refs_0_, bf16[8192,512]{1,0:T(8,128)(2,1)} %get-tuple-element.297.refs_1_, f32[256,512]{1,0:T(8,128)S(1)} %shared_projection.4.refs_2_), custom_call_target="tpu_custom_call" | custom-call | flops 536870 | bytes 3145 | tf_op jit(solution)/shard_map/cond/branch_1_fun/shared_projection/pallas_call | solution.py:344
  62.9 1.2 %conditional.7 = (bf16[256,512]{1,0:T(8,128)(2,1)}) conditional(s32[]{:T(128)} %bitcast.10, (f32[256,512]{1,0:T(8,128)S(1)}, f32[256,128]{1,0:T(8,128)S(1)}, bf16[96,512]{1,0:T(8,128)(2,1)S(1)}, bf16[96,512]{1,0:T(8,128)(2,1)S(1)}, bf16[96,512]{1,0:T(8,128)(2,1)S(1)}, /*index=5*/bf16[112,512]{1,0:T(8,128)(2,1)S(1)}) %tuple.103, ...), branch_computations={%region_6.0_spmd, %region_7.0_spmd} | conditional | flops 1611666 | bytes 73226696 | solution.py:516
  62.9 1.0 %join_corrections.7 = bf16[256,512]{1,0:T(8,128)(2,1)} custom-call(f32[256,512]{1,0:T(8,128)S(1)} %get-tuple-element.299.base_ref, f32[256,128]{1,0:T(8,128)S(1)} %get-tuple-element.300.place_ref, bf16[96,512]{1,0:T(8,128)(2,1)S(1)} %get-tuple-element.301.refs_0_, bf16[96,512]{1,0:T(8,128)(2,1)S(1)} %get-tuple-element.302.refs_1_, ...), custom_call_target="tpu_custom_call" | custom-call | flops 104857 | bytes 1196 | tf_op jit(solution)/shard_map/cond/branch_0_fun/join_corrections/pallas_call | solution.py:389
  (22 shorter events, 0.7 us)
Async XLA Ops:
  3.1 21.2 %collective-permute-start.13 = (bf16[96,2048]{1,0:T(8,128)(2,1)}, bf16[96,2048]{1,0:T(8,128)(2,1)S(1)}, u32[]{:S(2)}, u32[]{:S(2)}) collective-permute-start(bf16[96,2048]{1,0:T(8,128)(2,1)} %get-tuple-element.388), channel_id=1, source_target_pairs={{0,12},{4,8},{8,4},{12,0},{1,13},{5,9},{9,5},{13,1},{2,14},{6,10},... | collective-permute-start | bytes 1179656 | tf_op jit(solution)/shard_map/ppermute | solution.py:33
  10.6 31.3 %collective-permute-start.11 = (bf16[96,2048]{1,0:T(8,128)(2,1)S(1)}, bf16[96,2048]{1,0:T(8,128)(2,1)S(1)}, u32[]{:S(2)}, u32[]{:S(2)}) collective-permute-start(bf16[96,2048]{1,0:T(8,128)(2,1)S(1)} %get-tuple-element.390), channel_id=1, source_target_pairs={{0,8},{4,12},{8,0},{12,4},{1,9},{5,13},{9,1},{13,5},{2,10},{6,14},... | collective-permute-start | bytes 1179656 | tf_op jit(solution)/shard_map/ppermute | solution.py:33
  10.7 31.2 %collective-permute-start.12 = (bf16[96,2048]{1,0:T(8,128)(2,1)S(1)}, bf16[96,2048]{1,0:T(8,128)(2,1)S(1)}, u32[]{:S(2)}, u32[]{:S(2)}) collective-permute-start(bf16[96,2048]{1,0:T(8,128)(2,1)S(1)} %get-tuple-element.391), channel_id=1, source_target_pairs={{0,4},{4,0},{8,12},{12,8},{1,5},{5,1},{9,13},{13,9},{2,6},{6,2},{1... | collective-permute-start | bytes 1179656 | tf_op jit(solution)/shard_map/ppermute | solution.py:33
  14.8 41.9 %collective-permute-start.14 = (bf16[256,2048]{1,0:T(8,128)(2,1)}, bf16[256,2048]{1,0:T(8,128)(2,1)}, u32[]{:S(2)}, u32[]{:S(2)}) collective-permute-start(bf16[256,2048]{1,0:T(8,128)(2,1)} %act_ref.2), channel_id=1, source_target_pairs={{0,2},{1,3},{2,0},{3,1},{4,6},{5,7},{6,4},{7,5},{8,10},{9,11},{10,... | collective-permute-start | bytes 3145736 | tf_op jit(solution)/shard_map/ppermute | solution.py:33
  16.5 3.9 %collective-permute-start = (bf16[256,2048]{1,0:T(8,128)(2,1)}, bf16[256,2048]{1,0:T(8,128)(2,1)S(1)}, u32[]{:S(2)}, u32[]{:S(2)}) collective-permute-start(bf16[256,2048]{1,0:T(8,128)(2,1)} %get-tuple-element.289.refs_0_), channel_id=1, source_target_pairs={{0,1},{1,0},{2,3},{3,2},{4,5},{5,4},{6,7},{7,6},{8,9},{9,8},{10,11... | collective-permute-start | bytes 3145736 | tf_op jit(solution)/shard_map/cond/branch_1_fun/ppermute | solution.py:33
  45.5 1.9 %collective-permute-start.15 = (bf16[208,128]{1,0:T(8,128)(2,1)S(1)}, bf16[208,128]{1,0:T(8,128)(2,1)S(1)}, u32[]{:S(2)}, u32[]{:S(2)}) collective-permute-start(bf16[208,128]{1,0:T(8,128)(2,1)S(1)} %get-tuple-element.413), channel_id=1, source_target_pairs={{0,1},{1,0},{2,3},{3,2},{4,5},{5,4},{6,7},{7,6},{8,9},{9,8},{10,11... | collective-permute-start | bytes 159752 | tf_op jit(solution)/shard_map/ppermute | solution.py:33
  45.5 4.2 %collective-permute-start.16 = (bf16[208,128]{1,0:T(8,128)(2,1)S(1)}, bf16[208,128]{1,0:T(8,128)(2,1)S(1)}, u32[]{:S(2)}, u32[]{:S(2)}) collective-permute-start(bf16[208,128]{1,0:T(8,128)(2,1)S(1)} %get-tuple-element.414), channel_id=1, source_target_pairs={{0,2},{1,3},{2,0},{3,1},{4,6},{5,7},{6,4},{7,5},{8,10},{9,11},{10,... | collective-permute-start | bytes 159752 | tf_op jit(solution)/shard_map/ppermute | solution.py:33
  47.1 3.8 %collective-permute-start.17 = (bf16[208,128]{1,0:T(8,128)(2,1)S(1)}, bf16[208,128]{1,0:T(8,128)(2,1)S(1)}, u32[]{:S(2)}, u32[]{:S(2)}) collective-permute-start(bf16[208,128]{1,0:T(8,128)(2,1)S(1)} %get-tuple-element.415), channel_id=1, source_target_pairs={{0,3},{1,2},{2,1},{3,0},{4,7},{5,6},{6,5},{7,4},{8,11},{9,10},{10,... | collective-permute-start | bytes 159752 | tf_op jit(solution)/shard_map/ppermute | solution.py:33
  51.5 11.3 %collective-permute-start.18 = (bf16[96,512]{1,0:T(8,128)(2,1)S(1)}, bf16[96,512]{1,0:T(8,128)(2,1)S(1)}, u32[]{:S(2)}, u32[]{:S(2)}) collective-permute-start(bf16[96,512]{1,0:T(8,128)(2,1)S(1)} %get-tuple-element.417), channel_id=1, source_target_pairs={{0,12},{4,8},{8,4},{12,0},{1,13},{5,9},{9,5},{13,1},{2,14},{6,10},... | collective-permute-start | bytes 294920 | tf_op jit(solution)/shard_map/ppermute | solution.py:33
  54.1 8.8 %collective-permute-start.19 = (bf16[96,512]{1,0:T(8,128)(2,1)S(1)}, bf16[96,512]{1,0:T(8,128)(2,1)S(1)}, u32[]{:S(2)}, u32[]{:S(2)}) collective-permute-start(bf16[96,512]{1,0:T(8,128)(2,1)S(1)} %get-tuple-element.418), channel_id=1, source_target_pairs={{0,8},{4,12},{8,0},{12,4},{1,9},{5,13},{9,1},{13,5},{2,10},{6,14},... | collective-permute-start | bytes 294920 | tf_op jit(solution)/shard_map/ppermute | solution.py:33
  54.1 8.8 %collective-permute-start.20 = (bf16[96,512]{1,0:T(8,128)(2,1)S(1)}, bf16[96,512]{1,0:T(8,128)(2,1)S(1)}, u32[]{:S(2)}, u32[]{:S(2)}) collective-permute-start(bf16[96,512]{1,0:T(8,128)(2,1)S(1)} %get-tuple-element.419), channel_id=1, source_target_pairs={{0,4},{4,0},{8,12},{12,8},{1,5},{5,1},{9,13},{13,9},{2,6},{6,2},{1... | collective-permute-start | bytes 294920 | tf_op jit(solution)/shard_map/ppermute | solution.py:33
  56.7 6.2 %copy-start.3 = (f32[256,128]{1,0:T(8,128)S(1)}, f32[256,128]{1,0:T(8,128)}, u32[]{:S(2)}) copy-start(f32[256,128]{1,0:T(8,128)} %get-tuple-element.424) | copy-start | bytes 393220
  56.7 6.2 %copy-start.4 = (s32[256,1]{0,1:T(1,128)S(1)}, s32[256,1]{0,1:T(1,128)}, u32[]{:S(2)}) copy-start(s32[256,1]{0,1:T(1,128)} %param.17) | copy-start | bytes 3076
  56.7 6.2 %copy-start.5 = (s32[64]{0:T(128)S(1)}, s32[64]{0:T(128)}, u32[]{:S(2)}) copy-start(s32[64]{0:T(128)} %param.18) | copy-start | bytes 772
  56.7 3.3 %collective-permute-start.1 = (bf16[256,2048]{1,0:T(8,128)(2,1)}, bf16[256,2048]{1,0:T(8,128)(2,1)S(1)}, u32[]{:S(2)}, u32[]{:S(2)}) collective-permute-start(bf16[256,2048]{1,0:T(8,128)(2,1)} %get-tuple-element.296.refs_0_), channel_id=1, source_target_pairs={{0,1},{1,0},{2,3},{3,2},{4,5},{5,4},{6,7},{7,6},{8,9},{9,8},{10,11... | collective-permute-start | bytes 3145736 | tf_op jit(solution)/shard_map/cond/branch_1_fun/ppermute | solution.py:33
where the time goes:
time: 64.7 us; the launch traced here: 64.3 us
  Pallas kernels  30.1 us (47%)
  waiting for transfers between devices  18.2 us (28%)
  starting transfers between devices  14 us (22%)
  between operations  1.68 us (3%)
    ppermute x12, waiting for transfers between devices, swap(): return lax.ppermute(x, axis, [(i, i ^ k) for i in range(size)])  18.2 us
    ppermute x12, starting transfers between devices, swap(): return lax.ppermute(x, axis, [(i, i ^ k) for i in range(size)])  14 us
    pallas_call x3, Pallas kernels, base(): pl.pallas_call(functools.partial(base_kernel, count), grid_spec=pltpu.Pre...  9.87 us
    pallas_call x3, Pallas kernels, pack(): pl.pallas_call(functools.partial(pack_kernel, local_count, wide_size, lay...  8.24 us
    pallas_call x2, Pallas kernels, down(): pl.pallas_call(functools.partial(down_kernel, len(blocks), cols, narrow_s...  6.43 us
    pallas_call x1, Pallas kernels, stage(): pl.pallas_call(stage_kernel, out_shape=[pltpu.VMEM((features, adapters *...  3.86 us
  transfers between devices with their start and end apart: 12, of which 3 were waited for; matrix products, arithmetic and copies ran while one was open for 0% of the time, Pallas kernels for 41%

commit v1 on v0

--- a/solution.py
+++ b/solution.py
@@ -11,7 +11,9 @@
 LANES = 128
 MOST = 16
 OWN_ROWS = 112
-AWAY_ROWS = 96
+NEAR_ROWS = 112
+FAR_ROWS = 64
+SHARED_ROWS = 48
 LATER_ROWS = 32
 VMEM = pltpu.VMEM
 MIB = 1 << 20
@@ -21,11 +23,18 @@
 
 def first_turn(wide_size, local_count):
     most = -(-(local_count * MOST + 1) // 32) * 32
-    return [(k, 0, min(AWAY_ROWS if k else OWN_ROWS, most)) for k in reversed(range(wide_size))]
-
-
-def ends(blocks, wide_size):
-    return [max(start + count - 1 for j, start, count in blocks if j == k) for k in range(wide_size)]
+    plain = {k: min(FAR_ROWS if k > 1 else NEAR_ROWS if k else OWN_ROWS, most) for k in range(wide_size)}
+    far = range(2, wide_size)
+    shares = FAR_ROWS - 1 < local_count * MOST
+
+    def rows_for(k):
+        return [(k, True, SHARED_ROWS)] * shares * (k > 1) + [(k, False, plain[k])]
+
+    leaving = [(k, True, SHARED_ROWS) for k in far[::2]] if shares else []
+    leaving += [(k, False, plain[k]) for k in [*range(1, min(2, wide_size)), *far, 0]]
+    early = [entry for k in [*far[:1], 0] for entry in rows_for(k)]
+    rest = [entry for k in [*far[1:], *range(1, min(2, wide_size))] for entry in rows_for(k)]
+    return leaving, early, rest
 
 
 def swap(x, axis, k):
@@ -56,8 +65,11 @@
 
 
 def pack_kernel(
-    local_count, wide_size, layout, span, per_turn, where_ref, tenant_ref, slot_ref, act_ref, *refs
+    local_count, wide_size, turns, span, later, where_ref, tenant_ref, slot_ref, act_ref, *refs
 ):
+    leaving, early, rest = turns
+    layout = [(k, False, LATER_ROWS) for k in range(wide_size)] if later else leaving
+    answers = layout if later else early + rest
     picked = range(*span)
     begun_ref, refs = refs[0], refs[1:]
     last_span = span[1] == len(layout)
@@ -94,19 +106,40 @@
         goes.astype(bf16), earlier.astype(f32).astype(bf16), preferred_element_type=f32
     )
     position = jnp.sum(goes * before, axis=0, keepdims=True).astype(i32)
-    adapters = jnp.broadcast_to(adapter, (8, rows)).astype(bf16)
+    held = {k: count - 1 for k, shared, count in leaving if not shared}
+    end, extra = dict(held), {}
+    for k, shared, count in leaving:
+        if shared:
+            named_k = jnp.sum(goes[k : k + 1], axis=1, keepdims=True).astype(i32)
+            extra[k] = jnp.maximum(named_k - held[k], 0)
+            end[k] = held[k] + count - 1
+            end[k ^ 1] = held[k ^ 1] + count - 1 - jnp.minimum(extra[k], count - 1)
+    offsets, offset = {}, 0
+    for k, shared, count in answers:
+        offsets[k, shared] = offset
+        offset += count
     place = jnp.full((1, rows), -1, i32)
     more = jnp.zeros((1, rows), f32)
-    position = position - where_ref[2] * per_turn
-    for k, end in enumerate(ends(layout, wide_size)):
-        more = jnp.where((leap == k) & (position >= end), 1.0, more)
-    offset, here = 0, []
-    for k, start, count in layout:
-        mine = position - start
-        mine = jnp.where((leap == k) & (mine >= 0) & (mine < count - 1), mine, -1)
-        place = jnp.where(mine >= 0, mine + offset, place)
-        offset += count
+    here, adapters = [], []
+    for k, shared, count in layout:
+        numbers = adapter
+        if later:
+            mine = position - end[k] - where_ref[2] * (count - 1)
+            mine = jnp.where(leap == k, mine, -1)
+            more = jnp.where(mine >= count - 1, 1.0, more)
+        elif shared:
+            mine = jnp.where(leap == k, position - held[k], -1)
+            other = jnp.where(position >= held[k ^ 1], position - held[k ^ 1] + extra[k], -1)
+            mine = jnp.where(leap == k ^ 1, other, mine)
+            numbers = adapter + jnp.where(leap == k ^ 1, 1.0 * local_count, 0.0)
+        else:
+            mine = jnp.where(leap == k, position, -1)
+            more = jnp.where((leap == k) & (position >= end[k]), 1.0, more)
+        mine = jnp.where((mine >= 0) & (mine < count - 1), mine, -1)
+        for j in (k, k ^ 1) if shared else (k,):
+            place = jnp.where((mine >= 0) & (leap == j), mine + offsets[j, shared], place)
         here.append(mine)
+        adapters.append(jnp.broadcast_to(numbers, (8, rows)).astype(bf16))
     any_more = jnp.max(more, axis=1, keepdims=True)
 
     perm = jnp.concatenate(
@@ -116,9 +149,15 @@
         ],
         axis=0,
     )
-    all_ids = lax.dot_general(
-        adapters, perm, (((1,), (1,)), ((), ())), preferred_element_type=f32
-    )
+    all_ids = [
+        lax.dot_general(
+            adapters[n],
+            perm[m * LANES : (m + 1) * LANES],
+            (((1,), (1,)), ((), ())),
+            preferred_element_type=f32,
+        )[:1]
+        for m, n in enumerate(picked)
+    ]
     lane = lax.broadcasted_iota(i32, (1, LANES), 1)
     for n in range(loads):
         load(n).wait()
@@ -129,8 +168,7 @@
             count = layout[n][2]
             part = body[m * LANES : m * LANES + count]
             if c == 0:
-                ids = all_ids[:1, m * LANES : (m + 1) * LANES]
-                ids = jnp.where(lane == LANES - 1, any_more, ids)
+                ids = jnp.where(lane == LANES - 1, any_more, all_ids[m])
                 last = lax.broadcasted_iota(i32, (count, LANES), 0) == count - 1
                 first = jnp.where(last, ids, part[:, :LANES])
                 part = jnp.concatenate([first, part[:, LANES:]], axis=1)
@@ -139,15 +177,16 @@
         place_ref[...] = jnp.broadcast_to(place.astype(f32), (LANES, rows)).T
 
 
-def pack(where, tenant, slot, activations, local_count, wide_size, layout, span, per_turn):
+def pack(where, tenant, slot, activations, local_count, wide_size, turns, span, later):
     rows, features = activations.shape
-    counts = [count for _, _, count in layout[slice(*span)]]
-    places = [jax.ShapeDtypeStruct((rows, LANES), f32)] if span[1] == len(layout) else []
+    total = wide_size if later else len(turns[0])
+    counts = [LATER_ROWS if later else turns[0][n][2] for n in range(*span)]
+    places = [jax.ShapeDtypeStruct((rows, LANES), f32)] if span[1] == total else []
     loads = 4
     whole = pl.BlockSpec(memory_space=VMEM)
     scalar = pl.BlockSpec(memory_space=pltpu.SMEM)
     return pl.pallas_call(
-        functools.partial(pack_kernel, local_count, wide_size, layout, span, per_turn),
+        functools.partial(pack_kernel, local_count, wide_size, turns, span, later),
         out_shape=[
             jax.ShapeDtypeStruct((1, 1), i32),
             *places,
@@ -195,7 +234,8 @@
     )(in_hbm(down_weight), in_hbm(up_weight))
 
 
-def down_kernel(count, cols, narrow_size, per_step, where_ref, weight_ref, *refs):
+def down_kernel(shifts, cols, narrow_size, per_step, where_ref, weight_ref, *refs):
+    count = len(shifts)
     xs, refs = refs[:count], refs[count:]
     before, refs = (refs[:3], refs[3:]) if narrow_size else ((), refs)
     flag_ref, ids_ref, *outs, held_ref = refs
@@ -204,14 +244,14 @@
     flag = jnp.zeros((1, LANES), f32)
     ids = []
     offset = 0
-    for x in xs:
+    for x, shift in zip(xs, shifts):
         rows = x.shape[0]
         held_ref[pl.ds(offset, rows), :] = x[...]
         last = x[pl.ds(rows - 16, 16), :LANES].astype(f32)[15:]
         flag = jnp.maximum(flag, last)
         turned = jnp.broadcast_to(last, (LANES, LANES)).T[:rows]
         keep = lax.broadcasted_iota(i32, (rows, LANES), 0) < rows - 1
-        ids.append(jnp.where(keep, turned, 0.0))
+        ids.append(jnp.where(keep, turned - shift, 0.0))
         offset += rows
     ids = jnp.concatenate(ids, axis=0)
     lane = lax.broadcasted_iota(i32, (1, LANES), 1)
@@ -251,7 +291,7 @@
         outs[j][...] = jnp.where(start >= KEY_VALUE_COLS, values, keys).astype(outs[j].dtype)
 
 
-def down(where, blocks, weight, cols, before, narrow_size, scale):
+def down(where, blocks, shifts, weight, cols, before, narrow_size, scale):
     features, width = weight.shape
     new_rows = sum(b.shape[0] for b in blocks)
     per_step = min(4, width // LANES)
@@ -264,7 +304,7 @@
         rows = new_rows
         sums = [((rows, LANES), f32)]
     return pl.pallas_call(
-        functools.partial(down_kernel, len(blocks), cols, narrow_size, per_step),
+        functools.partial(down_kernel, shifts, cols, narrow_size, per_step),
         out_shape=[
             jax.ShapeDtypeStruct((1, 1), i32),
             jax.ShapeDtypeStruct((rows, LANES), f32),
@@ -403,10 +443,9 @@
     return up(ids, sums, up_weight, counts)
 
 
-def later_turn(turn, axes, total, done, tenant, slot, activations, down_weight, up_weight):
+def later_turn(turn, axes, total, turns, tenant, slot, activations, down_weight, up_weight):
     wide_size, narrow_size = lax.axis_size("wide"), lax.axis_size("narrow")
     where = jnp.stack([*axes, turn])
-    layout = [(k, end, LATER_ROWS) for k, end in enumerate(done)]
     _, place, *sent = pack(
         where,
         tenant,
@@ -414,15 +453,18 @@
         activations,
         down_weight.shape[0],
         wide_size,
-        layout,
+        turns,
         (0, wide_size),
-        LATER_ROWS - 1,
+        True,
     )
     got = [swap(b, "wide", k) if k else b for k, b in enumerate(sent)]
     cols = up_weight.shape[1]
     down_weight, up_weight = stage(down_weight, up_weight)
-    before = down(where, got[:1], down_weight, cols, None, 0, 0.001)
-    more, ids, *sums = down(where, got[1:], down_weight, cols, before, narrow_size, 0.001)
+    shifts = [0] * wide_size
+    before = down(where, got[:1], shifts[:1], down_weight, cols, None, 0, 0.001)
+    more, ids, *sums = down(
+        where, got[1:], shifts[1:], down_weight, cols, before, narrow_size, 0.001
+    )
     outs = raise_sums(ids, sums, up_weight, [b.shape[0] for b in got])
     answers = [swap(b, "wide", k) if k else b for k, b in enumerate(outs)]
     return join(total, place, answers, f32), more[0, 0]
@@ -446,13 +488,12 @@
     up_weight = adapter_up_weight.reshape(-1, adapter_up_weight.shape[-1])
 
     cols = up_weight.shape[1]
-    layout = first_turn(wide_size, local_count)
-    own = len(layout) - 1
-    routed = (local_count, wide_size, layout)
-    begun, *sent = pack(where, tenant, slot, activations, *routed, (0, 1), 0)
-    if own > 1:
-        sent += pack(where, tenant, slot, after(activations, *sent), *routed, (1, own), 0)[1:]
-    got = [swap(b, "wide", k) for (k, _, _), b in zip(layout, sent)]
+    turns = first_turn(wide_size, local_count)
+    leaving, early, rest = turns
+    own = len(leaving) - 1
+    routed = (local_count, wide_size, turns)
+    ahead = min(own, 1 + sum(shared for _, shared, _ in leaving))
+    begun, *sent = pack(where, tenant, slot, activations, *routed, (0, ahead), False)
     half = narrow_size // 2
 
     def step(work, *operands):
@@ -470,31 +511,57 @@
             bit //= 2
         return [acts[j] for j in sorted(acts)]
 
+    def pack_away(tenant, slot, activations):
+        blocks = pack(where, tenant, slot, activations, *routed, (ahead, own), False)[1:]
+        return blocks, spread(activations)[1:]
+
     def pack_own(tenant, slot, activations):
-        return pack(where, tenant, slot, activations, *routed, (own, own + 1), 0)[1:]
-
-    def work_before(activations, shared_weight, maps):
-        return base(where, spread(activations), 0, shared_weight, None), stage(*maps)
+        return pack(where, tenant, slot, activations, *routed, (own, own + 1), False)[1:]
+
+    def work_before(acts, shared_weight, maps):
+        return base(where, acts, 0, shared_weight, None), stage(*maps)
 
     def work_after(across, shared_weight, base_out):
         for n, act in enumerate(spread(across)):
             base_out = base(where, [act], half + n, shared_weight, base_out)
         return base_out
 
+    if own == ahead:
+        acts = spread(activations)[1:]
+    else:
+        away, acts = step(pack_away, tenant, slot, after(activations, *sent))
+        sent += away
+    acts = [activations, *acts]
+    got = {}
+    for (k, shared, _), block in zip(leaving, sent):
+        got[k, shared] = swap(block, "wide", k)
     shared_weight, maps = after_all((shared_weight, (adapter_down_weight, up_weight)), *sent)
     place, own_block = step(pack_own, tenant, slot, after(activations, *sent))
+    got[0, False] = own_block
     across = swap(after(activations, own_block), "narrow", half) if half else None
+    for k, shared, _ in leaving:
+        if shared:
+            got[k ^ 1, True] = swap(got[k, True], "wide", 1)
     base_out, (down_beside, up_beside) = step(
-        work_before, *after_all((activations, shared_weight, maps), own_block)
-    )
-    before = down(where, [got[0], after(own_block, base_out)], down_beside, cols, None, 0, 0.001)
+        work_before, *after_all((acts, shared_weight, maps), own_block)
+    )
+
+    def blocks_of(entries):
+        shifts = [local_count if shared and k % 2 else 0 for k, shared, _ in entries]
+        return [got[k, shared] for k, shared, _ in entries], shifts
+
+    blocks, shifts = blocks_of(early)
+    blocks[-1] = after(blocks[-1], base_out)
+    before = down(where, blocks, shifts, down_beside, cols, None, 0, 0.001)
+    blocks, shifts = blocks_of(rest)
     more, ids, *sums = down(
-        where, after_all(got[1:], *before), down_beside, cols, before, narrow_size, 20
-    )
-    counts = [layout[n][2] for n in (0, own, *range(1, own))]
-    outs = raise_sums(ids, sums, up_beside, counts)
-    outs = [outs[0], *outs[2:], outs[1]]
-    answers = [swap(b, "wide", k) if k else b for (k, _, _), b in zip(layout, outs)]
+        where, after_all(blocks, *before), shifts, down_beside, cols, before, narrow_size, 20
+    )
+    counts = {}
+    for k, _, count in early + rest:
+        counts[k] = counts.get(k, 0) + count
+    outs = raise_sums(ids, sums, up_beside, list(counts.values()))
+    answers = [swap(b, "wide", k) if k else b for k, b in zip(counts, outs)]
     if half:
         base_out = step(work_after, *after_all((across, shared_weight, base_out), *outs))
     more = more[0, 0]
@@ -506,7 +573,7 @@
         def turn_of(state):
             turn, _, total = state
             total, more = later_turn(
-                turn, axes, total, ends(layout, wide_size), tenant, slot, activations, adapter_down_weight, up_weight
+                turn, axes, total, turns, tenant, slot, activations, adapter_down_weight, up_weight
             )
             return turn + 1, more, total
 

time: 64.7 us -> 66.6 us (1.029)
  starting transfers between devices: 14 us -> 19.4 us
  waiting for transfers between devices: 18.2 us -> 14.7 us
    ppermute x12 -> x14, starting transfers between devices: 14 us -> 19.4 us  [swap(): return lax.ppermute(x, axis, [(i, i ^ k) for i in range(size)])]
    ppermute x12 -> x14, waiting for transfers between devices: 18.2 us -> 14.7 us  [swap(): return lax.ppermute(x, axis, [(i, i ^ k) for i in range(size)])]
  transfers between devices with their start and end apart: 12 -> 14, of which waited for: 3 -> 6; matrix products, arithmetic and copies ran while one was open for 0% -> 0% of each run, Pallas kernels for 41% -> 41%
where the time goes in v1:
time: 66.6 us; the launch traced here: 66.3 us
  Pallas kernels  30.3 us (45%)
  starting transfers between devices  19.4 us (29%)
  waiting for transfers between devices  14.7 us (22%)
  between operations  1.49 us (2%)
    ppermute x14, starting transfers between devices, swap(): return lax.ppermute(x, axis, [(i, i ^ k) for i in range(size)])  19.4 us
    ppermute x14, waiting for transfers between devices, swap(): return lax.ppermute(x, axis, [(i, i ^ k) for i in range(size)])  14.7 us
    pallas_call x3, Pallas kernels, base(): pl.pallas_call(functools.partial(base_kernel, count), grid_spec=pltpu.Pre...  10.2 us
    pallas_call x3, Pallas kernels, pack(): pl.pallas_call(functools.partial(pack_kernel, local_count, wide_size, tur...  7.29 us
    pallas_call x2, Pallas kernels, down(): pl.pallas_call(functools.partial(down_kernel, shifts, cols, narrow_size,...  7.27 us
    pallas_call x1, Pallas kernels, stage(): pl.pallas_call(stage_kernel, out_shape=[pltpu.VMEM((features, adapters *...  3.86 us
  transfers between devices with their start and end apart: 14, of which 6 were waited for; matrix products, arithmetic and copies ran while one was open for 0% of the time, Pallas kernels for 41%

profile of v1, /device:TPU:0, one launch (start us, length us, event | category | flops | bytes accessed | tf_op | source)
XLA Modules:
  0.0 66.3 jit_solution(9021878342205698570)
XLA Ops:
  0.1 2.4 %pack_rows.10 = (s32[1,1]{1,0:T(1,128)}, bf16[48,2048]{1,0:T(8,128)(2,1)S(1)}, bf16[112,2048]{1,0:T(8,128)(2,1)S(1)}) custom-call(s32[3]{0:T(128)S(1)} %pad_add_fusion.1.where_ref, s32[1,256]{1,0:T(1,128)} %bitcast.21, s32[1,64]{1,0:T(1,128)} %bitcast.25, bf16[256,2048]{1,0:T(8,128)(2,1)} %act_ref.1), custom_call_target="tpu_custom_call" | custom-call | flops 167772 | bytes 1703 | tf_op jit(solution)/shard_map/pack_rows/pallas_call | solution.py:188
  2.5 3.1 %collective-permute-start.14 = (bf16[112,2048]{1,0:T(8,128)(2,1)S(1)}, bf16[112,2048]{1,0:T(8,128)(2,1)S(1)}, u32[]{:S(2)}, u32[]{:S(2)}) collective-permute-start(bf16[112,2048]{1,0:T(8,128)(2,1)S(1)} %get-tuple-element.410), channel_id=1, source_target_pairs={{0,4},{4,0},{8,12},{12,8},{1,5},{5,1},{9,13},{13,9},{2,6},{6,2},{1... | collective-permute-start | bytes 1376264 | tf_op jit(solution)/shard_map/ppermute | solution.py:42
  5.6 2.6 %collective-permute-start.11 = (bf16[48,2048]{1,0:T(8,128)(2,1)S(1)}, bf16[48,2048]{1,0:T(8,128)(2,1)S(1)}, u32[]{:S(2)}, u32[]{:S(2)}) collective-permute-start(bf16[48,2048]{1,0:T(8,128)(2,1)S(1)} %get-tuple-element.409), channel_id=1, source_target_pairs={{0,8},{4,12},{8,0},{12,4},{1,9},{5,13},{9,1},{13,5},{2,10},{6,14},... | collective-permute-start | bytes 589832 | tf_op jit(solution)/shard_map/ppermute | solution.py:42
  8.8 3.1 %conditional.5 = (bf16[64,2048]{1,0:T(8,128)(2,1)S(1)}, bf16[64,2048]{1,0:T(8,128)(2,1)S(1)}, bf16[256,2048]{1,0:T(8,128)(2,1)}) conditional(s32[]{:T(128)} %bitcast.8, () %tuple.72, (s32[3]{0:T(128)S(1)}, s32[1,256]{1,0:T(1,128)}, s32[1,64]{1,0:T(1,128)}, bf16[256,2048]{1,0:T(8,128)(2,1)}) %tuple.118), branch_computations={%region_0.0_spmd, %region_1.0_spmd} | conditional | flops 134217 | bytes 4195940 | solution.py:505
  8.9 2.4 %pack_rows.8 = (s32[1,1]{1,0:T(1,128)}, bf16[64,2048]{1,0:T(8,128)(2,1)S(1)}, bf16[64,2048]{1,0:T(8,128)(2,1)S(1)}) custom-call(s32[3]{0:T(128)S(1)} %get-tuple-element.292.where_ref, s32[1,256]{1,0:T(1,128)} %get-tuple-element.293.tenant_ref, s32[1,64]{1,0:T(1,128)} %get-tuple-element.294.slot_ref, bf16[256,2048]{1,0:T(8,128)(2,1)} %get-tuple-element.295.act_ref), custom_call_target="tpu_custom_call" | custom-call | flops 134217 | bytes 1572 | tf_op jit(solution)/shard_map/cond/branch_1_fun/pack_rows/pallas_call | solution.py:188
  12.3 2.5 %collective-permute-start.13 = (bf16[64,2048]{1,0:T(8,128)(2,1)S(1)}, bf16[64,2048]{1,0:T(8,128)(2,1)}, u32[]{:S(2)}, u32[]{:S(2)}) collective-permute-start(bf16[64,2048]{1,0:T(8,128)(2,1)S(1)} %get-tuple-element.414), channel_id=1, source_target_pairs={{0,12},{4,8},{8,4},{12,0},{1,13},{5,9},{9,5},{13,1},{2,14},{6,10},... | collective-permute-start | bytes 786440 | tf_op jit(solution)/shard_map/ppermute | solution.py:42
  14.7 6.0 %collective-permute-done.11.refs_0_ = bf16[48,2048]{1,0:T(8,128)(2,1)S(1)} collective-permute-done((bf16[48,2048]{1,0:T(8,128)(2,1)S(1)}, bf16[48,2048]{1,0:T(8,128)(2,1)S(1)}, u32[]{:S(2)}, u32[]{:S(2)}) %collective-permute-start.11) | collective-permute-done | bytes 196640 | tf_op jit(solution)/shard_map/ppermute | solution.py:42
  20.8 3.5 %collective-permute-start.12 = (bf16[48,2048]{1,0:T(8,128)(2,1)S(1)}, bf16[48,2048]{1,0:T(8,128)(2,1)}, u32[]{:S(2)}, u32[]{:S(2)}) collective-permute-start(bf16[48,2048]{1,0:T(8,128)(2,1)S(1)} %collective-permute-done.11.refs_0_), channel_id=1, source_target_pairs={{0,4},{4,0},{8,12},{12,8},{1,5},{5,1},{9,13},{13,9},{2,6},{6,2},{1... | collective-permute-start | bytes 589832 | tf_op jit(solution)/shard_map/ppermute | solution.py:42
  24.3 2.4 %conditional.6 = (f32[256,128]{1,0:T(8,128)S(1)}, bf16[112,2048]{1,0:T(8,128)(2,1)S(1)}) conditional(s32[]{:T(128)} %bitcast.8, () %tuple.76, (s32[3]{0:T(128)S(1)}, s32[1,256]{1,0:T(1,128)}, s32[1,64]{1,0:T(1,128)}, bf16[256,2048]{1,0:T(8,128)(2,1)}) %tuple.119), branch_computations={%region_2.0_spmd, %region_3.0_spmd} | conditional | flops 117440 | bytes 589846 | solution.py:505
  24.3 2.4 %pack_rows.9 = (s32[1,1]{1,0:T(1,128)}, f32[256,128]{1,0:T(8,128)S(1)}, bf16[112,2048]{1,0:T(8,128)(2,1)S(1)}) custom-call(s32[3]{0:T(128)S(1)} %get-tuple-element.298.where_ref, s32[1,256]{1,0:T(1,128)} %get-tuple-element.299.tenant_ref, s32[1,64]{1,0:T(1,128)} %get-tuple-element.300.slot_ref, bf16[256,2048]{1,0:T(8,128)(2,1)} %get-tuple-element.301.act_ref), custom_call_target="tpu_custom_call" | custom-call | flops 117440 | bytes 1507 | tf_op jit(solution)/shard_map/cond/branch_1_fun/pack_rows/pallas_call | solution.py:188
  26.8 1.6 %collective-permute-start.16 = (bf16[256,2048]{1,0:T(8,128)(2,1)}, bf16[256,2048]{1,0:T(8,128)(2,1)}, u32[]{:S(2)}, u32[]{:S(2)}) collective-permute-start(bf16[256,2048]{1,0:T(8,128)(2,1)} %act_ref.1), channel_id=1, source_target_pairs={{0,2},{1,3},{2,0},{3,1},{4,6},{5,7},{6,4},{7,5},{8,10},{9,11},{10,... | collective-permute-start | bytes 3145736 | tf_op jit(solution)/shard_map/ppermute | solution.py:42
  28.3 8.0 %conditional.7 = (f32[256,512]{1,0:T(8,128)S(1)}, bf16[2048,2048]{1,0:T(8,128)(2,1)S(1)}, bf16[1024,512]{1,0:T(8,128)(2,1)S(1)}) conditional(s32[]{:T(128)} %bitcast.8, () %tuple.71, (s32[3]{0:T(128)S(1)}, bf16[256,2048]{1,0:T(8,128)(2,1)}, bf16[256,2048]{1,0:T(8,128)(2,1)}, bf16[8192,512]{1,0:T(8,128)(2,1)}, bf16[16,2048,128]{2,1,0:T(8,128)(2,1)}, ...), branch_computations={%region_4.0_spmd, %region_5.0_spmd} | conditional | flops 1073741 | bytes 9961504 | solution.py:505
  28.3 3.9 %stage_maps.4 = (bf16[2048,2048]{1,0:T(8,128)(2,1)S(1)}, bf16[1024,512]{1,0:T(8,128)(2,1)S(1)}) custom-call(bf16[16,2048,128]{2,1,0:T(8,128)(2,1)} %get-tuple-element.308.down_ref, bf16[1024,512]{1,0:T(8,128)(2,1)} %get-tuple-element.309.up_ref), custom_call_target="tpu_custom_call" | custom-call | tf_op jit(solution)/shard_map/cond/branch_1_fun/stage_maps/pallas_call | solution.py:222
  32.2 4.2 %shared_projection.3 = f32[256,512]{1,0:T(8,128)S(1)} custom-call(s32[3]{0:T(128)S(1)} %get-tuple-element.304.where_ref, bf16[256,2048]{1,0:T(8,128)(2,1)} %get-tuple-element.305.refs_0_, bf16[256,2048]{1,0:T(8,128)(2,1)} %get-tuple-element.306.refs_1_, bf16[8192,512]{1,0:T(8,128)(2,1)} %get-tuple-element.307.refs_2_), custom_call_target="tpu_custom_call" | custom-call | flops 1073741 | bytes 6291 | tf_op jit(solution)/shard_map/cond/branch_1_fun/shared_projection/pallas_call | solution.py:384
  37.5 3.0 %down_maps.12 = (s32[1,1]{1,0:T(1,128)}, f32[224,128]{1,0:T(8,128)S(1)}, f32[224,128]{1,0:T(8,128)S(1)}) custom-call(s32[3]{0:T(128)S(1)} %pad_add_fusion.1.where_ref, bf16[2048,2048]{1,0:T(8,128)(2,1)S(1)} %get-tuple-element.425.weight_ref, bf16[48,2048]{1,0:T(8,128)(2,1)S(1)} %collective-permute-done.11.refs_0_, ...), custom_call_target="tpu_custom_call" | custom-call | flops 1879048 | bytes 9306 | tf_op jit(solution)/shard_map/down_maps/pallas_call | solution.py:306
  40.5 4.3 %down_maps.13 = (s32[1,1]{1,0:T(1,128)}, f32[448,128]{1,0:T(8,128)S(1)}, f32[224,128]{1,0:T(8,128)S(1)}, bf16[224,128]{1,0:T(8,128)(2,1)S(1)}, bf16[224,128]{1,0...) custom-call(s32[3]{0:T(128)S(1)} %pad_add_fusion.1.where_ref, bf16[2048,2048]{1,0:T(8,128)(2,1)S(1)} %get-tuple-element.425.weight_ref, ...), custom_call_target="tpu_custom_call" | custom-call | flops 37580963840 | bytes 186122240 | tf_op jit(solution)/shard_map/down_maps/pallas_call | solution.py:306
  44.9 1.6 %collective-permute-start.18 = (bf16[224,128]{1,0:T(8,128)(2,1)S(1)}, bf16[224,128]{1,0:T(8,128)(2,1)S(1)}, u32[]{:S(2)}, u32[]{:S(2)}) collective-permute-start(bf16[224,128]{1,0:T(8,128)(2,1)S(1)} %get-tuple-element.439), channel_id=1, source_target_pairs={{0,2},{1,3},{2,0},{3,1},{4,6},{5,7},{6,4},{7,5},{8,10},{9,11},{10,... | collective-permute-start | bytes 172040 | tf_op jit(solution)/shard_map/ppermute | solution.py:42
  46.7 4.7 %collective-permute-done.18.refs_2_ = bf16[224,128]{1,0:T(8,128)(2,1)S(1)} collective-permute-done((bf16[224,128]{1,0:T(8,128)(2,1)S(1)}, bf16[224,128]{1,0:T(8,128)(2,1)S(1)}, u32[]{:S(2)}, u32[]{:S(2)}) %collective-permute-start.18) | collective-permute-done | bytes 57376 | tf_op jit(solution)/shard_map/ppermute | solution.py:42
  52.8 3.1 %collective-permute-start.21 = (bf16[112,512]{1,0:T(8,128)(2,1)S(1)}, bf16[112,512]{1,0:T(8,128)(2,1)S(1)}, u32[]{:S(2)}, u32[]{:S(2)}) collective-permute-start(bf16[112,512]{1,0:T(8,128)(2,1)S(1)} %get-tuple-element.444), channel_id=1, source_target_pairs={{0,12},{4,8},{8,4},{12,0},{1,13},{5,9},{9,5},{13,1},{2,14},{6,10},... | collective-permute-start | bytes 344072 | tf_op jit(solution)/shard_map/ppermute | solution.py:42
  56.5 6.1 %conditional.8 = (f32[256,512]{1,0:T(8,128)S(1)}) conditional(s32[]{:T(128)} %bitcast.8, () %tuple.83, (bf16[256,2048]{1,0:T(8,128)(2,1)}, s32[3]{0:T(128)S(1)}, bf16[8192,512]{1,0:T(8,128)(2,1)}, f32[256,512]{1,0:T(8,128)S(1)}) %tuple.86), branch_computations={%region_6.0_spmd, %region_7.0_spmd} | conditional | flops 1073740 | bytes 4200642 | solution.py:505
  56.6 3.2 %shared_projection.4.refs_2_ = f32[256,512]{1,0:T(8,128)S(1)} custom-call(s32[3]{0:T(128)S(1)} %get-tuple-element.312.where_ref, bf16[256,2048]{1,0:T(8,128)(2,1)} %get-tuple-element.313.refs_0_, bf16[8192,512]{1,0:T(8,128)(2,1)} %get-tuple-element.314.refs_1_, f32[256,512]{1,0:T(8,128)S(1)} %get-tuple-element.315.refs_2_), custom_call_target="tpu_custom_call" | custom-call | flops 536870 | bytes 3145 | tf_op jit(solution)/shard_map/cond/branch_1_fun/shared_projection/pallas_call | solution.py:384
  59.8 2.8 %shared_projection.5 = f32[256,512]{1,0:T(8,128)S(1)} custom-call(s32[3]{0:T(128)S(1)} %get-tuple-element.312.where_ref, bf16[256,2048]{1,0:T(8,128)(2,1)S(1)} %collective-permute-done.1.refs_0_, bf16[8192,512]{1,0:T(8,128)(2,1)} %get-tuple-element.314.refs_1_, f32[256,512]{1,0:T(8,128)S(1)} %shared_projection.4.refs_2_), custom_call_target="tpu_custom_call" | custom-call | flops 536870 | bytes 3145 | tf_op jit(solution)/shard_map/cond/branch_1_fun/shared_projection/pallas_call | solution.py:384
  62.6 1.4 %collective-permute-done.20 = bf16[112,512]{1,0:T(8,128)(2,1)S(1)} collective-permute-done((bf16[112,512]{1,0:T(8,128)(2,1)S(1)}, bf16[112,512]{1,0:T(8,128)(2,1)S(1)}, u32[]{:S(2)}, u32[]{:S(2)}) %collective-permute-start.20) | collective-permute-done | bytes 114720 | tf_op jit(solution)/shard_map/ppermute | solution.py:42
  64.9 1.2 %conditional.9 = (bf16[256,512]{1,0:T(8,128)(2,1)}) conditional(s32[]{:T(128)} %bitcast.10, (f32[256,512]{1,0:T(8,128)S(1)}, f32[256,128]{1,0:T(8,128)S(1)}, bf16[112,512]{1,0:T(8,128)(2,1)S(1)}, bf16[112,512]{1,0:T(8,128)(2,1)S(1)}, bf16[112,512]{1,0:T(8,128)(2,1)S(1)}, /*index=5*/bf16[112,512]{1,0:T(8,128)(2,1)S(1)}) %tuple.87, ...), branch_computations={%region_8.0_spmd, %region_9.0_spmd} | conditional | flops 1624249 | bytes 73226744 | solution.py:583
  (25 shorter events, 5.9 us)
Async XLA Ops:
  2.5 38.0 %collective-permute-start.14 = (bf16[112,2048]{1,0:T(8,128)(2,1)S(1)}, bf16[112,2048]{1,0:T(8,128)(2,1)S(1)}, u32[]{:S(2)}, u32[]{:S(2)}) collective-permute-start(bf16[112,2048]{1,0:T(8,128)(2,1)S(1)} %get-tuple-element.410), channel_id=1, source_target_pairs={{0,4},{4,0},{8,12},{12,8},{1,5},{5,1},{9,13},{13,9},{2,6},{6,2},{1... | collective-permute-start | bytes 1376264 | tf_op jit(solution)/shard_map/ppermute | solution.py:42
  5.6 15.2 %collective-permute-start.11 = (bf16[48,2048]{1,0:T(8,128)(2,1)S(1)}, bf16[48,2048]{1,0:T(8,128)(2,1)S(1)}, u32[]{:S(2)}, u32[]{:S(2)}) collective-permute-start(bf16[48,2048]{1,0:T(8,128)(2,1)S(1)} %get-tuple-element.409), channel_id=1, source_target_pairs={{0,8},{4,12},{8,0},{12,4},{1,9},{5,13},{9,1},{13,5},{2,10},{6,14},... | collective-permute-start | bytes 589832 | tf_op jit(solution)/shard_map/ppermute | solution.py:42
  8.9 3.1 %collective-permute-start = (bf16[256,2048]{1,0:T(8,128)(2,1)}, bf16[256,2048]{1,0:T(8,128)(2,1)}, u32[]{:S(2)}, u32[]{:S(2)}) collective-permute-start(bf16[256,2048]{1,0:T(8,128)(2,1)} %get-tuple-element.295.act_ref), channel_id=1, source_target_pairs={{0,1},{1,0},{2,3},{3,2},{4,5},{5,4},{6,7},{7,6},{8,9},{9,8},{10,11... | collective-permute-start | bytes 3145736 | tf_op jit(solution)/shard_map/cond/branch_1_fun/ppermute | solution.py:42
  11.9 25.5 %collective-permute-start.15 = (bf16[64,2048]{1,0:T(8,128)(2,1)S(1)}, bf16[64,2048]{1,0:T(8,128)(2,1)S(1)}, u32[]{:S(2)}, u32[]{:S(2)}) collective-permute-start(bf16[64,2048]{1,0:T(8,128)(2,1)S(1)} %get-tuple-element.413), channel_id=1, source_target_pairs={{0,8},{4,12},{8,0},{12,4},{1,9},{5,13},{9,1},{13,5},{2,10},{6,14},... | collective-permute-start | bytes 786440 | tf_op jit(solution)/shard_map/ppermute | solution.py:42
  12.3 28.2 %collective-permute-start.13 = (bf16[64,2048]{1,0:T(8,128)(2,1)S(1)}, bf16[64,2048]{1,0:T(8,128)(2,1)}, u32[]{:S(2)}, u32[]{:S(2)}) collective-permute-start(bf16[64,2048]{1,0:T(8,128)(2,1)S(1)} %get-tuple-element.414), channel_id=1, source_target_pairs={{0,12},{4,8},{8,4},{12,0},{1,13},{5,9},{9,5},{13,1},{2,14},{6,10},... | collective-permute-start | bytes 786440 | tf_op jit(solution)/shard_map/ppermute | solution.py:42
  20.8 19.7 %collective-permute-start.12 = (bf16[48,2048]{1,0:T(8,128)(2,1)S(1)}, bf16[48,2048]{1,0:T(8,128)(2,1)}, u32[]{:S(2)}, u32[]{:S(2)}) collective-permute-start(bf16[48,2048]{1,0:T(8,128)(2,1)S(1)} %collective-permute-done.11.refs_0_), channel_id=1, source_target_pairs={{0,4},{4,0},{8,12},{12,8},{1,5},{5,1},{9,13},{13,9},{2,6},{6,2},{1... | collective-permute-start | bytes 589832 | tf_op jit(solution)/shard_map/ppermute | solution.py:42
  26.8 29.7 %collective-permute-start.16 = (bf16[256,2048]{1,0:T(8,128)(2,1)}, bf16[256,2048]{1,0:T(8,128)(2,1)}, u32[]{:S(2)}, u32[]{:S(2)}) collective-permute-start(bf16[256,2048]{1,0:T(8,128)(2,1)} %act_ref.1), channel_id=1, source_target_pairs={{0,2},{1,3},{2,0},{3,1},{4,6},{5,7},{6,4},{7,5},{8,10},{9,11},{10,... | collective-permute-start | bytes 3145736 | tf_op jit(solution)/shard_map/ppermute | solution.py:42
  44.8 1.9 %collective-permute-start.17 = (bf16[224,128]{1,0:T(8,128)(2,1)S(1)}, bf16[224,128]{1,0:T(8,128)(2,1)S(1)}, u32[]{:S(2)}, u32[]{:S(2)}) collective-permute-start(bf16[224,128]{1,0:T(8,128)(2,1)S(1)} %get-tuple-element.438), channel_id=1, source_target_pairs={{0,1},{1,0},{2,3},{3,2},{4,5},{5,4},{6,7},{7,6},{8,9},{9,8},{10,11... | collective-permute-start | bytes 172040 | tf_op jit(solution)/shard_map/ppermute | solution.py:42
  44.9 6.6 %collective-permute-start.18 = (bf16[224,128]{1,0:T(8,128)(2,1)S(1)}, bf16[224,128]{1,0:T(8,128)(2,1)S(1)}, u32[]{:S(2)}, u32[]{:S(2)}) collective-permute-start(bf16[224,128]{1,0:T(8,128)(2,1)S(1)} %get-tuple-element.439), channel_id=1, source_target_pairs={{0,2},{1,3},{2,0},{3,1},{4,6},{5,7},{6,4},{7,5},{8,10},{9,11},{10,... | collective-permute-start | bytes 172040 | tf_op jit(solution)/shard_map/ppermute | solution.py:42
  46.4 5.0 %collective-permute-start.19 = (bf16[224,128]{1,0:T(8,128)(2,1)S(1)}, bf16[224,128]{1,0:T(8,128)(2,1)S(1)}, u32[]{:S(2)}, u32[]{:S(2)}) collective-permute-start(bf16[224,128]{1,0:T(8,128)(2,1)S(1)} %get-tuple-element.440), channel_id=1, source_target_pairs={{0,3},{1,2},{2,1},{3,0},{4,7},{5,6},{6,5},{7,4},{8,11},{9,10},{10,... | collective-permute-start | bytes 172040 | tf_op jit(solution)/shard_map/ppermute | solution.py:42
  52.1 11.9 %collective-permute-start.20 = (bf16[112,512]{1,0:T(8,128)(2,1)S(1)}, bf16[112,512]{1,0:T(8,128)(2,1)S(1)}, u32[]{:S(2)}, u32[]{:S(2)}) collective-permute-start(bf16[112,512]{1,0:T(8,128)(2,1)S(1)} %get-tuple-element.442), channel_id=1, source_target_pairs={{0,8},{4,12},{8,0},{12,4},{1,9},{5,13},{9,1},{13,5},{2,10},{6,14},... | collective-permute-start | bytes 344072 | tf_op jit(solution)/shard_map/ppermute | solution.py:42
  52.8 11.2 %collective-permute-start.21 = (bf16[112,512]{1,0:T(8,128)(2,1)S(1)}, bf16[112,512]{1,0:T(8,128)(2,1)S(1)}, u32[]{:S(2)}, u32[]{:S(2)}) collective-permute-start(bf16[112,512]{1,0:T(8,128)(2,1)S(1)} %get-tuple-element.444), channel_id=1, source_target_pairs={{0,12},{4,8},{8,4},{12,0},{1,13},{5,9},{9,5},{13,1},{2,14},{6,10},... | collective-permute-start | bytes 344072 | tf_op jit(solution)/shard_map/ppermute | solution.py:42
  55.9 9.0 %collective-permute-start.22 = (bf16[112,512]{1,0:T(8,128)(2,1)S(1)}, bf16[112,512]{1,0:T(8,128)(2,1)S(1)}, u32[]{:S(2)}, u32[]{:S(2)}) collective-permute-start(bf16[112,512]{1,0:T(8,128)(2,1)S(1)} %get-tuple-element.445), channel_id=1, source_target_pairs={{0,4},{4,0},{8,12},{12,8},{1,5},{5,1},{9,13},{13,9},{2,6},{6,2},{1... | collective-permute-start | bytes 344072 | tf_op jit(solution)/shard_map/ppermute | solution.py:42
  56.5 8.4 %copy-start.3 = (s32[256,1]{0,1:T(1,128)S(1)}, s32[256,1]{0,1:T(1,128)}, u32[]{:S(2)}) copy-start(s32[256,1]{0,1:T(1,128)} %param.19) | copy-start | bytes 3076
  56.5 8.4 %copy-start.4 = (s32[64]{0:T(128)S(1)}, s32[64]{0:T(128)}, u32[]{:S(2)}) copy-start(s32[64]{0:T(128)} %param.20) | copy-start | bytes 772
  56.5 3.3 %collective-permute-start.1 = (bf16[256,2048]{1,0:T(8,128)(2,1)}, bf16[256,2048]{1,0:T(8,128)(2,1)S(1)}, u32[]{:S(2)}, u32[]{:S(2)}) collective-permute-start(bf16[256,2048]{1,0:T(8,128)(2,1)} %get-tuple-element.313.refs_0_), channel_id=1, source_target_pairs={{0,1},{1,0},{2,3},{3,2},{4,5},{5,4},{6,7},{7,6},{8,9},{9,8},{10,11... | collective-permute-start | bytes 3145736 | tf_op jit(solution)/shard_map/cond/branch_1_fun/ppermute | solution.py:42

commit v2 on v1

--- a/solution.py
+++ b/solution.py
@@ -538,13 +538,14 @@
     shared_weight, maps = after_all((shared_weight, (adapter_down_weight, up_weight)), *sent)
     place, own_block = step(pack_own, tenant, slot, after(activations, *sent))
     got[0, False] = own_block
-    across = swap(after(activations, own_block), "narrow", half) if half else None
+    across = swap(after(activations, *sent[:ahead]), "narrow", half) if half else None
+    base_out, (down_beside, up_beside) = step(
+        work_before, *after_all((acts, shared_weight, maps), own_block)
+    )
+
     for k, shared, _ in leaving:
         if shared:
-            got[k ^ 1, True] = swap(got[k, True], "wide", 1)
-    base_out, (down_beside, up_beside) = step(
-        work_before, *after_all((acts, shared_weight, maps), own_block)
-    )
+            got[k ^ 1, True] = swap(after(got[k, True], base_out), "wide", 1)
 
     def blocks_of(entries):
         shifts = [local_count if shared and k % 2 else 0 for k, shared, _ in entries]
@@ -555,7 +556,7 @@
     before = down(where, blocks, shifts, down_beside, cols, None, 0, 0.001)
     blocks, shifts = blocks_of(rest)
     more, ids, *sums = down(
-        where, after_all(blocks, *before), shifts, down_beside, cols, before, narrow_size, 20
+        where, after_all(blocks, *before), shifts, down_beside, cols, before, narrow_size, 0.001
     )
     counts = {}
     for k, _, count in early + rest:

time: 66.6 us -> 66.7 us (level)
  starting transfers between devices: 19.4 us -> 17.6 us
  waiting for transfers between devices: 14.7 us -> 16.4 us
    ppermute x14, starting transfers between devices: 19.4 us -> 17.6 us  [swap(): return lax.ppermute(x, axis, [(i, i ^ k) for i in range(size)])]
    ppermute x14, waiting for transfers between devices: 14.7 us -> 16.4 us  [swap(): return lax.ppermute(x, axis, [(i, i ^ k) for i in range(size)])]
    pallas_call x3, Pallas kernels: 7.29 us -> 8.01 us  [pack(): pl.pallas_call(functools.partial(pack_kernel, local_count, wide_size, tur...]
  transfers between devices with their start and end apart: 14 -> 14, of which waited for: 6 -> 6; matrix products, arithmetic and copies ran while one was open for 0% -> 0% of each run, Pallas kernels for 41% -> 40%
where the time goes in v2:
time: 66.7 us; the launch traced here: 66.4 us
  Pallas kernels  30.5 us (46%)
  starting transfers between devices  17.6 us (26%)
  waiting for transfers between devices  16.4 us (25%)
  between operations  1.49 us (2%)
    ppermute x14, starting transfers between devices, swap(): return lax.ppermute(x, axis, [(i, i ^ k) for i in range(size)])  17.6 us
    ppermute x14, waiting for transfers between devices, swap(): return lax.ppermute(x, axis, [(i, i ^ k) for i in range(size)])  16.4 us
    pallas_call x3, Pallas kernels, base(): pl.pallas_call(functools.partial(base_kernel, count), grid_spec=pltpu.Pre...  10.2 us
    pallas_call x3, Pallas kernels, pack(): pl.pallas_call(functools.partial(pack_kernel, local_count, wide_size, tur...  8.01 us
    pallas_call x2, Pallas kernels, down(): pl.pallas_call(functools.partial(down_kernel, shifts, cols, narrow_size,...  6.77 us
    pallas_call x1, Pallas kernels, stage(): pl.pallas_call(stage_kernel, out_shape=[pltpu.VMEM((features, adapters *...  3.87 us
  transfers between devices with their start and end apart: 14, of which 6 were waited for; matrix products, arithmetic and copies ran while one was open for 0% of the time, Pallas kernels for 40%

profile of v2, /device:TPU:0, one launch (start us, length us, event | category | flops | bytes accessed | tf_op | source)
XLA Modules:
  0.0 66.4 jit_solution(7400627708648849987)
XLA Ops:
  0.1 3.1 %pack_rows.10 = (s32[1,1]{1,0:T(1,128)}, bf16[48,2048]{1,0:T(8,128)(2,1)S(1)}, bf16[112,2048]{1,0:T(8,128)(2,1)}) custom-call(s32[3]{0:T(128)S(1)} %pad_add_fusion.1.where_ref, s32[1,256]{1,0:T(1,128)} %bitcast.21, s32[1,64]{1,0:T(1,128)} %bitcast.25, bf16[256,2048]{1,0:T(8,128)(2,1)} %act_ref.1), custom_call_target="tpu_custom_call" | custom-call | flops 167772 | bytes 1703 | tf_op jit(solution)/shard_map/pack_rows/pallas_call | solution.py:188
  3.2 3.0 %collective-permute-start.16 = (bf16[256,2048]{1,0:T(8,128)(2,1)}, bf16[256,2048]{1,0:T(8,128)(2,1)}, u32[]{:S(2)}, u32[]{:S(2)}) collective-permute-start(bf16[256,2048]{1,0:T(8,128)(2,1)} %act_ref.1), channel_id=1, source_target_pairs={{0,2},{1,3},{2,0},{3,1},{4,6},{5,7},{6,4},{7,5},{8,10},{9,11},{10,... | collective-permute-start | bytes 3145736 | tf_op jit(solution)/shard_map/ppermute | solution.py:42
  6.2 1.6 %collective-permute-start.14 = (bf16[112,2048]{1,0:T(8,128)(2,1)}, bf16[112,2048]{1,0:T(8,128)(2,1)S(1)}, u32[]{:S(2)}, u32[]{:S(2)}) collective-permute-start(bf16[112,2048]{1,0:T(8,128)(2,1)} %get-tuple-element.410), channel_id=1, source_target_pairs={{0,4},{4,0},{8,12},{12,8},{1,5},{5,1},{9,13},{13,9},{2,6},{6,2},{1... | collective-permute-start | bytes 1376264 | tf_op jit(solution)/shard_map/ppermute | solution.py:42
  7.8 2.6 %collective-permute-start.11 = (bf16[48,2048]{1,0:T(8,128)(2,1)S(1)}, bf16[48,2048]{1,0:T(8,128)(2,1)S(1)}, u32[]{:S(2)}, u32[]{:S(2)}) collective-permute-start(bf16[48,2048]{1,0:T(8,128)(2,1)S(1)} %get-tuple-element.409), channel_id=1, source_target_pairs={{0,8},{4,12},{8,0},{12,4},{1,9},{5,13},{9,1},{13,5},{2,10},{6,14},... | collective-permute-start | bytes 589832 | tf_op jit(solution)/shard_map/ppermute | solution.py:42
  11.1 3.1 %conditional.5 = (bf16[64,2048]{1,0:T(8,128)(2,1)S(1)}, bf16[64,2048]{1,0:T(8,128)(2,1)S(1)}, bf16[256,2048]{1,0:T(8,128)(2,1)}) conditional(s32[]{:T(128)} %bitcast.8, () %tuple.72, (s32[3]{0:T(128)S(1)}, s32[1,256]{1,0:T(1,128)}, s32[1,64]{1,0:T(1,128)}, bf16[256,2048]{1,0:T(8,128)(2,1)}) %tuple.118), branch_computations={%region_0.0_spmd, %region_1.0_spmd} | conditional | flops 134217 | bytes 4195940 | solution.py:505
  11.2 2.4 %pack_rows.8 = (s32[1,1]{1,0:T(1,128)}, bf16[64,2048]{1,0:T(8,128)(2,1)S(1)}, bf16[64,2048]{1,0:T(8,128)(2,1)S(1)}) custom-call(s32[3]{0:T(128)S(1)} %get-tuple-element.292.where_ref, s32[1,256]{1,0:T(1,128)} %get-tuple-element.293.tenant_ref, s32[1,64]{1,0:T(1,128)} %get-tuple-element.294.slot_ref, bf16[256,2048]{1,0:T(8,128)(2,1)} %get-tuple-element.295.act_ref), custom_call_target="tpu_custom_call" | custom-call | flops 134217 | bytes 1572 | tf_op jit(solution)/shard_map/cond/branch_1_fun/pack_rows/pallas_call | solution.py:188
  14.5 2.5 %collective-permute-start.13 = (bf16[64,2048]{1,0:T(8,128)(2,1)S(1)}, bf16[64,2048]{1,0:T(8,128)(2,1)S(1)}, u32[]{:S(2)}, u32[]{:S(2)}) collective-permute-start(bf16[64,2048]{1,0:T(8,128)(2,1)S(1)} %get-tuple-element.414), channel_id=1, source_target_pairs={{0,12},{4,8},{8,4},{12,0},{1,13},{5,9},{9,5},{13,1},{2,14},{6,10},... | collective-permute-start | bytes 786440 | tf_op jit(solution)/shard_map/ppermute | solution.py:42
  17.0 2.4 %conditional.6 = (f32[256,128]{1,0:T(8,128)S(1)}, bf16[112,2048]{1,0:T(8,128)(2,1)S(1)}) conditional(s32[]{:T(128)} %bitcast.8, () %tuple.76, (s32[3]{0:T(128)S(1)}, s32[1,256]{1,0:T(1,128)}, s32[1,64]{1,0:T(1,128)}, bf16[256,2048]{1,0:T(8,128)(2,1)}) %tuple.119), branch_computations={%region_2.0_spmd, %region_3.0_spmd} | conditional | flops 117440 | bytes 589846 | solution.py:505
  17.0 2.4 %pack_rows.9 = (s32[1,1]{1,0:T(1,128)}, f32[256,128]{1,0:T(8,128)S(1)}, bf16[112,2048]{1,0:T(8,128)(2,1)S(1)}) custom-call(s32[3]{0:T(128)S(1)} %get-tuple-element.298.where_ref, s32[1,256]{1,0:T(1,128)} %get-tuple-element.299.tenant_ref, s32[1,64]{1,0:T(1,128)} %get-tuple-element.300.slot_ref, bf16[256,2048]{1,0:T(8,128)(2,1)} %get-tuple-element.301.act_ref), custom_call_target="tpu_custom_call" | custom-call | flops 117440 | bytes 1507 | tf_op jit(solution)/shard_map/cond/branch_1_fun/pack_rows/pallas_call | solution.py:188
  19.4 8.1 %conditional.7 = (f32[256,512]{1,0:T(8,128)S(1)}, bf16[2048,2048]{1,0:T(8,128)(2,1)S(1)}, bf16[1024,512]{1,0:T(8,128)(2,1)S(1)}) conditional(s32[]{:T(128)} %bitcast.8, () %tuple.71, (s32[3]{0:T(128)S(1)}, bf16[256,2048]{1,0:T(8,128)(2,1)}, bf16[256,2048]{1,0:T(8,128)(2,1)}, bf16[8192,512]{1,0:T(8,128)(2,1)}, bf16[16,2048,128]{2,1,0:T(8,128)(2,1)}, ...), branch_computations={%region_4.0_spmd, %region_5.0_spmd} | conditional | flops 1073741 | bytes 9961504 | solution.py:505
  19.4 3.9 %stage_maps.4 = (bf16[2048,2048]{1,0:T(8,128)(2,1)S(1)}, bf16[1024,512]{1,0:T(8,128)(2,1)S(1)}) custom-call(bf16[16,2048,128]{2,1,0:T(8,128)(2,1)} %get-tuple-element.308.down_ref, bf16[1024,512]{1,0:T(8,128)(2,1)} %get-tuple-element.309.up_ref), custom_call_target="tpu_custom_call" | custom-call | tf_op jit(solution)/shard_map/cond/branch_1_fun/stage_maps/pallas_call | solution.py:222
  23.3 4.2 %shared_projection.3 = f32[256,512]{1,0:T(8,128)S(1)} custom-call(s32[3]{0:T(128)S(1)} %get-tuple-element.304.where_ref, bf16[256,2048]{1,0:T(8,128)(2,1)} %get-tuple-element.305.refs_0_, bf16[256,2048]{1,0:T(8,128)(2,1)} %get-tuple-element.306.refs_1_, bf16[8192,512]{1,0:T(8,128)(2,1)} %get-tuple-element.307.refs_2_), custom_call_target="tpu_custom_call" | custom-call | flops 1073741 | bytes 6291 | tf_op jit(solution)/shard_map/cond/branch_1_fun/shared_projection/pallas_call | solution.py:384
  28.2 11.5 %collective-permute-done.15.refs_1_ = bf16[64,2048]{1,0:T(8,128)(2,1)S(1)} collective-permute-done((bf16[64,2048]{1,0:T(8,128)(2,1)S(1)}, bf16[64,2048]{1,0:T(8,128)(2,1)S(1)}, u32[]{:S(2)}, u32[]{:S(2)}) %collective-permute-start.15) | collective-permute-done | bytes 262176 | tf_op jit(solution)/shard_map/ppermute | solution.py:42
  39.7 3.0 %down_maps.12 = (s32[1,1]{1,0:T(1,128)}, f32[224,128]{1,0:T(8,128)S(1)}, f32[224,128]{1,0:T(8,128)S(1)}) custom-call(s32[3]{0:T(128)S(1)} %pad_add_fusion.1.where_ref, bf16[2048,2048]{1,0:T(8,128)(2,1)S(1)} %get-tuple-element.425.weight_ref, bf16[48,2048]{1,0:T(8,128)(2,1)S(1)} %collective-permute-done.11.refs_0_, ...), custom_call_target="tpu_custom_call" | custom-call | flops 1879048 | bytes 9306 | tf_op jit(solution)/shard_map/down_maps/pallas_call | solution.py:306
  42.8 3.8 %down_maps.13 = (s32[1,1]{1,0:T(1,128)}, f32[448,128]{1,0:T(8,128)S(1)}, f32[224,128]{1,0:T(8,128)S(1)}, bf16[224,128]{1,0:T(8,128)(2,1)S(1)}, bf16[224,128]{1,0...) custom-call(s32[3]{0:T(128)S(1)} %pad_add_fusion.1.where_ref, bf16[2048,2048]{1,0:T(8,128)(2,1)S(1)} %get-tuple-element.425.weight_ref, ...), custom_call_target="tpu_custom_call" | custom-call | flops 1879048 | bytes 9306 | tf_op jit(solution)/shard_map/down_maps/pallas_call | solution.py:306
  47.2 1.3 %collective-permute-start.19 = (bf16[224,128]{1,0:T(8,128)(2,1)S(1)}, bf16[224,128]{1,0:T(8,128)(2,1)S(1)}, u32[]{:S(2)}, u32[]{:S(2)}) collective-permute-start(bf16[224,128]{1,0:T(8,128)(2,1)S(1)} %get-tuple-element.440), channel_id=1, source_target_pairs={{0,3},{1,2},{2,1},{3,0},{4,7},{5,6},{6,5},{7,4},{8,11},{9,10},{10,... | collective-permute-start | bytes 172040 | tf_op jit(solution)/shard_map/ppermute | solution.py:42
  48.5 2.9 %collective-permute-done.18.refs_2_ = bf16[224,128]{1,0:T(8,128)(2,1)S(1)} collective-permute-done((bf16[224,128]{1,0:T(8,128)(2,1)S(1)}, bf16[224,128]{1,0:T(8,128)(2,1)S(1)}, u32[]{:S(2)}, u32[]{:S(2)}) %collective-permute-start.18) | collective-permute-done | bytes 57376 | tf_op jit(solution)/shard_map/ppermute | solution.py:42
  52.4 1.4 %collective-permute-start.20 = (bf16[112,512]{1,0:T(8,128)(2,1)S(1)}, bf16[112,512]{1,0:T(8,128)(2,1)S(1)}, u32[]{:S(2)}, u32[]{:S(2)}) collective-permute-start(bf16[112,512]{1,0:T(8,128)(2,1)S(1)} %get-tuple-element.442), channel_id=1, source_target_pairs={{0,8},{4,12},{8,0},{12,4},{1,9},{5,13},{9,1},{13,5},{2,10},{6,14},... | collective-permute-start | bytes 344072 | tf_op jit(solution)/shard_map/ppermute | solution.py:42
  53.8 3.4 %collective-permute-start.21 = (bf16[112,512]{1,0:T(8,128)(2,1)S(1)}, bf16[112,512]{1,0:T(8,128)(2,1)S(1)}, u32[]{:S(2)}, u32[]{:S(2)}) collective-permute-start(bf16[112,512]{1,0:T(8,128)(2,1)S(1)} %get-tuple-element.444), channel_id=1, source_target_pairs={{0,12},{4,8},{8,4},{12,0},{1,13},{5,9},{9,5},{13,1},{2,14},{6,10},... | collective-permute-start | bytes 344072 | tf_op jit(solution)/shard_map/ppermute | solution.py:42
  57.8 6.1 %conditional.8 = (f32[256,512]{1,0:T(8,128)S(1)}) conditional(s32[]{:T(128)} %bitcast.8, () %tuple.84, (bf16[256,2048]{1,0:T(8,128)(2,1)}, s32[3]{0:T(128)S(1)}, bf16[8192,512]{1,0:T(8,128)(2,1)}, f32[256,512]{1,0:T(8,128)S(1)}) %tuple.86), branch_computations={%region_6.0_spmd, %region_7.0_spmd} | conditional | flops 1073740 | bytes 4200642 | solution.py:505
  57.9 3.2 %shared_projection.4.refs_2_ = f32[256,512]{1,0:T(8,128)S(1)} custom-call(s32[3]{0:T(128)S(1)} %get-tuple-element.312.where_ref, bf16[256,2048]{1,0:T(8,128)(2,1)} %get-tuple-element.313.refs_0_, bf16[8192,512]{1,0:T(8,128)(2,1)} %get-tuple-element.314.refs_1_, f32[256,512]{1,0:T(8,128)S(1)} %get-tuple-element.315.refs_2_), custom_call_target="tpu_custom_call" | custom-call | flops 536870 | bytes 3145 | tf_op jit(solution)/shard_map/cond/branch_1_fun/shared_projection/pallas_call | solution.py:384
  61.1 2.8 %shared_projection.5 = f32[256,512]{1,0:T(8,128)S(1)} custom-call(s32[3]{0:T(128)S(1)} %get-tuple-element.312.where_ref, bf16[256,2048]{1,0:T(8,128)(2,1)S(1)} %collective-permute-done.1.refs_0_, bf16[8192,512]{1,0:T(8,128)(2,1)} %get-tuple-element.314.refs_1_, f32[256,512]{1,0:T(8,128)S(1)} %shared_projection.4.refs_2_), custom_call_target="tpu_custom_call" | custom-call | flops 536870 | bytes 3145 | tf_op jit(solution)/shard_map/cond/branch_1_fun/shared_projection/pallas_call | solution.py:384
  65.0 1.2 %conditional.9 = (bf16[256,512]{1,0:T(8,128)(2,1)}) conditional(s32[]{:T(128)} %bitcast.10, (f32[256,512]{1,0:T(8,128)S(1)}, f32[256,128]{1,0:T(8,128)S(1)}, bf16[112,512]{1,0:T(8,128)(2,1)S(1)}, bf16[112,512]{1,0:T(8,128)(2,1)S(1)}, bf16[112,512]{1,0:T(8,128)(2,1)S(1)}, /*index=5*/bf16[112,512]{1,0:T(8,128)(2,1)S(1)}) %tuple.87, ...), branch_computations={%region_8.0_spmd, %region_9.0_spmd} | conditional | flops 1624249 | bytes 73226744 | solution.py:584
  65.0 1.0 %join_corrections.7 = bf16[256,512]{1,0:T(8,128)(2,1)} custom-call(f32[256,512]{1,0:T(8,128)S(1)} %get-tuple-element.316.base_ref, f32[256,128]{1,0:T(8,128)S(1)} %get-tuple-element.317.place_ref, bf16[112,512]{1,0:T(8,128)(2,1)S(1)} %get-tuple-element.318.refs_0_, bf16[112,512]{1,0:T(8,128)(2,1)S(1)} %get-tuple-element.319.refs_1_, ...), custom_call_target="tpu_custom_call" | custom-call | flops 117440 | bytes 1245 | tf_op jit(solution)/shard_map/cond/branch_0_fun/join_corrections/pallas_call | solution.py:429
  (25 shorter events, 4.7 us)
Async XLA Ops:
  3.2 54.5 %collective-permute-start.16 = (bf16[256,2048]{1,0:T(8,128)(2,1)}, bf16[256,2048]{1,0:T(8,128)(2,1)}, u32[]{:S(2)}, u32[]{:S(2)}) collective-permute-start(bf16[256,2048]{1,0:T(8,128)(2,1)} %act_ref.1), channel_id=1, source_target_pairs={{0,2},{1,3},{2,0},{3,1},{4,6},{5,7},{6,4},{7,5},{8,10},{9,11},{10,... | collective-permute-start | bytes 3145736 | tf_op jit(solution)/shard_map/ppermute | solution.py:42
  6.2 36.5 %collective-permute-start.14 = (bf16[112,2048]{1,0:T(8,128)(2,1)}, bf16[112,2048]{1,0:T(8,128)(2,1)S(1)}, u32[]{:S(2)}, u32[]{:S(2)}) collective-permute-start(bf16[112,2048]{1,0:T(8,128)(2,1)} %get-tuple-element.410), channel_id=1, source_target_pairs={{0,4},{4,0},{8,12},{12,8},{1,5},{5,1},{9,13},{13,9},{2,6},{6,2},{1... | collective-permute-start | bytes 1376264 | tf_op jit(solution)/shard_map/ppermute | solution.py:42
  7.8 19.7 %collective-permute-start.11 = (bf16[48,2048]{1,0:T(8,128)(2,1)S(1)}, bf16[48,2048]{1,0:T(8,128)(2,1)S(1)}, u32[]{:S(2)}, u32[]{:S(2)}) collective-permute-start(bf16[48,2048]{1,0:T(8,128)(2,1)S(1)} %get-tuple-element.409), channel_id=1, source_target_pairs={{0,8},{4,12},{8,0},{12,4},{1,9},{5,13},{9,1},{13,5},{2,10},{6,14},... | collective-permute-start | bytes 589832 | tf_op jit(solution)/shard_map/ppermute | solution.py:42
  11.1 3.1 %collective-permute-start = (bf16[256,2048]{1,0:T(8,128)(2,1)}, bf16[256,2048]{1,0:T(8,128)(2,1)}, u32[]{:S(2)}, u32[]{:S(2)}) collective-permute-start(bf16[256,2048]{1,0:T(8,128)(2,1)} %get-tuple-element.295.act_ref), channel_id=1, source_target_pairs={{0,1},{1,0},{2,3},{3,2},{4,5},{5,4},{6,7},{7,6},{8,9},{9,8},{10,11... | collective-permute-start | bytes 3145736 | tf_op jit(solution)/shard_map/cond/branch_1_fun/ppermute | solution.py:42
  14.1 25.6 %collective-permute-start.15 = (bf16[64,2048]{1,0:T(8,128)(2,1)S(1)}, bf16[64,2048]{1,0:T(8,128)(2,1)S(1)}, u32[]{:S(2)}, u32[]{:S(2)}) collective-permute-start(bf16[64,2048]{1,0:T(8,128)(2,1)S(1)} %get-tuple-element.413), channel_id=1, source_target_pairs={{0,8},{4,12},{8,0},{12,4},{1,9},{5,13},{9,1},{13,5},{2,10},{6,14},... | collective-permute-start | bytes 786440 | tf_op jit(solution)/shard_map/ppermute | solution.py:42
  14.5 28.3 %collective-permute-start.13 = (bf16[64,2048]{1,0:T(8,128)(2,1)S(1)}, bf16[64,2048]{1,0:T(8,128)(2,1)S(1)}, u32[]{:S(2)}, u32[]{:S(2)}) collective-permute-start(bf16[64,2048]{1,0:T(8,128)(2,1)S(1)} %get-tuple-element.414), channel_id=1, source_target_pairs={{0,12},{4,8},{8,4},{12,0},{1,13},{5,9},{9,5},{13,1},{2,14},{6,10},... | collective-permute-start | bytes 786440 | tf_op jit(solution)/shard_map/ppermute | solution.py:42
  27.5 15.3 %collective-permute-start.12 = (bf16[48,2048]{1,0:T(8,128)(2,1)S(1)}, bf16[48,2048]{1,0:T(8,128)(2,1)S(1)}, u32[]{:S(2)}, u32[]{:S(2)}) collective-permute-start(bf16[48,2048]{1,0:T(8,128)(2,1)S(1)} %collective-permute-done.11.refs_0_), channel_id=1, source_target_pairs={{0,4},{4,0},{8,12},{12,8},{1,5},{5,1},{9,13},{13,9},{2,6},{6,2},{1... | collective-permute-start | bytes 589832 | tf_op jit(solution)/shard_map/ppermute | solution.py:42
  46.5 1.9 %collective-permute-start.17 = (bf16[224,128]{1,0:T(8,128)(2,1)S(1)}, bf16[224,128]{1,0:T(8,128)(2,1)S(1)}, u32[]{:S(2)}, u32[]{:S(2)}) collective-permute-start(bf16[224,128]{1,0:T(8,128)(2,1)S(1)} %get-tuple-element.438), channel_id=1, source_target_pairs={{0,1},{1,0},{2,3},{3,2},{4,5},{5,4},{6,7},{7,6},{8,9},{9,8},{10,11... | collective-permute-start | bytes 172040 | tf_op jit(solution)/shard_map/ppermute | solution.py:42
  46.6 4.8 %collective-permute-start.18 = (bf16[224,128]{1,0:T(8,128)(2,1)S(1)}, bf16[224,128]{1,0:T(8,128)(2,1)S(1)}, u32[]{:S(2)}, u32[]{:S(2)}) collective-permute-start(bf16[224,128]{1,0:T(8,128)(2,1)S(1)} %get-tuple-element.439), channel_id=1, source_target_pairs={{0,2},{1,3},{2,0},{3,1},{4,6},{5,7},{6,4},{7,5},{8,10},{9,11},{10,... | collective-permute-start | bytes 172040 | tf_op jit(solution)/shard_map/ppermute | solution.py:42
  47.2 4.5 %collective-permute-start.19 = (bf16[224,128]{1,0:T(8,128)(2,1)S(1)}, bf16[224,128]{1,0:T(8,128)(2,1)S(1)}, u32[]{:S(2)}, u32[]{:S(2)}) collective-permute-start(bf16[224,128]{1,0:T(8,128)(2,1)S(1)} %get-tuple-element.440), channel_id=1, source_target_pairs={{0,3},{1,2},{2,1},{3,0},{4,7},{5,6},{6,5},{7,4},{8,11},{9,10},{10,... | collective-permute-start | bytes 172040 | tf_op jit(solution)/shard_map/ppermute | solution.py:42
  52.4 11.9 %collective-permute-start.20 = (bf16[112,512]{1,0:T(8,128)(2,1)S(1)}, bf16[112,512]{1,0:T(8,128)(2,1)S(1)}, u32[]{:S(2)}, u32[]{:S(2)}) collective-permute-start(bf16[112,512]{1,0:T(8,128)(2,1)S(1)} %get-tuple-element.442), channel_id=1, source_target_pairs={{0,8},{4,12},{8,0},{12,4},{1,9},{5,13},{9,1},{13,5},{2,10},{6,14},... | collective-permute-start | bytes 344072 | tf_op jit(solution)/shard_map/ppermute | solution.py:42
  53.8 10.5 %collective-permute-start.21 = (bf16[112,512]{1,0:T(8,128)(2,1)S(1)}, bf16[112,512]{1,0:T(8,128)(2,1)S(1)}, u32[]{:S(2)}, u32[]{:S(2)}) collective-permute-start(bf16[112,512]{1,0:T(8,128)(2,1)S(1)} %get-tuple-element.444), channel_id=1, source_target_pairs={{0,12},{4,8},{8,4},{12,0},{1,13},{5,9},{9,5},{13,1},{2,14},{6,10},... | collective-permute-start | bytes 344072 | tf_op jit(solution)/shard_map/ppermute | solution.py:42
  57.2 7.8 %collective-permute-start.22 = (bf16[112,512]{1,0:T(8,128)(2,1)S(1)}, bf16[112,512]{1,0:T(8,128)(2,1)S(1)}, u32[]{:S(2)}, u32[]{:S(2)}) collective-permute-start(bf16[112,512]{1,0:T(8,128)(2,1)S(1)} %get-tuple-element.445), channel_id=1, source_target_pairs={{0,4},{4,0},{8,12},{12,8},{1,5},{5,1},{9,13},{13,9},{2,6},{6,2},{1... | collective-permute-start | bytes 344072 | tf_op jit(solution)/shard_map/ppermute | solution.py:42
  57.8 7.3 %copy-start.3 = (s32[256,1]{0,1:T(1,128)S(1)}, s32[256,1]{0,1:T(1,128)}, u32[]{:S(2)}) copy-start(s32[256,1]{0,1:T(1,128)} %param.19) | copy-start | bytes 3076
  57.8 7.3 %copy-start.4 = (s32[64]{0:T(128)S(1)}, s32[64]{0:T(128)}, u32[]{:S(2)}) copy-start(s32[64]{0:T(128)} %param.20) | copy-start | bytes 772
  57.8 3.3 %collective-permute-start.1 = (bf16[256,2048]{1,0:T(8,128)(2,1)}, bf16[256,2048]{1,0:T(8,128)(2,1)S(1)}, u32[]{:S(2)}, u32[]{:S(2)}) collective-permute-start(bf16[256,2048]{1,0:T(8,128)(2,1)} %get-tuple-element.313.refs_0_), channel_id=1, source_target_pairs={{0,1},{1,0},{2,3},{3,2},{4,5},{5,4},{6,7},{7,6},{8,9},{9,8},{10,11... | collective-permute-start | bytes 3145736 | tf_op jit(solution)/shard_map/cond/branch_1_fun/ppermute | solution.py:42

commit v3 on v2

--- a/solution.py
+++ b/solution.py
@@ -27,14 +27,16 @@
     far = range(2, wide_size)
     shares = FAR_ROWS - 1 < local_count * MOST
 
-    def rows_for(k):
-        return [(k, True, SHARED_ROWS)] * shares * (k > 1) + [(k, False, plain[k])]
-
-    leaving = [(k, True, SHARED_ROWS) for k in far[::2]] if shares else []
-    leaving += [(k, False, plain[k]) for k in [*range(1, min(2, wide_size)), *far, 0]]
-    early = [entry for k in [*far[:1], 0] for entry in rows_for(k)]
-    rest = [entry for k in [*far[1:], *range(1, min(2, wide_size))] for entry in rows_for(k)]
-    return leaving, early, rest
+    near = [(k, False, plain[k]) for k in range(min(2, wide_size))][::-1]
+    direct = [(k, True, SHARED_ROWS) for k in far[::2]] if shares else []
+    passed = [(k, True, SHARED_ROWS) for k in far[1::2]] if shares else []
+    apart = [(k, False, plain[k]) for k in far]
+    leaving = [*direct, *near[:-1], *apart, near[-1]]
+    return leaving, [*direct, *near], [*apart, *passed]
+
+
+def answer_order(early, rest):
+    return sorted(early + rest, key=lambda entry: (-entry[0], entry[1]))
 
 
 def swap(x, axis, k):
@@ -69,7 +71,7 @@
 ):
     leaving, early, rest = turns
     layout = [(k, False, LATER_ROWS) for k in range(wide_size)] if later else leaving
-    answers = layout if later else early + rest
+    answers = layout if later else answer_order(early, rest)
     picked = range(*span)
     begun_ref, refs = refs[0], refs[1:]
     last_span = span[1] == len(layout)
@@ -323,7 +325,7 @@
     )(where, weight, *blocks, *(before if narrow_size else []))
 
 
-def up_kernel(narrow_size, ids_ref, *refs):
+def up_kernel(narrow_size, pieces, ids_ref, *refs):
     parts, weight_ref, outs = refs[:narrow_size], refs[narrow_size], refs[narrow_size + 1 :]
     total = parts[0][...]
     for part in parts[1:]:
@@ -343,17 +345,16 @@
         for pair in range(adapters // 2)
     ]
     found = jnp.dot(jnp.concatenate(left, axis=1), weight_ref[...], preferred_element_type=f32)
-    offset = 0
-    for out in outs:
-        rows = out.shape[0]
-        out[...] = found[offset : offset + rows].astype(bf16)
-        offset += rows
-
-
-def up(ids, parts, weight, counts):
+    for out, spans in zip(outs, pieces):
+        parts_of = [found[start : start + count] for start, count in spans]
+        out[...] = jnp.concatenate(parts_of, axis=0).astype(bf16)
+
+
+def up(ids, parts, weight, pieces):
     cols = weight.shape[1]
+    counts = [sum(count for _, count in spans) for spans in pieces]
     return pl.pallas_call(
-        functools.partial(up_kernel, len(parts)),
+        functools.partial(up_kernel, len(parts), pieces),
         out_shape=[jax.ShapeDtypeStruct((c, cols), bf16) for c in counts],
         compiler_params=params(10),
         cost_estimate=cost(2 * sum(counts) * weight.size, 2 * weight.size + 2 * sum(counts) * (cols + 512)),
@@ -438,9 +439,9 @@
     )(base_out, place, *corrections)
 
 
-def raise_sums(ids, sums, up_weight, counts):
+def raise_sums(ids, sums, up_weight, pieces):
     sums = [swap(part, "narrow", j) if j else part for j, part in enumerate(sums)]
-    return up(ids, sums, up_weight, counts)
+    return up(ids, sums, up_weight, pieces)
 
 
 def later_turn(turn, axes, total, turns, tenant, slot, activations, down_weight, up_weight):
@@ -465,7 +466,8 @@
     more, ids, *sums = down(
         where, got[1:], shifts[1:], down_weight, cols, before, narrow_size, 0.001
     )
-    outs = raise_sums(ids, sums, up_weight, [b.shape[0] for b in got])
+    pieces = [[(k * LATER_ROWS, LATER_ROWS)] for k in range(wide_size)]
+    outs = raise_sums(ids, sums, up_weight, pieces)
     answers = [swap(b, "wide", k) if k else b for k, b in enumerate(outs)]
     return join(total, place, answers, f32), more[0, 0]
 
@@ -558,11 +560,15 @@
     more, ids, *sums = down(
         where, after_all(blocks, *before), shifts, down_beside, cols, before, narrow_size, 0.001
     )
-    counts = {}
-    for k, _, count in early + rest:
-        counts[k] = counts.get(k, 0) + count
-    outs = raise_sums(ids, sums, up_beside, list(counts.values()))
-    answers = [swap(b, "wide", k) if k else b for k, b in zip(counts, outs)]
+    starts, start = {}, 0
+    for k, shared, count in early + rest:
+        starts[k, shared] = start
+        start += count
+    spans = {}
+    for k, shared, count in answer_order(early, rest):
+        spans.setdefault(k, []).append((starts[k, shared], count))
+    outs = raise_sums(ids, sums, up_beside, list(spans.values()))
+    answers = [swap(b, "wide", k) if k else b for k, b in zip(spans, outs)]
     if half:
         base_out = step(work_after, *after_all((across, shared_weight, base_out), *outs))
     more = more[0, 0]

time: 66.7 us -> 67.6 us (1.013)
  waiting for transfers between devices: 16.4 us -> 17.4 us
    ppermute x14, waiting for transfers between devices: 16.4 us -> 17.4 us  [swap(): return lax.ppermute(x, axis, [(i, i ^ k) for i in range(size)])]
  transfers between devices with their start and end apart: 14 -> 14, of which waited for: 6 -> 6; matrix products, arithmetic and copies ran while one was open for 0% -> 0% of each run, Pallas kernels for 40% -> 39%
where the time goes in v3:
time: 67.6 us; the launch traced here: 67.3 us
  Pallas kernels  30.6 us (45%)
  starting transfers between devices  17.4 us (26%)
  waiting for transfers between devices  17.4 us (26%)
  between operations  1.48 us (2%)
    ppermute x14, starting transfers between devices, swap(): return lax.ppermute(x, axis, [(i, i ^ k) for i in range(size)])  17.4 us
    ppermute x14, waiting for transfers between devices, swap(): return lax.ppermute(x, axis, [(i, i ^ k) for i in range(size)])  17.4 us
    pallas_call x3, Pallas kernels, base(): pl.pallas_call(functools.partial(base_kernel, count), grid_spec=pltpu.Pre...  10.2 us
    pallas_call x3, Pallas kernels, pack(): pl.pallas_call(functools.partial(pack_kernel, local_count, wide_size, tur...  8.01 us
    pallas_call x2, Pallas kernels, down(): pl.pallas_call(functools.partial(down_kernel, shifts, cols, narrow_size,...  6.78 us
    pallas_call x1, Pallas kernels, stage(): pl.pallas_call(stage_kernel, out_shape=[pltpu.VMEM((features, adapters *...  3.87 us
  transfers between devices with their start and end apart: 14, of which 6 were waited for; matrix products, arithmetic and copies ran while one was open for 0% of the time, Pallas kernels for 39%

profile of v3, /device:TPU:0, one launch (start us, length us, event | category | flops | bytes accessed | tf_op | source)
XLA Modules:
  0.0 67.3 jit_solution(17707109033221235489)
XLA Ops:
  0.1 3.1 %pack_rows.10 = (s32[1,1]{1,0:T(1,128)}, bf16[48,2048]{1,0:T(8,128)(2,1)S(1)}, bf16[112,2048]{1,0:T(8,128)(2,1)}) custom-call(s32[3]{0:T(128)S(1)} %pad_add_fusion.1.where_ref, s32[1,256]{1,0:T(1,128)} %bitcast.21, s32[1,64]{1,0:T(1,128)} %bitcast.25, bf16[256,2048]{1,0:T(8,128)(2,1)} %act_ref.1), custom_call_target="tpu_custom_call" | custom-call | flops 167772 | bytes 1703 | tf_op jit(solution)/shard_map/pack_rows/pallas_call | solution.py:190
  3.2 3.0 %collective-permute-start.16 = (bf16[256,2048]{1,0:T(8,128)(2,1)}, bf16[256,2048]{1,0:T(8,128)(2,1)}, u32[]{:S(2)}, u32[]{:S(2)}) collective-permute-start(bf16[256,2048]{1,0:T(8,128)(2,1)} %act_ref.1), channel_id=1, source_target_pairs={{0,2},{1,3},{2,0},{3,1},{4,6},{5,7},{6,4},{7,5},{8,10},{9,11},{10,... | collective-permute-start | bytes 3145736 | tf_op jit(solution)/shard_map/ppermute | solution.py:44
  6.2 1.6 %collective-permute-start.15 = (bf16[112,2048]{1,0:T(8,128)(2,1)}, bf16[112,2048]{1,0:T(8,128)(2,1)S(1)}, u32[]{:S(2)}, u32[]{:S(2)}) collective-permute-start(bf16[112,2048]{1,0:T(8,128)(2,1)} %get-tuple-element.410), channel_id=1, source_target_pairs={{0,4},{4,0},{8,12},{12,8},{1,5},{5,1},{9,13},{13,9},{2,6},{6,2},{1... | collective-permute-start | bytes 1376264 | tf_op jit(solution)/shard_map/ppermute | solution.py:44
  7.8 2.6 %collective-permute-start.13 = (bf16[48,2048]{1,0:T(8,128)(2,1)S(1)}, bf16[48,2048]{1,0:T(8,128)(2,1)S(1)}, u32[]{:S(2)}, u32[]{:S(2)}) collective-permute-start(bf16[48,2048]{1,0:T(8,128)(2,1)S(1)} %get-tuple-element.409), channel_id=1, source_target_pairs={{0,8},{4,12},{8,0},{12,4},{1,9},{5,13},{9,1},{13,5},{2,10},{6,14},... | collective-permute-start | bytes 589832 | tf_op jit(solution)/shard_map/ppermute | solution.py:44
  11.1 3.1 %conditional.5 = (bf16[64,2048]{1,0:T(8,128)(2,1)S(1)}, bf16[64,2048]{1,0:T(8,128)(2,1)S(1)}, bf16[256,2048]{1,0:T(8,128)(2,1)}) conditional(s32[]{:T(128)} %bitcast.8, () %tuple.72, (s32[3]{0:T(128)S(1)}, s32[1,256]{1,0:T(1,128)}, s32[1,64]{1,0:T(1,128)}, bf16[256,2048]{1,0:T(8,128)(2,1)}) %tuple.118), branch_computations={%region_0.0_spmd, %region_1.0_spmd} | conditional | flops 134217 | bytes 4195940 | solution.py:507
  11.2 2.4 %pack_rows.8 = (s32[1,1]{1,0:T(1,128)}, bf16[64,2048]{1,0:T(8,128)(2,1)S(1)}, bf16[64,2048]{1,0:T(8,128)(2,1)S(1)}) custom-call(s32[3]{0:T(128)S(1)} %get-tuple-element.292.where_ref, s32[1,256]{1,0:T(1,128)} %get-tuple-element.293.tenant_ref, s32[1,64]{1,0:T(1,128)} %get-tuple-element.294.slot_ref, bf16[256,2048]{1,0:T(8,128)(2,1)} %get-tuple-element.295.act_ref), custom_call_target="tpu_custom_call" | custom-call | flops 134217 | bytes 1572 | tf_op jit(solution)/shard_map/cond/branch_1_fun/pack_rows/pallas_call | solution.py:190
  14.5 2.5 %collective-permute-start.12 = (bf16[64,2048]{1,0:T(8,128)(2,1)S(1)}, bf16[64,2048]{1,0:T(8,128)(2,1)S(1)}, u32[]{:S(2)}, u32[]{:S(2)}) collective-permute-start(bf16[64,2048]{1,0:T(8,128)(2,1)S(1)} %get-tuple-element.414), channel_id=1, source_target_pairs={{0,12},{4,8},{8,4},{12,0},{1,13},{5,9},{9,5},{13,1},{2,14},{6,10},... | collective-permute-start | bytes 786440 | tf_op jit(solution)/shard_map/ppermute | solution.py:44
  17.0 2.4 %conditional.6 = (f32[256,128]{1,0:T(8,128)S(1)}, bf16[112,2048]{1,0:T(8,128)(2,1)S(1)}) conditional(s32[]{:T(128)} %bitcast.8, () %tuple.76, (s32[3]{0:T(128)S(1)}, s32[1,256]{1,0:T(1,128)}, s32[1,64]{1,0:T(1,128)}, bf16[256,2048]{1,0:T(8,128)(2,1)}) %tuple.119), branch_computations={%region_2.0_spmd, %region_3.0_spmd} | conditional | flops 117440 | bytes 589846 | solution.py:507
  17.0 2.4 %pack_rows.9 = (s32[1,1]{1,0:T(1,128)}, f32[256,128]{1,0:T(8,128)S(1)}, bf16[112,2048]{1,0:T(8,128)(2,1)S(1)}) custom-call(s32[3]{0:T(128)S(1)} %get-tuple-element.298.where_ref, s32[1,256]{1,0:T(1,128)} %get-tuple-element.299.tenant_ref, s32[1,64]{1,0:T(1,128)} %get-tuple-element.300.slot_ref, bf16[256,2048]{1,0:T(8,128)(2,1)} %get-tuple-element.301.act_ref), custom_call_target="tpu_custom_call" | custom-call | flops 117440 | bytes 1507 | tf_op jit(solution)/shard_map/cond/branch_1_fun/pack_rows/pallas_call | solution.py:190
  19.4 8.1 %conditional.7 = (f32[256,512]{1,0:T(8,128)S(1)}, bf16[2048,2048]{1,0:T(8,128)(2,1)S(1)}, bf16[1024,512]{1,0:T(8,128)(2,1)S(1)}) conditional(s32[]{:T(128)} %bitcast.8, () %tuple.71, (s32[3]{0:T(128)S(1)}, bf16[256,2048]{1,0:T(8,128)(2,1)}, bf16[256,2048]{1,0:T(8,128)(2,1)}, bf16[8192,512]{1,0:T(8,128)(2,1)}, bf16[16,2048,128]{2,1,0:T(8,128)(2,1)}, ...), branch_computations={%region_4.0_spmd, %region_5.0_spmd} | conditional | flops 1073741 | bytes 9961504 | solution.py:507
  19.4 3.9 %stage_maps.4 = (bf16[2048,2048]{1,0:T(8,128)(2,1)S(1)}, bf16[1024,512]{1,0:T(8,128)(2,1)S(1)}) custom-call(bf16[16,2048,128]{2,1,0:T(8,128)(2,1)} %get-tuple-element.308.down_ref, bf16[1024,512]{1,0:T(8,128)(2,1)} %get-tuple-element.309.up_ref), custom_call_target="tpu_custom_call" | custom-call | tf_op jit(solution)/shard_map/cond/branch_1_fun/stage_maps/pallas_call | solution.py:224
  23.3 4.2 %shared_projection.3 = f32[256,512]{1,0:T(8,128)S(1)} custom-call(s32[3]{0:T(128)S(1)} %get-tuple-element.304.where_ref, bf16[256,2048]{1,0:T(8,128)(2,1)} %get-tuple-element.305.refs_0_, bf16[256,2048]{1,0:T(8,128)(2,1)} %get-tuple-element.306.refs_1_, bf16[8192,512]{1,0:T(8,128)(2,1)} %get-tuple-element.307.refs_2_), custom_call_target="tpu_custom_call" | custom-call | flops 1073741 | bytes 6291 | tf_op jit(solution)/shard_map/cond/branch_1_fun/shared_projection/pallas_call | solution.py:385
  28.2 3.4 %down_maps.12 = (s32[1,1]{1,0:T(1,128)}, f32[272,128]{1,0:T(8,128)S(1)}, f32[272,128]{1,0:T(8,128)S(1)}) custom-call(s32[3]{0:T(128)S(1)} %pad_add_fusion.1.where_ref, bf16[2048,2048]{1,0:T(8,128)(2,1)S(1)} %get-tuple-element.425.weight_ref, bf16[48,2048]{1,0:T(8,128)(2,1)S(1)} %collective-permute-done.13.refs_0_, ...), custom_call_target="tpu_custom_call" | custom-call | flops 2281701 | bytes 9502 | tf_op jit(solution)/shard_map/down_maps/pallas_call | solution.py:308
  31.6 8.1 %collective-permute-done.11.refs_0_ = bf16[64,2048]{1,0:T(8,128)(2,1)S(1)} collective-permute-done((bf16[64,2048]{1,0:T(8,128)(2,1)S(1)}, bf16[64,2048]{1,0:T(8,128)(2,1)S(1)}, u32[]{:S(2)}, u32[]{:S(2)}) %collective-permute-start.11) | collective-permute-done | bytes 262176 | tf_op jit(solution)/shard_map/ppermute | solution.py:44
  39.7 2.3 %collective-permute-done.14.refs_2_ = bf16[48,2048]{1,0:T(8,128)(2,1)S(1)} collective-permute-done((bf16[48,2048]{1,0:T(8,128)(2,1)S(1)}, bf16[48,2048]{1,0:T(8,128)(2,1)S(1)}, u32[]{:S(2)}, u32[]{:S(2)}) %collective-permute-start.14) | collective-permute-done | bytes 196640 | tf_op jit(solution)/shard_map/ppermute | solution.py:44
  42.0 3.4 %down_maps.13 = (s32[1,1]{1,0:T(1,128)}, f32[448,128]{1,0:T(8,128)S(1)}, f32[224,128]{1,0:T(8,128)S(1)}, bf16[224,128]{1,0:T(8,128)(2,1)S(1)}, bf16[224,128]{1,0...) custom-call(s32[3]{0:T(128)S(1)} %pad_add_fusion.1.where_ref, bf16[2048,2048]{1,0:T(8,128)(2,1)S(1)} %get-tuple-element.425.weight_ref, ...), custom_call_target="tpu_custom_call" | custom-call | flops 1476395 | bytes 9109 | tf_op jit(solution)/shard_map/down_maps/pallas_call | solution.py:308
  46.1 1.2 %collective-permute-start.19 = (bf16[224,128]{1,0:T(8,128)(2,1)S(1)}, bf16[224,128]{1,0:T(8,128)(2,1)S(1)}, u32[]{:S(2)}, u32[]{:S(2)}) collective-permute-start(bf16[224,128]{1,0:T(8,128)(2,1)S(1)} %get-tuple-element.440), channel_id=1, source_target_pairs={{0,3},{1,2},{2,1},{3,0},{4,7},{5,6},{6,5},{7,4},{8,11},{9,10},{10,... | collective-permute-start | bytes 172040 | tf_op jit(solution)/shard_map/ppermute | solution.py:44
  47.4 2.9 %collective-permute-done.18.refs_2_ = bf16[224,128]{1,0:T(8,128)(2,1)S(1)} collective-permute-done((bf16[224,128]{1,0:T(8,128)(2,1)S(1)}, bf16[224,128]{1,0:T(8,128)(2,1)S(1)}, u32[]{:S(2)}, u32[]{:S(2)}) %collective-permute-start.18) | collective-permute-done | bytes 57376 | tf_op jit(solution)/shard_map/ppermute | solution.py:44
  51.6 4.3 %collective-permute-start.21 = (bf16[112,512]{1,0:T(8,128)(2,1)S(1)}, bf16[112,512]{1,0:T(8,128)(2,1)S(1)}, u32[]{:S(2)}, u32[]{:S(2)}) collective-permute-start(bf16[112,512]{1,0:T(8,128)(2,1)S(1)} %get-tuple-element.443), channel_id=1, source_target_pairs={{0,8},{4,12},{8,0},{12,4},{1,9},{5,13},{9,1},{13,5},{2,10},{6,14},... | collective-permute-start | bytes 344072 | tf_op jit(solution)/shard_map/ppermute | solution.py:44
  56.5 6.1 %conditional.8 = (f32[256,512]{1,0:T(8,128)S(1)}) conditional(s32[]{:T(128)} %bitcast.8, () %tuple.84, (bf16[256,2048]{1,0:T(8,128)(2,1)}, s32[3]{0:T(128)S(1)}, bf16[8192,512]{1,0:T(8,128)(2,1)}, f32[256,512]{1,0:T(8,128)S(1)}) %tuple.86), branch_computations={%region_6.0_spmd, %region_7.0_spmd} | conditional | flops 1073740 | bytes 4200642 | solution.py:507
  56.6 3.2 %shared_projection.4.refs_2_ = f32[256,512]{1,0:T(8,128)S(1)} custom-call(s32[3]{0:T(128)S(1)} %get-tuple-element.312.where_ref, bf16[256,2048]{1,0:T(8,128)(2,1)} %get-tuple-element.313.refs_0_, bf16[8192,512]{1,0:T(8,128)(2,1)} %get-tuple-element.314.refs_1_, f32[256,512]{1,0:T(8,128)S(1)} %get-tuple-element.315.refs_2_), custom_call_target="tpu_custom_call" | custom-call | flops 536870 | bytes 3145 | tf_op jit(solution)/shard_map/cond/branch_1_fun/shared_projection/pallas_call | solution.py:385
  59.8 2.8 %shared_projection.5 = f32[256,512]{1,0:T(8,128)S(1)} custom-call(s32[3]{0:T(128)S(1)} %get-tuple-element.312.where_ref, bf16[256,2048]{1,0:T(8,128)(2,1)S(1)} %collective-permute-done.1.refs_0_, bf16[8192,512]{1,0:T(8,128)(2,1)} %get-tuple-element.314.refs_1_, f32[256,512]{1,0:T(8,128)S(1)} %shared_projection.4.refs_2_), custom_call_target="tpu_custom_call" | custom-call | flops 536870 | bytes 3145 | tf_op jit(solution)/shard_map/cond/branch_1_fun/shared_projection/pallas_call | solution.py:385
  62.6 3.2 %collective-permute-done.21 = bf16[112,512]{1,0:T(8,128)(2,1)S(1)} collective-permute-done((bf16[112,512]{1,0:T(8,128)(2,1)S(1)}, bf16[112,512]{1,0:T(8,128)(2,1)S(1)}, u32[]{:S(2)}, u32[]{:S(2)}) %collective-permute-start.21) | collective-permute-done | bytes 114720 | tf_op jit(solution)/shard_map/ppermute | solution.py:44
  65.9 1.2 %conditional.9 = (bf16[256,512]{1,0:T(8,128)(2,1)}) conditional(s32[]{:T(128)} %bitcast.10, (f32[256,512]{1,0:T(8,128)S(1)}, f32[256,128]{1,0:T(8,128)S(1)}, bf16[112,512]{1,0:T(8,128)(2,1)S(1)}, bf16[112,512]{1,0:T(8,128)(2,1)S(1)}, bf16[112,512]{1,0:T(8,128)(2,1)S(1)}, /*index=5*/bf16[112,512]{1,0:T(8,128)(2,1)S(1)}) %tuple.87, ...), branch_computations={%region_8.0_spmd, %region_9.0_spmd} | conditional | flops 1624249 | bytes 73226744 | solution.py:590
  (25 shorter events, 4.9 us)
Async XLA Ops:
  3.2 53.2 %collective-permute-start.16 = (bf16[256,2048]{1,0:T(8,128)(2,1)}, bf16[256,2048]{1,0:T(8,128)(2,1)}, u32[]{:S(2)}, u32[]{:S(2)}) collective-permute-start(bf16[256,2048]{1,0:T(8,128)(2,1)} %act_ref.1), channel_id=1, source_target_pairs={{0,2},{1,3},{2,0},{3,1},{4,6},{5,7},{6,4},{7,5},{8,10},{9,11},{10,... | collective-permute-start | bytes 3145736 | tf_op jit(solution)/shard_map/ppermute | solution.py:44
  6.2 22.0 %collective-permute-start.15 = (bf16[112,2048]{1,0:T(8,128)(2,1)}, bf16[112,2048]{1,0:T(8,128)(2,1)S(1)}, u32[]{:S(2)}, u32[]{:S(2)}) collective-permute-start(bf16[112,2048]{1,0:T(8,128)(2,1)} %get-tuple-element.410), channel_id=1, source_target_pairs={{0,4},{4,0},{8,12},{12,8},{1,5},{5,1},{9,13},{13,9},{2,6},{6,2},{1... | collective-permute-start | bytes 1376264 | tf_op jit(solution)/shard_map/ppermute | solution.py:44
  7.8 19.7 %collective-permute-start.13 = (bf16[48,2048]{1,0:T(8,128)(2,1)S(1)}, bf16[48,2048]{1,0:T(8,128)(2,1)S(1)}, u32[]{:S(2)}, u32[]{:S(2)}) collective-permute-start(bf16[48,2048]{1,0:T(8,128)(2,1)S(1)} %get-tuple-element.409), channel_id=1, source_target_pairs={{0,8},{4,12},{8,0},{12,4},{1,9},{5,13},{9,1},{13,5},{2,10},{6,14},... | collective-permute-start | bytes 589832 | tf_op jit(solution)/shard_map/ppermute | solution.py:44
  11.1 3.1 %collective-permute-start = (bf16[256,2048]{1,0:T(8,128)(2,1)}, bf16[256,2048]{1,0:T(8,128)(2,1)}, u32[]{:S(2)}, u32[]{:S(2)}) collective-permute-start(bf16[256,2048]{1,0:T(8,128)(2,1)} %get-tuple-element.295.act_ref), channel_id=1, source_target_pairs={{0,1},{1,0},{2,3},{3,2},{4,5},{5,4},{6,7},{7,6},{8,9},{9,8},{10,11... | collective-permute-start | bytes 3145736 | tf_op jit(solution)/shard_map/cond/branch_1_fun/ppermute | solution.py:44
  14.1 25.6 %collective-permute-start.11 = (bf16[64,2048]{1,0:T(8,128)(2,1)S(1)}, bf16[64,2048]{1,0:T(8,128)(2,1)S(1)}, u32[]{:S(2)}, u32[]{:S(2)}) collective-permute-start(bf16[64,2048]{1,0:T(8,128)(2,1)S(1)} %get-tuple-element.413), channel_id=1, source_target_pairs={{0,8},{4,12},{8,0},{12,4},{1,9},{5,13},{9,1},{13,5},{2,10},{6,14},... | collective-permute-start | bytes 786440 | tf_op jit(solution)/shard_map/ppermute | solution.py:44
  14.5 25.3 %collective-permute-start.12 = (bf16[64,2048]{1,0:T(8,128)(2,1)S(1)}, bf16[64,2048]{1,0:T(8,128)(2,1)S(1)}, u32[]{:S(2)}, u32[]{:S(2)}) collective-permute-start(bf16[64,2048]{1,0:T(8,128)(2,1)S(1)} %get-tuple-element.414), channel_id=1, source_target_pairs={{0,12},{4,8},{8,4},{12,0},{1,13},{5,9},{9,5},{13,1},{2,14},{6,10},... | collective-permute-start | bytes 786440 | tf_op jit(solution)/shard_map/ppermute | solution.py:44
  27.5 14.5 %collective-permute-start.14 = (bf16[48,2048]{1,0:T(8,128)(2,1)S(1)}, bf16[48,2048]{1,0:T(8,128)(2,1)S(1)}, u32[]{:S(2)}, u32[]{:S(2)}) collective-permute-start(bf16[48,2048]{1,0:T(8,128)(2,1)S(1)} %collective-permute-done.13.refs_0_), channel_id=1, source_target_pairs={{0,4},{4,0},{8,12},{12,8},{1,5},{5,1},{9,13},{13,9},{2,6},{6,2},{1... | collective-permute-start | bytes 589832 | tf_op jit(solution)/shard_map/ppermute | solution.py:44
  45.4 1.9 %collective-permute-start.17 = (bf16[224,128]{1,0:T(8,128)(2,1)S(1)}, bf16[224,128]{1,0:T(8,128)(2,1)S(1)}, u32[]{:S(2)}, u32[]{:S(2)}) collective-permute-start(bf16[224,128]{1,0:T(8,128)(2,1)S(1)} %get-tuple-element.438), channel_id=1, source_target_pairs={{0,1},{1,0},{2,3},{3,2},{4,5},{5,4},{6,7},{7,6},{8,9},{9,8},{10,11... | collective-permute-start | bytes 172040 | tf_op jit(solution)/shard_map/ppermute | solution.py:44
  45.5 4.8 %collective-permute-start.18 = (bf16[224,128]{1,0:T(8,128)(2,1)S(1)}, bf16[224,128]{1,0:T(8,128)(2,1)S(1)}, u32[]{:S(2)}, u32[]{:S(2)}) collective-permute-start(bf16[224,128]{1,0:T(8,128)(2,1)S(1)} %get-tuple-element.439), channel_id=1, source_target_pairs={{0,2},{1,3},{2,0},{3,1},{4,6},{5,7},{6,4},{7,5},{8,10},{9,11},{10,... | collective-permute-start | bytes 172040 | tf_op jit(solution)/shard_map/ppermute | solution.py:44
  46.1 4.5 %collective-permute-start.19 = (bf16[224,128]{1,0:T(8,128)(2,1)S(1)}, bf16[224,128]{1,0:T(8,128)(2,1)S(1)}, u32[]{:S(2)}, u32[]{:S(2)}) collective-permute-start(bf16[224,128]{1,0:T(8,128)(2,1)S(1)} %get-tuple-element.440), channel_id=1, source_target_pairs={{0,3},{1,2},{2,1},{3,0},{4,7},{5,6},{6,5},{7,4},{8,11},{9,10},{10,... | collective-permute-start | bytes 172040 | tf_op jit(solution)/shard_map/ppermute | solution.py:44
  51.3 11.3 %collective-permute-start.20 = (bf16[112,512]{1,0:T(8,128)(2,1)S(1)}, bf16[112,512]{1,0:T(8,128)(2,1)S(1)}, u32[]{:S(2)}, u32[]{:S(2)}) collective-permute-start(bf16[112,512]{1,0:T(8,128)(2,1)S(1)} %get-tuple-element.442), channel_id=1, source_target_pairs={{0,12},{4,8},{8,4},{12,0},{1,13},{5,9},{9,5},{13,1},{2,14},{6,10},... | collective-permute-start | bytes 344072 | tf_op jit(solution)/shard_map/ppermute | solution.py:44
  51.6 14.3 %collective-permute-start.21 = (bf16[112,512]{1,0:T(8,128)(2,1)S(1)}, bf16[112,512]{1,0:T(8,128)(2,1)S(1)}, u32[]{:S(2)}, u32[]{:S(2)}) collective-permute-start(bf16[112,512]{1,0:T(8,128)(2,1)S(1)} %get-tuple-element.443), channel_id=1, source_target_pairs={{0,8},{4,12},{8,0},{12,4},{1,9},{5,13},{9,1},{13,5},{2,10},{6,14},... | collective-permute-start | bytes 344072 | tf_op jit(solution)/shard_map/ppermute | solution.py:44
  55.9 9.9 %collective-permute-start.22 = (bf16[112,512]{1,0:T(8,128)(2,1)S(1)}, bf16[112,512]{1,0:T(8,128)(2,1)S(1)}, u32[]{:S(2)}, u32[]{:S(2)}) collective-permute-start(bf16[112,512]{1,0:T(8,128)(2,1)S(1)} %get-tuple-element.444), channel_id=1, source_target_pairs={{0,4},{4,0},{8,12},{12,8},{1,5},{5,1},{9,13},{13,9},{2,6},{6,2},{1... | collective-permute-start | bytes 344072 | tf_op jit(solution)/shard_map/ppermute | solution.py:44
  56.5 9.4 %copy-start.3 = (s32[256,1]{0,1:T(1,128)S(1)}, s32[256,1]{0,1:T(1,128)}, u32[]{:S(2)}) copy-start(s32[256,1]{0,1:T(1,128)} %param.19) | copy-start | bytes 3076
  56.5 9.4 %copy-start.4 = (s32[64]{0:T(128)S(1)}, s32[64]{0:T(128)}, u32[]{:S(2)}) copy-start(s32[64]{0:T(128)} %param.20) | copy-start | bytes 772
  56.5 3.3 %collective-permute-start.1 = (bf16[256,2048]{1,0:T(8,128)(2,1)}, bf16[256,2048]{1,0:T(8,128)(2,1)S(1)}, u32[]{:S(2)}, u32[]{:S(2)}) collective-permute-start(bf16[256,2048]{1,0:T(8,128)(2,1)} %get-tuple-element.313.refs_0_), channel_id=1, source_target_pairs={{0,1},{1,0},{2,3},{3,2},{4,5},{5,4},{6,7},{7,6},{8,9},{9,8},{10,11... | collective-permute-start | bytes 3145736 | tf_op jit(solution)/shard_map/cond/branch_1_fun/ppermute | solution.py:44

commit v4 on v3

--- a/solution.py
+++ b/solution.py
@@ -15,6 +15,7 @@
 FAR_ROWS = 64
 SHARED_ROWS = 48
 LATER_ROWS = 32
+DOWN_SCALE = 6
 VMEM = pltpu.VMEM
 MIB = 1 << 20
 
@@ -28,11 +29,12 @@
     shares = FAR_ROWS - 1 < local_count * MOST
 
     near = [(k, False, plain[k]) for k in range(min(2, wide_size))][::-1]
-    direct = [(k, True, SHARED_ROWS) for k in far[::2]] if shares else []
-    passed = [(k, True, SHARED_ROWS) for k in far[1::2]] if shares else []
-    apart = [(k, False, plain[k]) for k in far]
-    leaving = [*direct, *near[:-1], *apart, near[-1]]
-    return leaving, [*direct, *near], [*apart, *passed]
+    apart, passed = [], []
+    for k in far[::-1]:
+        apart += [(k, False, plain[k])] + [(k, True, SHARED_ROWS)] * (shares and k % 2)
+        passed += [(k, True, SHARED_ROWS)] * (shares and k % 2 == 0)
+    ahead = 1 + shares if apart else 1
+    return [*apart, *near], [*apart[:ahead], *near], [*apart[ahead:], *passed]
 
 
 def answer_order(early, rest):
@@ -77,6 +79,9 @@
     last_span = span[1] == len(layout)
     place_ref, refs = (refs[0], refs[1:]) if last_span else (None, refs)
     blocks = dict(zip(picked, refs[:-2]))
+    if len(refs) - 2 < len(picked):
+        starts = [sum(layout[m][2] for m in picked[:n]) for n in range(len(picked))]
+        blocks = {n: refs[0].at[pl.ds(start, layout[n][2]), :] for n, start in zip(picked, starts)}
     act_held, in_sem = refs[-2:]
     rows, features = act_held.shape
     chunks = 4
@@ -179,10 +184,13 @@
         place_ref[...] = jnp.broadcast_to(place.astype(f32), (LANES, rows)).T
 
 
-def pack(where, tenant, slot, activations, local_count, wide_size, turns, span, later):
+def pack(
+    where, tenant, slot, activations, local_count, wide_size, turns, span, later, in_one=False
+):
     rows, features = activations.shape
     total = wide_size if later else len(turns[0])
     counts = [LATER_ROWS if later else turns[0][n][2] for n in range(*span)]
+    counts = [sum(counts)] if in_one else counts
     places = [jax.ShapeDtypeStruct((rows, LANES), f32)] if span[1] == total else []
     loads = 4
     whole = pl.BlockSpec(memory_space=VMEM)
@@ -236,8 +244,8 @@
     )(in_hbm(down_weight), in_hbm(up_weight))
 
 
-def down_kernel(shifts, cols, narrow_size, per_step, where_ref, weight_ref, *refs):
-    count = len(shifts)
+def down_kernel(views, cols, narrow_size, per_step, where_ref, weight_ref, *refs):
+    count = len(views)
     xs, refs = refs[:count], refs[count:]
     before, refs = (refs[:3], refs[3:]) if narrow_size else ((), refs)
     flag_ref, ids_ref, *outs, held_ref = refs
@@ -246,10 +254,9 @@
     flag = jnp.zeros((1, LANES), f32)
     ids = []
     offset = 0
-    for x, shift in zip(xs, shifts):
-        rows = x.shape[0]
-        held_ref[pl.ds(offset, rows), :] = x[...]
-        last = x[pl.ds(rows - 16, 16), :LANES].astype(f32)[15:]
+    for x, (begin, rows, shift) in zip(xs, views):
+        held_ref[pl.ds(offset, rows), :] = x[pl.ds(begin, rows), :]
+        last = x[pl.ds(begin + rows - 16, 16), :LANES].astype(f32)[15:]
         flag = jnp.maximum(flag, last)
         turned = jnp.broadcast_to(last, (LANES, LANES)).T[:rows]
         keep = lax.broadcasted_iota(i32, (rows, LANES), 0) < rows - 1
@@ -293,9 +300,9 @@
         outs[j][...] = jnp.where(start >= KEY_VALUE_COLS, values, keys).astype(outs[j].dtype)
 
 
-def down(where, blocks, shifts, weight, cols, before, narrow_size, scale):
+def down(where, blocks, views, weight, cols, before, narrow_size, scale):
     features, width = weight.shape
-    new_rows = sum(b.shape[0] for b in blocks)
+    new_rows = sum(rows for _, rows, _ in views)
     per_step = min(4, width // LANES)
     whole = pl.BlockSpec(memory_space=VMEM)
     scalar = pl.BlockSpec(memory_space=pltpu.SMEM)
@@ -306,7 +313,7 @@
         rows = new_rows
         sums = [((rows, LANES), f32)]
     return pl.pallas_call(
-        functools.partial(down_kernel, shifts, cols, narrow_size, per_step),
+        functools.partial(down_kernel, views, cols, narrow_size, per_step),
         out_shape=[
             jax.ShapeDtypeStruct((1, 1), i32),
             jax.ShapeDtypeStruct((rows, LANES), f32),
@@ -461,10 +468,10 @@
     got = [swap(b, "wide", k) if k else b for k, b in enumerate(sent)]
     cols = up_weight.shape[1]
     down_weight, up_weight = stage(down_weight, up_weight)
-    shifts = [0] * wide_size
-    before = down(where, got[:1], shifts[:1], down_weight, cols, None, 0, 0.001)
+    views = [(0, LATER_ROWS, 0)] * wide_size
+    before = down(where, got[:1], views[:1], down_weight, cols, None, 0, 0.001)
     more, ids, *sums = down(
-        where, got[1:], shifts[1:], down_weight, cols, before, narrow_size, 0.001
+        where, got[1:], views[1:], down_weight, cols, before, narrow_size, 0.001
     )
     pieces = [[(k * LATER_ROWS, LATER_ROWS)] for k in range(wide_size)]
     outs = raise_sums(ids, sums, up_weight, pieces)
@@ -494,8 +501,11 @@
     leaving, early, rest = turns
     own = len(leaving) - 1
     routed = (local_count, wide_size, turns)
-    ahead = min(own, 1 + sum(shared for _, shared, _ in leaving))
-    begun, *sent = pack(where, tenant, slot, activations, *routed, (0, ahead), False)
+    ahead = 1 + sum(shared for _, shared, _ in leaving[:2])
+    begun, first = pack(where, tenant, slot, activations, *routed, (0, ahead), False, True)
+    sent = []
+    if own > ahead:
+        sent = pack(where, tenant, slot, after(activations, first), *routed, (ahead, own), False)[1:]
     half = narrow_size // 2
 
     def step(work, *operands):
@@ -513,52 +523,49 @@
             bit //= 2
         return [acts[j] for j in sorted(acts)]
 
-    def pack_away(tenant, slot, activations):
-        blocks = pack(where, tenant, slot, activations, *routed, (ahead, own), False)[1:]
-        return blocks, spread(activations)[1:]
-
     def pack_own(tenant, slot, activations):
         return pack(where, tenant, slot, activations, *routed, (own, own + 1), False)[1:]
 
-    def work_before(acts, shared_weight, maps):
-        return base(where, acts, 0, shared_weight, None), stage(*maps)
+    def work_before(activations, shared_weight, maps):
+        return base(where, spread(activations), 0, shared_weight, None), stage(*maps)
 
     def work_after(across, shared_weight, base_out):
         for n, act in enumerate(spread(across)):
             base_out = base(where, [act], half + n, shared_weight, base_out)
         return base_out
 
-    if own == ahead:
-        acts = spread(activations)[1:]
-    else:
-        away, acts = step(pack_away, tenant, slot, after(activations, *sent))
-        sent += away
-    acts = [activations, *acts]
     got = {}
-    for (k, shared, _), block in zip(leaving, sent):
-        got[k, shared] = swap(block, "wide", k)
-    shared_weight, maps = after_all((shared_weight, (adapter_down_weight, up_weight)), *sent)
-    place, own_block = step(pack_own, tenant, slot, after(activations, *sent))
-    got[0, False] = own_block
-    across = swap(after(activations, *sent[:ahead]), "narrow", half) if half else None
+    arrived = swap(first, "wide", leaving[0][0])
+    for n, (k, shared, count) in enumerate(leaving[:ahead]):
+        got[k, shared] = arrived, sum(entry[2] for entry in leaving[:n])
+    for (k, shared, _), block in zip(leaving[ahead:], sent):
+        got[k, shared] = swap(block, "wide", k), 0
+    shared_weight, maps = after_all((shared_weight, (adapter_down_weight, up_weight)), first, *sent)
+    place, own_block = step(pack_own, tenant, slot, after(activations, first, *sent))
+    across = swap(after(activations, own_block), "narrow", half) if half else None
     base_out, (down_beside, up_beside) = step(
-        work_before, *after_all((acts, shared_weight, maps), own_block)
-    )
-
-    for k, shared, _ in leaving:
+        work_before, *after_all((activations, shared_weight, maps), own_block)
+    )
+    got[0, False] = after(own_block, base_out), 0
+    for k, shared, count in leaving:
         if shared:
-            got[k ^ 1, True] = swap(after(got[k, True], base_out), "wide", 1)
+            block, begin = got[k, True]
+            block = after(block, base_out)
+            got[k ^ 1, True] = swap(block[begin : begin + count], "wide", 1), 0
 
     def blocks_of(entries):
-        shifts = [local_count if shared and k % 2 else 0 for k, shared, _ in entries]
-        return [got[k, shared] for k, shared, _ in entries], shifts
-
-    blocks, shifts = blocks_of(early)
-    blocks[-1] = after(blocks[-1], base_out)
-    before = down(where, blocks, shifts, down_beside, cols, None, 0, 0.001)
-    blocks, shifts = blocks_of(rest)
+        blocks = [got[k, shared][0] for k, shared, _ in entries]
+        views = [
+            (got[k, shared][1], count, local_count if shared and k % 2 == 0 else 0)
+            for k, shared, count in entries
+        ]
+        return blocks, views
+
+    blocks, views = blocks_of(early)
+    before = down(where, blocks, views, down_beside, cols, None, 0, 0.001)
+    blocks, views = blocks_of(rest)
     more, ids, *sums = down(
-        where, after_all(blocks, *before), shifts, down_beside, cols, before, narrow_size, 0.001
+        where, after_all(blocks, *before), views, down_beside, cols, before, narrow_size, DOWN_SCALE
     )
     starts, start = {}, 0
     for k, shared, count in early + rest:

time: 67.6 us -> 63.2 us (0.935)
  waiting for transfers between devices: 17.4 us -> 10.6 us
  starting transfers between devices: 17.4 us -> 19.6 us
    ppermute x14 -> x13, waiting for transfers between devices: 17.4 us -> 10.6 us  [swap(): return lax.ppermute(x, axis, [(i, i ^ k) for i in range(size)])]
    ppermute x14 -> x13, starting transfers between devices: 17.4 us -> 19.6 us  [swap(): return lax.ppermute(x, axis, [(i, i ^ k) for i in range(size)])]
  transfers between devices with their start and end apart: 14 -> 13, of which waited for: 6 -> 4; matrix products, arithmetic and copies ran while one was open for 0% -> 0% of each run, Pallas kernels for 39% -> 44%
where the time goes in v4:
time: 63.2 us; the launch traced here: 62.9 us
  Pallas kernels  30.8 us (49%)
  starting transfers between devices  19.6 us (31%)
  waiting for transfers between devices  10.6 us (17%)
  between operations  1.5 us (2%)
    ppermute x13, starting transfers between devices, swap(): return lax.ppermute(x, axis, [(i, i ^ k) for i in range(size)])  19.6 us
    ppermute x13, waiting for transfers between devices, swap(): return lax.ppermute(x, axis, [(i, i ^ k) for i in range(size)])  10.6 us
    pallas_call x3, Pallas kernels, base(): pl.pallas_call(functools.partial(base_kernel, count), grid_spec=pltpu.Pre...  9.87 us
    pallas_call x3, Pallas kernels, pack(): pl.pallas_call(functools.partial(pack_kernel, local_count, wide_size, tur...  7.93 us
    pallas_call x2, Pallas kernels, down(): pl.pallas_call(functools.partial(down_kernel, views, cols, narrow_size, p...  7.4 us
    pallas_call x1, Pallas kernels, stage(): pl.pallas_call(stage_kernel, out_shape=[pltpu.VMEM((features, adapters *...  3.86 us
  transfers between devices with their start and end apart: 13, of which 4 were waited for; matrix products, arithmetic and copies ran while one was open for 0% of the time, Pallas kernels for 44%

profile of v4, /device:TPU:0, one launch (start us, length us, event | category | flops | bytes accessed | tf_op | source)
XLA Modules:
  0.0 62.9 jit_solution(5264522114232535850)
XLA Ops:
  0.1 2.4 %pack_rows.9 = (s32[1,1]{1,0:T(1,128)}, bf16[112,2048]{1,0:T(8,128)(2,1)S(1)}) custom-call(s32[3]{0:T(128)S(1)} %pad_add_fusion.1.where_ref, s32[1,256]{1,0:T(1,128)} %bitcast.21, s32[1,64]{1,0:T(1,128)} %bitcast.25, bf16[256,2048]{1,0:T(8,128)(2,1)} %act_ref.2), custom_call_target="tpu_custom_call" | custom-call | flops 117440 | bytes 1507 | tf_op jit(solution)/shard_map/pack_rows/pallas_call | solution.py:198
  2.5 5.1 %collective-permute-start.12 = (bf16[112,2048]{1,0:T(8,128)(2,1)S(1)}, bf16[112,2048]{1,0:T(8,128)(2,1)S(1)}, u32[]{:S(2)}, u32[]{:S(2)}) collective-permute-start(bf16[112,2048]{1,0:T(8,128)(2,1)S(1)} %get-tuple-element.389), channel_id=1, source_target_pairs={{0,12},{4,8},{8,4},{12,0},{1,13},{5,9},{9,5},{13,1},{2,14},{6,10},... | collective-permute-start | bytes 1376264 | tf_op jit(solution)/shard_map/ppermute | solution.py:46
  7.6 3.1 %pack_rows.10 = (s32[1,1]{1,0:T(1,128)}, bf16[64,2048]{1,0:T(8,128)(2,1)}, bf16[112,2048]{1,0:T(8,128)(2,1)S(1)}) custom-call(s32[3]{0:T(128)S(1)} %pad_add_fusion.1.where_ref, s32[1,256]{1,0:T(1,128)} %bitcast.22, s32[1,64]{1,0:T(1,128)} %bitcast.26, bf16[256,2048]{1,0:T(8,128)(2,1)} %act_ref.2), custom_call_target="tpu_custom_call" | custom-call | flops 184549 | bytes 1769 | tf_op jit(solution)/shard_map/pack_rows/pallas_call | solution.py:198
  11.3 2.5 %conditional.4 = (f32[256,128]{1,0:T(8,128)S(1)}, bf16[112,2048]{1,0:T(8,128)(2,1)S(1)}) conditional(s32[]{:T(128)} %bitcast.8, () %tuple.67, (s32[3]{0:T(128)S(1)}, s32[1,256]{1,0:T(1,128)}, s32[1,64]{1,0:T(1,128)}, bf16[256,2048]{1,0:T(8,128)(2,1)}) %tuple.107), branch_computations={%region_0.0_spmd, %region_1.0_spmd} | conditional | flops 117440 | bytes 589846 | solution.py:517
  11.4 2.4 %pack_rows.8 = (s32[1,1]{1,0:T(1,128)}, f32[256,128]{1,0:T(8,128)S(1)}, bf16[112,2048]{1,0:T(8,128)(2,1)S(1)}) custom-call(s32[3]{0:T(128)S(1)} %get-tuple-element.282.where_ref, s32[1,256]{1,0:T(1,128)} %get-tuple-element.283.tenant_ref, s32[1,64]{1,0:T(1,128)} %get-tuple-element.284.slot_ref, bf16[256,2048]{1,0:T(8,128)(2,1)} %get-tuple-element.285.act_ref), custom_call_target="tpu_custom_call" | custom-call | flops 117440 | bytes 1507 | tf_op jit(solution)/shard_map/cond/branch_1_fun/pack_rows/pallas_call | solution.py:198
  13.8 1.6 %collective-permute-start.15 = (bf16[256,2048]{1,0:T(8,128)(2,1)}, bf16[256,2048]{1,0:T(8,128)(2,1)}, u32[]{:S(2)}, u32[]{:S(2)}) collective-permute-start(bf16[256,2048]{1,0:T(8,128)(2,1)} %act_ref.2), channel_id=1, source_target_pairs={{0,2},{1,3},{2,0},{3,1},{4,6},{5,7},{6,4},{7,5},{8,10},{9,11},{10,... | collective-permute-start | bytes 3145736 | tf_op jit(solution)/shard_map/ppermute | solution.py:46
  16.1 7.8 %conditional.5 = (f32[256,512]{1,0:T(8,128)S(1)}, bf16[2048,2048]{1,0:T(8,128)(2,1)S(1)}, bf16[1024,512]{1,0:T(8,128)(2,1)S(1)}) conditional(s32[]{:T(128)} %bitcast.8, () %tuple.64, (bf16[256,2048]{1,0:T(8,128)(2,1)}, s32[3]{0:T(128)S(1)}, bf16[8192,512]{1,0:T(8,128)(2,1)}, bf16[16,2048,128]{2,1,0:T(8,128)(2,1)}, bf16[1024,512]{1,0:T(8,128)(2,1)}) %tuple.103), branch_computations={%region_2.0_spmd, %region_3.0_spmd} | conditional | flops 1073741 | bytes 9961504 | solution.py:517
  16.1 3.9 %stage_maps.4 = (bf16[2048,2048]{1,0:T(8,128)(2,1)S(1)}, bf16[1024,512]{1,0:T(8,128)(2,1)S(1)}) custom-call(bf16[16,2048,128]{2,1,0:T(8,128)(2,1)} %get-tuple-element.291.down_ref, bf16[1024,512]{1,0:T(8,128)(2,1)} %get-tuple-element.292.up_ref), custom_call_target="tpu_custom_call" | custom-call | tf_op jit(solution)/shard_map/cond/branch_1_fun/stage_maps/pallas_call | solution.py:232
  20.0 3.9 %shared_projection.3 = f32[256,512]{1,0:T(8,128)S(1)} custom-call(s32[3]{0:T(128)S(1)} %get-tuple-element.288.where_ref, bf16[256,2048]{1,0:T(8,128)(2,1)} %get-tuple-element.289.refs_0_, bf16[256,2048]{1,0:T(8,128)(2,1)S(1)} %collective-permute-done.refs_1_, bf16[8192,512]{1,0:T(8,128)(2,1)} %get-tuple-element.290.refs_2_), custom_call_target="tpu_custom_call" | custom-call | flops 1073741 | bytes 6291 | tf_op jit(solution)/shard_map/cond/branch_1_fun/shared_projection/pallas_call | solution.py:392
  23.9 5.7 %collective-permute-start.13 = (bf16[48,2048]{1,0:T(8,128)(2,1)S(1)}, bf16[48,2048]{1,0:T(8,128)(2,1)S(1)}, u32[]{:S(2)}, u32[]{:S(2)}) collective-permute-start(bf16[48,2048]{1,0:T(8,128)(2,1)S(1)} %slice.3), channel_id=1, source_target_pairs={{0,4},{4,0},{8,12},{12,8},{1,5},{5,1},{9,13},{13,9},{2,6},{6,2},{1... | collective-permute-start | bytes 589832 | tf_op jit(solution)/shard_map/ppermute | solution.py:46
  29.6 3.9 %down_maps.12 = (s32[1,1]{1,0:T(1,128)}, f32[336,128]{1,0:T(8,128)S(1)}, f32[336,128]{1,0:T(8,128)S(1)}) custom-call(s32[3]{0:T(128)S(1)} %pad_add_fusion.1.where_ref, bf16[2048,2048]{1,0:T(8,128)(2,1)S(1)} %get-tuple-element.402.weight_ref, bf16[112,2048]{1,0:T(8,128)(2,1)S(1)} %collective-permute-done.12.refs_0_.refs_1_, ...), custom_call_target="tpu_custom_call" | custom-call | flops 2818572 | bytes 9764 | tf_op jit(solution)/shard_map/down_maps/pallas_call | solution.py:315
  33.5 4.9 %collective-permute-done.11.refs_0_ = bf16[64,2048]{1,0:T(8,128)(2,1)} collective-permute-done((bf16[64,2048]{1,0:T(8,128)(2,1)}, bf16[64,2048]{1,0:T(8,128)(2,1)}, u32[]{:S(2)}, u32[]{:S(2)}) %collective-permute-start.11) | collective-permute-done | bytes 262176 | tf_op jit(solution)/shard_map/ppermute | solution.py:46
  38.5 3.5 %down_maps.13 = (s32[1,1]{1,0:T(1,128)}, f32[448,128]{1,0:T(8,128)S(1)}, f32[224,128]{1,0:T(8,128)S(1)}, bf16[224,128]{1,0:T(8,128)(2,1)S(1)}, bf16[224,128]{1,0...) custom-call(s32[3]{0:T(128)S(1)} %pad_add_fusion.1.where_ref, bf16[2048,2048]{1,0:T(8,128)(2,1)S(1)} %get-tuple-element.402.weight_ref, ...), custom_call_target="tpu_custom_call" | custom-call | flops 5637144576 | bytes 53084160 | tf_op jit(solution)/shard_map/down_maps/pallas_call | solution.py:315
  42.0 1.6 %collective-permute-start.17 = (bf16[224,128]{1,0:T(8,128)(2,1)S(1)}, bf16[224,128]{1,0:T(8,128)(2,1)S(1)}, u32[]{:S(2)}, u32[]{:S(2)}) collective-permute-start(bf16[224,128]{1,0:T(8,128)(2,1)S(1)} %get-tuple-element.416), channel_id=1, source_target_pairs={{0,2},{1,3},{2,0},{3,1},{4,6},{5,7},{6,4},{7,5},{8,10},{9,11},{10,... | collective-permute-start | bytes 172040 | tf_op jit(solution)/shard_map/ppermute | solution.py:46
  43.9 2.5 %collective-permute-done.17.refs_2_ = bf16[224,128]{1,0:T(8,128)(2,1)S(1)} collective-permute-done((bf16[224,128]{1,0:T(8,128)(2,1)S(1)}, bf16[224,128]{1,0:T(8,128)(2,1)S(1)}, u32[]{:S(2)}, u32[]{:S(2)}) %collective-permute-start.17) | collective-permute-done | bytes 57376 | tf_op jit(solution)/shard_map/ppermute | solution.py:46
  46.4 1.1 %collective-permute-done.18.refs_3_ = bf16[224,128]{1,0:T(8,128)(2,1)S(1)} collective-permute-done((bf16[224,128]{1,0:T(8,128)(2,1)S(1)}, bf16[224,128]{1,0:T(8,128)(2,1)S(1)}, u32[]{:S(2)}, u32[]{:S(2)}) %collective-permute-start.18) | collective-permute-done | bytes 57376 | tf_op jit(solution)/shard_map/ppermute | solution.py:46
  48.1 3.0 %collective-permute-start.19 = (bf16[112,512]{1,0:T(8,128)(2,1)S(1)}, bf16[112,512]{1,0:T(8,128)(2,1)S(1)}, u32[]{:S(2)}, u32[]{:S(2)}) collective-permute-start(bf16[112,512]{1,0:T(8,128)(2,1)S(1)} %get-tuple-element.419), channel_id=1, source_target_pairs={{0,12},{4,8},{8,4},{12,0},{1,13},{5,9},{9,5},{13,1},{2,14},{6,10},... | collective-permute-start | bytes 344072 | tf_op jit(solution)/shard_map/ppermute | solution.py:46
  51.2 1.4 %collective-permute-start.21 = (bf16[112,512]{1,0:T(8,128)(2,1)S(1)}, bf16[112,512]{1,0:T(8,128)(2,1)S(1)}, u32[]{:S(2)}, u32[]{:S(2)}) collective-permute-start(bf16[112,512]{1,0:T(8,128)(2,1)S(1)} %get-tuple-element.421), channel_id=1, source_target_pairs={{0,4},{4,0},{8,12},{12,8},{1,5},{5,1},{9,13},{13,9},{2,6},{6,2},{1... | collective-permute-start | bytes 344072 | tf_op jit(solution)/shard_map/ppermute | solution.py:46
  53.3 6.1 %conditional.6 = (f32[256,512]{1,0:T(8,128)S(1)}) conditional(s32[]{:T(128)} %bitcast.8, () %tuple.75, (bf16[256,2048]{1,0:T(8,128)(2,1)}, s32[3]{0:T(128)S(1)}, bf16[8192,512]{1,0:T(8,128)(2,1)}, f32[256,512]{1,0:T(8,128)S(1)}) %tuple.78), branch_computations={%region_4.0_spmd, %region_5.0_spmd} | conditional | flops 1073740 | bytes 4200642 | solution.py:517
  53.4 3.2 %shared_projection.4.refs_2_ = f32[256,512]{1,0:T(8,128)S(1)} custom-call(s32[3]{0:T(128)S(1)} %get-tuple-element.295.where_ref, bf16[256,2048]{1,0:T(8,128)(2,1)} %get-tuple-element.296.refs_0_, bf16[8192,512]{1,0:T(8,128)(2,1)} %get-tuple-element.297.refs_1_, f32[256,512]{1,0:T(8,128)S(1)} %get-tuple-element.298.refs_2_), custom_call_target="tpu_custom_call" | custom-call | flops 536870 | bytes 3145 | tf_op jit(solution)/shard_map/cond/branch_1_fun/shared_projection/pallas_call | solution.py:392
  56.6 2.8 %shared_projection.5 = f32[256,512]{1,0:T(8,128)S(1)} custom-call(s32[3]{0:T(128)S(1)} %get-tuple-element.295.where_ref, bf16[256,2048]{1,0:T(8,128)(2,1)S(1)} %collective-permute-done.1.refs_0_, bf16[8192,512]{1,0:T(8,128)(2,1)} %get-tuple-element.297.refs_1_, f32[256,512]{1,0:T(8,128)S(1)} %shared_projection.4.refs_2_), custom_call_target="tpu_custom_call" | custom-call | flops 536870 | bytes 3145 | tf_op jit(solution)/shard_map/cond/branch_1_fun/shared_projection/pallas_call | solution.py:392
  59.4 2.0 %collective-permute-done.20 = bf16[112,512]{1,0:T(8,128)(2,1)S(1)} collective-permute-done((bf16[112,512]{1,0:T(8,128)(2,1)S(1)}, bf16[112,512]{1,0:T(8,128)(2,1)S(1)}, u32[]{:S(2)}, u32[]{:S(2)}) %collective-permute-start.20) | collective-permute-done | bytes 114720 | tf_op jit(solution)/shard_map/ppermute | solution.py:46
  61.5 1.2 %conditional.7 = (bf16[256,512]{1,0:T(8,128)(2,1)}) conditional(s32[]{:T(128)} %bitcast.10, (f32[256,512]{1,0:T(8,128)S(1)}, f32[256,128]{1,0:T(8,128)S(1)}, bf16[112,512]{1,0:T(8,128)(2,1)S(1)}, bf16[112,512]{1,0:T(8,128)(2,1)S(1)}, bf16[112,512]{1,0:T(8,128)(2,1)S(1)}, /*index=5*/bf16[112,512]{1,0:T(8,128)(2,1)S(1)}) %tuple.79, ...), branch_computations={%region_6.0_spmd, %region_7.0_spmd} | conditional | flops 1624249 | bytes 73226744 | solution.py:597
  61.5 1.0 %join_corrections.7 = bf16[256,512]{1,0:T(8,128)(2,1)} custom-call(f32[256,512]{1,0:T(8,128)S(1)} %get-tuple-element.299.base_ref, f32[256,128]{1,0:T(8,128)S(1)} %get-tuple-element.300.place_ref, bf16[112,512]{1,0:T(8,128)(2,1)S(1)} %get-tuple-element.301.refs_0_, bf16[112,512]{1,0:T(8,128)(2,1)S(1)} %get-tuple-element.302.refs_1_, ...), custom_call_target="tpu_custom_call" | custom-call | flops 117440 | bytes 1245 | tf_op jit(solution)/shard_map/cond/branch_0_fun/join_corrections/pallas_call | solution.py:437
  (23 shorter events, 2.1 us)
Async XLA Ops:
  2.5 21.4 %collective-permute-start.12 = (bf16[112,2048]{1,0:T(8,128)(2,1)S(1)}, bf16[112,2048]{1,0:T(8,128)(2,1)S(1)}, u32[]{:S(2)}, u32[]{:S(2)}) collective-permute-start(bf16[112,2048]{1,0:T(8,128)(2,1)S(1)} %get-tuple-element.389), channel_id=1, source_target_pairs={{0,12},{4,8},{8,4},{12,0},{1,13},{5,9},{9,5},{13,1},{2,14},{6,10},... | collective-permute-start | bytes 1376264 | tf_op jit(solution)/shard_map/ppermute | solution.py:46
  10.7 18.9 %collective-permute-start.14 = (bf16[112,2048]{1,0:T(8,128)(2,1)S(1)}, bf16[112,2048]{1,0:T(8,128)(2,1)S(1)}, u32[]{:S(2)}, u32[]{:S(2)}) collective-permute-start(bf16[112,2048]{1,0:T(8,128)(2,1)S(1)} %get-tuple-element.392), channel_id=1, source_target_pairs={{0,4},{4,0},{8,12},{12,8},{1,5},{5,1},{9,13},{13,9},{2,6},{6,2},{1... | collective-permute-start | bytes 1376264 | tf_op jit(solution)/shard_map/ppermute | solution.py:46
  13.8 39.5 %collective-permute-start.15 = (bf16[256,2048]{1,0:T(8,128)(2,1)}, bf16[256,2048]{1,0:T(8,128)(2,1)}, u32[]{:S(2)}, u32[]{:S(2)}) collective-permute-start(bf16[256,2048]{1,0:T(8,128)(2,1)} %act_ref.2), channel_id=1, source_target_pairs={{0,2},{1,3},{2,0},{3,1},{4,6},{5,7},{6,4},{7,5},{8,10},{9,11},{10,... | collective-permute-start | bytes 3145736 | tf_op jit(solution)/shard_map/ppermute | solution.py:46
  15.4 23.1 %collective-permute-start.11 = (bf16[64,2048]{1,0:T(8,128)(2,1)}, bf16[64,2048]{1,0:T(8,128)(2,1)}, u32[]{:S(2)}, u32[]{:S(2)}) collective-permute-start(bf16[64,2048]{1,0:T(8,128)(2,1)} %get-tuple-element.391), channel_id=1, source_target_pairs={{0,8},{4,12},{8,0},{12,4},{1,9},{5,13},{9,1},{13,5},{2,10},{6,14},... | collective-permute-start | bytes 786440 | tf_op jit(solution)/shard_map/ppermute | solution.py:46
  16.1 3.9 %collective-permute-start = (bf16[256,2048]{1,0:T(8,128)(2,1)}, bf16[256,2048]{1,0:T(8,128)(2,1)S(1)}, u32[]{:S(2)}, u32[]{:S(2)}) collective-permute-start(bf16[256,2048]{1,0:T(8,128)(2,1)} %get-tuple-element.289.refs_0_), channel_id=1, source_target_pairs={{0,1},{1,0},{2,3},{3,2},{4,5},{5,4},{6,7},{7,6},{8,9},{9,8},{10,11... | collective-permute-start | bytes 3145736 | tf_op jit(solution)/shard_map/cond/branch_1_fun/ppermute | solution.py:46
  23.9 14.5 %collective-permute-start.13 = (bf16[48,2048]{1,0:T(8,128)(2,1)S(1)}, bf16[48,2048]{1,0:T(8,128)(2,1)S(1)}, u32[]{:S(2)}, u32[]{:S(2)}) collective-permute-start(bf16[48,2048]{1,0:T(8,128)(2,1)S(1)} %slice.3), channel_id=1, source_target_pairs={{0,4},{4,0},{8,12},{12,8},{1,5},{5,1},{9,13},{13,9},{2,6},{6,2},{1... | collective-permute-start | bytes 589832 | tf_op jit(solution)/shard_map/ppermute | solution.py:46
  41.9 1.9 %collective-permute-start.16 = (bf16[224,128]{1,0:T(8,128)(2,1)S(1)}, bf16[224,128]{1,0:T(8,128)(2,1)S(1)}, u32[]{:S(2)}, u32[]{:S(2)}) collective-permute-start(bf16[224,128]{1,0:T(8,128)(2,1)S(1)} %get-tuple-element.415), channel_id=1, source_target_pairs={{0,1},{1,0},{2,3},{3,2},{4,5},{5,4},{6,7},{7,6},{8,9},{9,8},{10,11... | collective-permute-start | bytes 172040 | tf_op jit(solution)/shard_map/ppermute | solution.py:46
  42.0 4.3 %collective-permute-start.17 = (bf16[224,128]{1,0:T(8,128)(2,1)S(1)}, bf16[224,128]{1,0:T(8,128)(2,1)S(1)}, u32[]{:S(2)}, u32[]{:S(2)}) collective-permute-start(bf16[224,128]{1,0:T(8,128)(2,1)S(1)} %get-tuple-element.416), channel_id=1, source_target_pairs={{0,2},{1,3},{2,0},{3,1},{4,6},{5,7},{6,4},{7,5},{8,10},{9,11},{10,... | collective-permute-start | bytes 172040 | tf_op jit(solution)/shard_map/ppermute | solution.py:46
  43.6 3.9 %collective-permute-start.18 = (bf16[224,128]{1,0:T(8,128)(2,1)S(1)}, bf16[224,128]{1,0:T(8,128)(2,1)S(1)}, u32[]{:S(2)}, u32[]{:S(2)}) collective-permute-start(bf16[224,128]{1,0:T(8,128)(2,1)S(1)} %get-tuple-element.417), channel_id=1, source_target_pairs={{0,3},{1,2},{2,1},{3,0},{4,7},{5,6},{6,5},{7,4},{8,11},{9,10},{10,... | collective-permute-start | bytes 172040 | tf_op jit(solution)/shard_map/ppermute | solution.py:46
  48.1 11.3 %collective-permute-start.19 = (bf16[112,512]{1,0:T(8,128)(2,1)S(1)}, bf16[112,512]{1,0:T(8,128)(2,1)S(1)}, u32[]{:S(2)}, u32[]{:S(2)}) collective-permute-start(bf16[112,512]{1,0:T(8,128)(2,1)S(1)} %get-tuple-element.419), channel_id=1, source_target_pairs={{0,12},{4,8},{8,4},{12,0},{1,13},{5,9},{9,5},{13,1},{2,14},{6,10},... | collective-permute-start | bytes 344072 | tf_op jit(solution)/shard_map/ppermute | solution.py:46
  51.2 10.3 %collective-permute-start.20 = (bf16[112,512]{1,0:T(8,128)(2,1)S(1)}, bf16[112,512]{1,0:T(8,128)(2,1)S(1)}, u32[]{:S(2)}, u32[]{:S(2)}) collective-permute-start(bf16[112,512]{1,0:T(8,128)(2,1)S(1)} %get-tuple-element.420), channel_id=1, source_target_pairs={{0,8},{4,12},{8,0},{12,4},{1,9},{5,13},{9,1},{13,5},{2,10},{6,14},... | collective-permute-start | bytes 344072 | tf_op jit(solution)/shard_map/ppermute | solution.py:46
  51.2 10.3 %collective-permute-start.21 = (bf16[112,512]{1,0:T(8,128)(2,1)S(1)}, bf16[112,512]{1,0:T(8,128)(2,1)S(1)}, u32[]{:S(2)}, u32[]{:S(2)}) collective-permute-start(bf16[112,512]{1,0:T(8,128)(2,1)S(1)} %get-tuple-element.421), channel_id=1, source_target_pairs={{0,4},{4,0},{8,12},{12,8},{1,5},{5,1},{9,13},{13,9},{2,6},{6,2},{1... | collective-permute-start | bytes 344072 | tf_op jit(solution)/shard_map/ppermute | solution.py:46
  53.3 8.2 %copy-start.3 = (s32[256,1]{0,1:T(1,128)S(1)}, s32[256,1]{0,1:T(1,128)}, u32[]{:S(2)}) copy-start(s32[256,1]{0,1:T(1,128)} %param.17) | copy-start | bytes 3076
  53.3 8.2 %copy-start.4 = (s32[64]{0:T(128)S(1)}, s32[64]{0:T(128)}, u32[]{:S(2)}) copy-start(s32[64]{0:T(128)} %param.18) | copy-start | bytes 772
  53.3 3.3 %collective-permute-start.1 = (bf16[256,2048]{1,0:T(8,128)(2,1)}, bf16[256,2048]{1,0:T(8,128)(2,1)S(1)}, u32[]{:S(2)}, u32[]{:S(2)}) collective-permute-start(bf16[256,2048]{1,0:T(8,128)(2,1)} %get-tuple-element.296.refs_0_), channel_id=1, source_target_pairs={{0,1},{1,0},{2,3},{3,2},{4,5},{5,4},{6,7},{7,6},{8,9},{9,8},{10,11... | collective-permute-start | bytes 3145736 | tf_op jit(solution)/shard_map/cond/branch_1_fun/ppermute | solution.py:46

commit v5 on v4

--- a/solution.py
+++ b/solution.py
@@ -303,7 +303,7 @@
 def down(where, blocks, views, weight, cols, before, narrow_size, scale):
     features, width = weight.shape
     new_rows = sum(rows for _, rows, _ in views)
-    per_step = min(4, width // LANES)
+    per_step = min(8, width // LANES)
     whole = pl.BlockSpec(memory_space=VMEM)
     scalar = pl.BlockSpec(memory_space=pltpu.SMEM)
     if narrow_size:

time: 63.2 us -> 63.2 us (level)
  no operation moved by 1% of the time
where the time goes in v5:
time: 63.2 us; the launch traced here: 62.9 us
  Pallas kernels  30.8 us (49%)
  starting transfers between devices  19.6 us (31%)
  waiting for transfers between devices  10.6 us (17%)
  between operations  1.5 us (2%)
    ppermute x13, starting transfers between devices, swap(): return lax.ppermute(x, axis, [(i, i ^ k) for i in range(size)])  19.6 us
    ppermute x13, waiting for transfers between devices, swap(): return lax.ppermute(x, axis, [(i, i ^ k) for i in range(size)])  10.6 us
    pallas_call x3, Pallas kernels, base(): pl.pallas_call(functools.partial(base_kernel, count), grid_spec=pltpu.Pre...  9.87 us
    pallas_call x3, Pallas kernels, pack(): pl.pallas_call(functools.partial(pack_kernel, local_count, wide_size, tur...  7.93 us
    pallas_call x2, Pallas kernels, down(): pl.pallas_call(functools.partial(down_kernel, views, cols, narrow_size, p...  7.4 us
    pallas_call x1, Pallas kernels, stage(): pl.pallas_call(stage_kernel, out_shape=[pltpu.VMEM((features, adapters *...  3.86 us
  transfers between devices with their start and end apart: 13, of which 4 were waited for; matrix products, arithmetic and copies ran while one was open for 0% of the time, Pallas kernels for 44%

profile of v5, /device:TPU:0, one launch (start us, length us, event | category | flops | bytes accessed | tf_op | source)
XLA Modules:
  0.0 62.9 jit_solution(5264522114232535850)
XLA Ops:
  0.1 2.4 %pack_rows.9 = (s32[1,1]{1,0:T(1,128)}, bf16[112,2048]{1,0:T(8,128)(2,1)S(1)}) custom-call(s32[3]{0:T(128)S(1)} %pad_add_fusion.1.where_ref, s32[1,256]{1,0:T(1,128)} %bitcast.21, s32[1,64]{1,0:T(1,128)} %bitcast.25, bf16[256,2048]{1,0:T(8,128)(2,1)} %act_ref.2), custom_call_target="tpu_custom_call" | custom-call | flops 117440 | bytes 1507 | tf_op jit(solution)/shard_map/pack_rows/pallas_call | solution.py:198
  2.5 5.1 %collective-permute-start.12 = (bf16[112,2048]{1,0:T(8,128)(2,1)S(1)}, bf16[112,2048]{1,0:T(8,128)(2,1)S(1)}, u32[]{:S(2)}, u32[]{:S(2)}) collective-permute-start(bf16[112,2048]{1,0:T(8,128)(2,1)S(1)} %get-tuple-element.389), channel_id=1, source_target_pairs={{0,12},{4,8},{8,4},{12,0},{1,13},{5,9},{9,5},{13,1},{2,14},{6,10},... | collective-permute-start | bytes 1376264 | tf_op jit(solution)/shard_map/ppermute | solution.py:46
  7.6 3.1 %pack_rows.10 = (s32[1,1]{1,0:T(1,128)}, bf16[64,2048]{1,0:T(8,128)(2,1)}, bf16[112,2048]{1,0:T(8,128)(2,1)S(1)}) custom-call(s32[3]{0:T(128)S(1)} %pad_add_fusion.1.where_ref, s32[1,256]{1,0:T(1,128)} %bitcast.22, s32[1,64]{1,0:T(1,128)} %bitcast.26, bf16[256,2048]{1,0:T(8,128)(2,1)} %act_ref.2), custom_call_target="tpu_custom_call" | custom-call | flops 184549 | bytes 1769 | tf_op jit(solution)/shard_map/pack_rows/pallas_call | solution.py:198
  11.3 2.5 %conditional.4 = (f32[256,128]{1,0:T(8,128)S(1)}, bf16[112,2048]{1,0:T(8,128)(2,1)S(1)}) conditional(s32[]{:T(128)} %bitcast.8, () %tuple.67, (s32[3]{0:T(128)S(1)}, s32[1,256]{1,0:T(1,128)}, s32[1,64]{1,0:T(1,128)}, bf16[256,2048]{1,0:T(8,128)(2,1)}) %tuple.107), branch_computations={%region_0.0_spmd, %region_1.0_spmd} | conditional | flops 117440 | bytes 589846 | solution.py:517
  11.4 2.4 %pack_rows.8 = (s32[1,1]{1,0:T(1,128)}, f32[256,128]{1,0:T(8,128)S(1)}, bf16[112,2048]{1,0:T(8,128)(2,1)S(1)}) custom-call(s32[3]{0:T(128)S(1)} %get-tuple-element.282.where_ref, s32[1,256]{1,0:T(1,128)} %get-tuple-element.283.tenant_ref, s32[1,64]{1,0:T(1,128)} %get-tuple-element.284.slot_ref, bf16[256,2048]{1,0:T(8,128)(2,1)} %get-tuple-element.285.act_ref), custom_call_target="tpu_custom_call" | custom-call | flops 117440 | bytes 1507 | tf_op jit(solution)/shard_map/cond/branch_1_fun/pack_rows/pallas_call | solution.py:198
  13.8 1.6 %collective-permute-start.15 = (bf16[256,2048]{1,0:T(8,128)(2,1)}, bf16[256,2048]{1,0:T(8,128)(2,1)}, u32[]{:S(2)}, u32[]{:S(2)}) collective-permute-start(bf16[256,2048]{1,0:T(8,128)(2,1)} %act_ref.2), channel_id=1, source_target_pairs={{0,2},{1,3},{2,0},{3,1},{4,6},{5,7},{6,4},{7,5},{8,10},{9,11},{10,... | collective-permute-start | bytes 3145736 | tf_op jit(solution)/shard_map/ppermute | solution.py:46
  16.1 7.8 %conditional.5 = (f32[256,512]{1,0:T(8,128)S(1)}, bf16[2048,2048]{1,0:T(8,128)(2,1)S(1)}, bf16[1024,512]{1,0:T(8,128)(2,1)S(1)}) conditional(s32[]{:T(128)} %bitcast.8, () %tuple.64, (bf16[256,2048]{1,0:T(8,128)(2,1)}, s32[3]{0:T(128)S(1)}, bf16[8192,512]{1,0:T(8,128)(2,1)}, bf16[16,2048,128]{2,1,0:T(8,128)(2,1)}, bf16[1024,512]{1,0:T(8,128)(2,1)}) %tuple.103), branch_computations={%region_2.0_spmd, %region_3.0_spmd} | conditional | flops 1073741 | bytes 9961504 | solution.py:517
  16.1 3.9 %stage_maps.4 = (bf16[2048,2048]{1,0:T(8,128)(2,1)S(1)}, bf16[1024,512]{1,0:T(8,128)(2,1)S(1)}) custom-call(bf16[16,2048,128]{2,1,0:T(8,128)(2,1)} %get-tuple-element.291.down_ref, bf16[1024,512]{1,0:T(8,128)(2,1)} %get-tuple-element.292.up_ref), custom_call_target="tpu_custom_call" | custom-call | tf_op jit(solution)/shard_map/cond/branch_1_fun/stage_maps/pallas_call | solution.py:232
  20.0 3.9 %shared_projection.3 = f32[256,512]{1,0:T(8,128)S(1)} custom-call(s32[3]{0:T(128)S(1)} %get-tuple-element.288.where_ref, bf16[256,2048]{1,0:T(8,128)(2,1)} %get-tuple-element.289.refs_0_, bf16[256,2048]{1,0:T(8,128)(2,1)S(1)} %collective-permute-done.refs_1_, bf16[8192,512]{1,0:T(8,128)(2,1)} %get-tuple-element.290.refs_2_), custom_call_target="tpu_custom_call" | custom-call | flops 1073741 | bytes 6291 | tf_op jit(solution)/shard_map/cond/branch_1_fun/shared_projection/pallas_call | solution.py:392
  23.9 5.7 %collective-permute-start.13 = (bf16[48,2048]{1,0:T(8,128)(2,1)S(1)}, bf16[48,2048]{1,0:T(8,128)(2,1)S(1)}, u32[]{:S(2)}, u32[]{:S(2)}) collective-permute-start(bf16[48,2048]{1,0:T(8,128)(2,1)S(1)} %slice.3), channel_id=1, source_target_pairs={{0,4},{4,0},{8,12},{12,8},{1,5},{5,1},{9,13},{13,9},{2,6},{6,2},{1... | collective-permute-start | bytes 589832 | tf_op jit(solution)/shard_map/ppermute | solution.py:46
  29.6 3.9 %down_maps.12 = (s32[1,1]{1,0:T(1,128)}, f32[336,128]{1,0:T(8,128)S(1)}, f32[336,128]{1,0:T(8,128)S(1)}) custom-call(s32[3]{0:T(128)S(1)} %pad_add_fusion.1.where_ref, bf16[2048,2048]{1,0:T(8,128)(2,1)S(1)} %get-tuple-element.402.weight_ref, bf16[112,2048]{1,0:T(8,128)(2,1)S(1)} %collective-permute-done.12.refs_0_.refs_1_, ...), custom_call_target="tpu_custom_call" | custom-call | flops 2818572 | bytes 9764 | tf_op jit(solution)/shard_map/down_maps/pallas_call | solution.py:315
  33.5 4.9 %collective-permute-done.11.refs_0_ = bf16[64,2048]{1,0:T(8,128)(2,1)} collective-permute-done((bf16[64,2048]{1,0:T(8,128)(2,1)}, bf16[64,2048]{1,0:T(8,128)(2,1)}, u32[]{:S(2)}, u32[]{:S(2)}) %collective-permute-start.11) | collective-permute-done | bytes 262176 | tf_op jit(solution)/shard_map/ppermute | solution.py:46
  38.5 3.5 %down_maps.13 = (s32[1,1]{1,0:T(1,128)}, f32[448,128]{1,0:T(8,128)S(1)}, f32[224,128]{1,0:T(8,128)S(1)}, bf16[224,128]{1,0:T(8,128)(2,1)S(1)}, bf16[224,128]{1,0...) custom-call(s32[3]{0:T(128)S(1)} %pad_add_fusion.1.where_ref, bf16[2048,2048]{1,0:T(8,128)(2,1)S(1)} %get-tuple-element.402.weight_ref, ...), custom_call_target="tpu_custom_call" | custom-call | flops 5637144576 | bytes 53084160 | tf_op jit(solution)/shard_map/down_maps/pallas_call | solution.py:315
  42.0 1.6 %collective-permute-start.17 = (bf16[224,128]{1,0:T(8,128)(2,1)S(1)}, bf16[224,128]{1,0:T(8,128)(2,1)S(1)}, u32[]{:S(2)}, u32[]{:S(2)}) collective-permute-start(bf16[224,128]{1,0:T(8,128)(2,1)S(1)} %get-tuple-element.416), channel_id=1, source_target_pairs={{0,2},{1,3},{2,0},{3,1},{4,6},{5,7},{6,4},{7,5},{8,10},{9,11},{10,... | collective-permute-start | bytes 172040 | tf_op jit(solution)/shard_map/ppermute | solution.py:46
  43.9 2.5 %collective-permute-done.17.refs_2_ = bf16[224,128]{1,0:T(8,128)(2,1)S(1)} collective-permute-done((bf16[224,128]{1,0:T(8,128)(2,1)S(1)}, bf16[224,128]{1,0:T(8,128)(2,1)S(1)}, u32[]{:S(2)}, u32[]{:S(2)}) %collective-permute-start.17) | collective-permute-done | bytes 57376 | tf_op jit(solution)/shard_map/ppermute | solution.py:46
  46.4 1.1 %collective-permute-done.18.refs_3_ = bf16[224,128]{1,0:T(8,128)(2,1)S(1)} collective-permute-done((bf16[224,128]{1,0:T(8,128)(2,1)S(1)}, bf16[224,128]{1,0:T(8,128)(2,1)S(1)}, u32[]{:S(2)}, u32[]{:S(2)}) %collective-permute-start.18) | collective-permute-done | bytes 57376 | tf_op jit(solution)/shard_map/ppermute | solution.py:46
  48.1 3.0 %collective-permute-start.19 = (bf16[112,512]{1,0:T(8,128)(2,1)S(1)}, bf16[112,512]{1,0:T(8,128)(2,1)S(1)}, u32[]{:S(2)}, u32[]{:S(2)}) collective-permute-start(bf16[112,512]{1,0:T(8,128)(2,1)S(1)} %get-tuple-element.419), channel_id=1, source_target_pairs={{0,12},{4,8},{8,4},{12,0},{1,13},{5,9},{9,5},{13,1},{2,14},{6,10},... | collective-permute-start | bytes 344072 | tf_op jit(solution)/shard_map/ppermute | solution.py:46
  51.2 1.4 %collective-permute-start.21 = (bf16[112,512]{1,0:T(8,128)(2,1)S(1)}, bf16[112,512]{1,0:T(8,128)(2,1)S(1)}, u32[]{:S(2)}, u32[]{:S(2)}) collective-permute-start(bf16[112,512]{1,0:T(8,128)(2,1)S(1)} %get-tuple-element.421), channel_id=1, source_target_pairs={{0,4},{4,0},{8,12},{12,8},{1,5},{5,1},{9,13},{13,9},{2,6},{6,2},{1... | collective-permute-start | bytes 344072 | tf_op jit(solution)/shard_map/ppermute | solution.py:46
  53.3 6.1 %conditional.6 = (f32[256,512]{1,0:T(8,128)S(1)}) conditional(s32[]{:T(128)} %bitcast.8, () %tuple.75, (bf16[256,2048]{1,0:T(8,128)(2,1)}, s32[3]{0:T(128)S(1)}, bf16[8192,512]{1,0:T(8,128)(2,1)}, f32[256,512]{1,0:T(8,128)S(1)}) %tuple.78), branch_computations={%region_4.0_spmd, %region_5.0_spmd} | conditional | flops 1073740 | bytes 4200642 | solution.py:517
  53.4 3.2 %shared_projection.4.refs_2_ = f32[256,512]{1,0:T(8,128)S(1)} custom-call(s32[3]{0:T(128)S(1)} %get-tuple-element.295.where_ref, bf16[256,2048]{1,0:T(8,128)(2,1)} %get-tuple-element.296.refs_0_, bf16[8192,512]{1,0:T(8,128)(2,1)} %get-tuple-element.297.refs_1_, f32[256,512]{1,0:T(8,128)S(1)} %get-tuple-element.298.refs_2_), custom_call_target="tpu_custom_call" | custom-call | flops 536870 | bytes 3145 | tf_op jit(solution)/shard_map/cond/branch_1_fun/shared_projection/pallas_call | solution.py:392
  56.6 2.8 %shared_projection.5 = f32[256,512]{1,0:T(8,128)S(1)} custom-call(s32[3]{0:T(128)S(1)} %get-tuple-element.295.where_ref, bf16[256,2048]{1,0:T(8,128)(2,1)S(1)} %collective-permute-done.1.refs_0_, bf16[8192,512]{1,0:T(8,128)(2,1)} %get-tuple-element.297.refs_1_, f32[256,512]{1,0:T(8,128)S(1)} %shared_projection.4.refs_2_), custom_call_target="tpu_custom_call" | custom-call | flops 536870 | bytes 3145 | tf_op jit(solution)/shard_map/cond/branch_1_fun/shared_projection/pallas_call | solution.py:392
  59.4 2.0 %collective-permute-done.20 = bf16[112,512]{1,0:T(8,128)(2,1)S(1)} collective-permute-done((bf16[112,512]{1,0:T(8,128)(2,1)S(1)}, bf16[112,512]{1,0:T(8,128)(2,1)S(1)}, u32[]{:S(2)}, u32[]{:S(2)}) %collective-permute-start.20) | collective-permute-done | bytes 114720 | tf_op jit(solution)/shard_map/ppermute | solution.py:46
  61.5 1.2 %conditional.7 = (bf16[256,512]{1,0:T(8,128)(2,1)}) conditional(s32[]{:T(128)} %bitcast.10, (f32[256,512]{1,0:T(8,128)S(1)}, f32[256,128]{1,0:T(8,128)S(1)}, bf16[112,512]{1,0:T(8,128)(2,1)S(1)}, bf16[112,512]{1,0:T(8,128)(2,1)S(1)}, bf16[112,512]{1,0:T(8,128)(2,1)S(1)}, /*index=5*/bf16[112,512]{1,0:T(8,128)(2,1)S(1)}) %tuple.79, ...), branch_computations={%region_6.0_spmd, %region_7.0_spmd} | conditional | flops 1624249 | bytes 73226744 | solution.py:597
  61.5 1.0 %join_corrections.7 = bf16[256,512]{1,0:T(8,128)(2,1)} custom-call(f32[256,512]{1,0:T(8,128)S(1)} %get-tuple-element.299.base_ref, f32[256,128]{1,0:T(8,128)S(1)} %get-tuple-element.300.place_ref, bf16[112,512]{1,0:T(8,128)(2,1)S(1)} %get-tuple-element.301.refs_0_, bf16[112,512]{1,0:T(8,128)(2,1)S(1)} %get-tuple-element.302.refs_1_, ...), custom_call_target="tpu_custom_call" | custom-call | flops 117440 | bytes 1245 | tf_op jit(solution)/shard_map/cond/branch_0_fun/join_corrections/pallas_call | solution.py:437
  (23 shorter events, 2.1 us)
Async XLA Ops:
  2.5 21.4 %collective-permute-start.12 = (bf16[112,2048]{1,0:T(8,128)(2,1)S(1)}, bf16[112,2048]{1,0:T(8,128)(2,1)S(1)}, u32[]{:S(2)}, u32[]{:S(2)}) collective-permute-start(bf16[112,2048]{1,0:T(8,128)(2,1)S(1)} %get-tuple-element.389), channel_id=1, source_target_pairs={{0,12},{4,8},{8,4},{12,0},{1,13},{5,9},{9,5},{13,1},{2,14},{6,10},... | collective-permute-start | bytes 1376264 | tf_op jit(solution)/shard_map/ppermute | solution.py:46
  10.7 18.9 %collective-permute-start.14 = (bf16[112,2048]{1,0:T(8,128)(2,1)S(1)}, bf16[112,2048]{1,0:T(8,128)(2,1)S(1)}, u32[]{:S(2)}, u32[]{:S(2)}) collective-permute-start(bf16[112,2048]{1,0:T(8,128)(2,1)S(1)} %get-tuple-element.392), channel_id=1, source_target_pairs={{0,4},{4,0},{8,12},{12,8},{1,5},{5,1},{9,13},{13,9},{2,6},{6,2},{1... | collective-permute-start | bytes 1376264 | tf_op jit(solution)/shard_map/ppermute | solution.py:46
  13.8 39.5 %collective-permute-start.15 = (bf16[256,2048]{1,0:T(8,128)(2,1)}, bf16[256,2048]{1,0:T(8,128)(2,1)}, u32[]{:S(2)}, u32[]{:S(2)}) collective-permute-start(bf16[256,2048]{1,0:T(8,128)(2,1)} %act_ref.2), channel_id=1, source_target_pairs={{0,2},{1,3},{2,0},{3,1},{4,6},{5,7},{6,4},{7,5},{8,10},{9,11},{10,... | collective-permute-start | bytes 3145736 | tf_op jit(solution)/shard_map/ppermute | solution.py:46
  15.4 23.1 %collective-permute-start.11 = (bf16[64,2048]{1,0:T(8,128)(2,1)}, bf16[64,2048]{1,0:T(8,128)(2,1)}, u32[]{:S(2)}, u32[]{:S(2)}) collective-permute-start(bf16[64,2048]{1,0:T(8,128)(2,1)} %get-tuple-element.391), channel_id=1, source_target_pairs={{0,8},{4,12},{8,0},{12,4},{1,9},{5,13},{9,1},{13,5},{2,10},{6,14},... | collective-permute-start | bytes 786440 | tf_op jit(solution)/shard_map/ppermute | solution.py:46
  16.1 3.9 %collective-permute-start = (bf16[256,2048]{1,0:T(8,128)(2,1)}, bf16[256,2048]{1,0:T(8,128)(2,1)S(1)}, u32[]{:S(2)}, u32[]{:S(2)}) collective-permute-start(bf16[256,2048]{1,0:T(8,128)(2,1)} %get-tuple-element.289.refs_0_), channel_id=1, source_target_pairs={{0,1},{1,0},{2,3},{3,2},{4,5},{5,4},{6,7},{7,6},{8,9},{9,8},{10,11... | collective-permute-start | bytes 3145736 | tf_op jit(solution)/shard_map/cond/branch_1_fun/ppermute | solution.py:46
  23.9 14.5 %collective-permute-start.13 = (bf16[48,2048]{1,0:T(8,128)(2,1)S(1)}, bf16[48,2048]{1,0:T(8,128)(2,1)S(1)}, u32[]{:S(2)}, u32[]{:S(2)}) collective-permute-start(bf16[48,2048]{1,0:T(8,128)(2,1)S(1)} %slice.3), channel_id=1, source_target_pairs={{0,4},{4,0},{8,12},{12,8},{1,5},{5,1},{9,13},{13,9},{2,6},{6,2},{1... | collective-permute-start | bytes 589832 | tf_op jit(solution)/shard_map/ppermute | solution.py:46
  41.9 1.9 %collective-permute-start.16 = (bf16[224,128]{1,0:T(8,128)(2,1)S(1)}, bf16[224,128]{1,0:T(8,128)(2,1)S(1)}, u32[]{:S(2)}, u32[]{:S(2)}) collective-permute-start(bf16[224,128]{1,0:T(8,128)(2,1)S(1)} %get-tuple-element.415), channel_id=1, source_target_pairs={{0,1},{1,0},{2,3},{3,2},{4,5},{5,4},{6,7},{7,6},{8,9},{9,8},{10,11... | collective-permute-start | bytes 172040 | tf_op jit(solution)/shard_map/ppermute | solution.py:46
  42.0 4.3 %collective-permute-start.17 = (bf16[224,128]{1,0:T(8,128)(2,1)S(1)}, bf16[224,128]{1,0:T(8,128)(2,1)S(1)}, u32[]{:S(2)}, u32[]{:S(2)}) collective-permute-start(bf16[224,128]{1,0:T(8,128)(2,1)S(1)} %get-tuple-element.416), channel_id=1, source_target_pairs={{0,2},{1,3},{2,0},{3,1},{4,6},{5,7},{6,4},{7,5},{8,10},{9,11},{10,... | collective-permute-start | bytes 172040 | tf_op jit(solution)/shard_map/ppermute | solution.py:46
  43.6 3.9 %collective-permute-start.18 = (bf16[224,128]{1,0:T(8,128)(2,1)S(1)}, bf16[224,128]{1,0:T(8,128)(2,1)S(1)}, u32[]{:S(2)}, u32[]{:S(2)}) collective-permute-start(bf16[224,128]{1,0:T(8,128)(2,1)S(1)} %get-tuple-element.417), channel_id=1, source_target_pairs={{0,3},{1,2},{2,1},{3,0},{4,7},{5,6},{6,5},{7,4},{8,11},{9,10},{10,... | collective-permute-start | bytes 172040 | tf_op jit(solution)/shard_map/ppermute | solution.py:46
  48.1 11.3 %collective-permute-start.19 = (bf16[112,512]{1,0:T(8,128)(2,1)S(1)}, bf16[112,512]{1,0:T(8,128)(2,1)S(1)}, u32[]{:S(2)}, u32[]{:S(2)}) collective-permute-start(bf16[112,512]{1,0:T(8,128)(2,1)S(1)} %get-tuple-element.419), channel_id=1, source_target_pairs={{0,12},{4,8},{8,4},{12,0},{1,13},{5,9},{9,5},{13,1},{2,14},{6,10},... | collective-permute-start | bytes 344072 | tf_op jit(solution)/shard_map/ppermute | solution.py:46
  51.2 10.3 %collective-permute-start.20 = (bf16[112,512]{1,0:T(8,128)(2,1)S(1)}, bf16[112,512]{1,0:T(8,128)(2,1)S(1)}, u32[]{:S(2)}, u32[]{:S(2)}) collective-permute-start(bf16[112,512]{1,0:T(8,128)(2,1)S(1)} %get-tuple-element.420), channel_id=1, source_target_pairs={{0,8},{4,12},{8,0},{12,4},{1,9},{5,13},{9,1},{13,5},{2,10},{6,14},... | collective-permute-start | bytes 344072 | tf_op jit(solution)/shard_map/ppermute | solution.py:46
  51.2 10.3 %collective-permute-start.21 = (bf16[112,512]{1,0:T(8,128)(2,1)S(1)}, bf16[112,512]{1,0:T(8,128)(2,1)S(1)}, u32[]{:S(2)}, u32[]{:S(2)}) collective-permute-start(bf16[112,512]{1,0:T(8,128)(2,1)S(1)} %get-tuple-element.421), channel_id=1, source_target_pairs={{0,4},{4,0},{8,12},{12,8},{1,5},{5,1},{9,13},{13,9},{2,6},{6,2},{1... | collective-permute-start | bytes 344072 | tf_op jit(solution)/shard_map/ppermute | solution.py:46
  53.3 8.2 %copy-start.3 = (s32[256,1]{0,1:T(1,128)S(1)}, s32[256,1]{0,1:T(1,128)}, u32[]{:S(2)}) copy-start(s32[256,1]{0,1:T(1,128)} %param.17) | copy-start | bytes 3076
  53.3 8.2 %copy-start.4 = (s32[64]{0:T(128)S(1)}, s32[64]{0:T(128)}, u32[]{:S(2)}) copy-start(s32[64]{0:T(128)} %param.18) | copy-start | bytes 772
  53.3 3.3 %collective-permute-start.1 = (bf16[256,2048]{1,0:T(8,128)(2,1)}, bf16[256,2048]{1,0:T(8,128)(2,1)S(1)}, u32[]{:S(2)}, u32[]{:S(2)}) collective-permute-start(bf16[256,2048]{1,0:T(8,128)(2,1)} %get-tuple-element.296.refs_0_), channel_id=1, source_target_pairs={{0,1},{1,0},{2,3},{3,2},{4,5},{5,4},{6,7},{7,6},{8,9},{9,8},{10,11... | collective-permute-start | bytes 3145736 | tf_op jit(solution)/shard_map/cond/branch_1_fun/ppermute | solution.py:46

commit v6 on v4

--- a/solution.py
+++ b/solution.py
@@ -38,7 +38,7 @@
 
 
 def answer_order(early, rest):
-    return sorted(early + rest, key=lambda entry: (-entry[0], entry[1]))
+    return sorted(early + rest, key=lambda entry: (-(entry[0] ^ 1), entry[1]))
 
 
 def swap(x, axis, k):

time: 63.2 us -> 62.3 us (0.986)
  starting transfers between devices: 19.6 us -> 18.8 us
    ppermute x13, starting transfers between devices: 19.6 us -> 18.8 us  [swap(): return lax.ppermute(x, axis, [(i, i ^ k) for i in range(size)])]
  transfers between devices with their start and end apart: 13 -> 13, of which waited for: 4 -> 5; matrix products, arithmetic and copies ran while one was open for 0% -> 0% of each run, Pallas kernels for 44% -> 44%
where the time goes in v6:
time: 62.3 us; the launch traced here: 62 us
  Pallas kernels  30.8 us (49%)
  starting transfers between devices  18.8 us (30%)
  waiting for transfers between devices  10.5 us (17%)
  between operations  1.49 us (2%)
    ppermute x13, starting transfers between devices, swap(): return lax.ppermute(x, axis, [(i, i ^ k) for i in range(size)])  18.8 us
    ppermute x13, waiting for transfers between devices, swap(): return lax.ppermute(x, axis, [(i, i ^ k) for i in range(size)])  10.5 us
    pallas_call x3, Pallas kernels, base(): pl.pallas_call(functools.partial(base_kernel, count), grid_spec=pltpu.Pre...  9.87 us
    pallas_call x3, Pallas kernels, pack(): pl.pallas_call(functools.partial(pack_kernel, local_count, wide_size, tur...  7.93 us
    pallas_call x2, Pallas kernels, down(): pl.pallas_call(functools.partial(down_kernel, views, cols, narrow_size, p...  7.4 us
    pallas_call x1, Pallas kernels, stage(): pl.pallas_call(stage_kernel, out_shape=[pltpu.VMEM((features, adapters *...  3.86 us
  transfers between devices with their start and end apart: 13, of which 5 were waited for; matrix products, arithmetic and copies ran while one was open for 0% of the time, Pallas kernels for 44%

profile of v6, /device:TPU:0, one launch (start us, length us, event | category | flops | bytes accessed | tf_op | source)
XLA Modules:
  0.0 62.0 jit_solution(14864952476659988750)
XLA Ops:
  0.1 2.4 %pack_rows.9 = (s32[1,1]{1,0:T(1,128)}, bf16[112,2048]{1,0:T(8,128)(2,1)S(1)}) custom-call(s32[3]{0:T(128)S(1)} %pad_add_fusion.1.where_ref, s32[1,256]{1,0:T(1,128)} %bitcast.21, s32[1,64]{1,0:T(1,128)} %bitcast.25, bf16[256,2048]{1,0:T(8,128)(2,1)} %act_ref.2), custom_call_target="tpu_custom_call" | custom-call | flops 117440 | bytes 1507 | tf_op jit(solution)/shard_map/pack_rows/pallas_call | solution.py:198
  2.5 5.1 %collective-permute-start.12 = (bf16[112,2048]{1,0:T(8,128)(2,1)S(1)}, bf16[112,2048]{1,0:T(8,128)(2,1)S(1)}, u32[]{:S(2)}, u32[]{:S(2)}) collective-permute-start(bf16[112,2048]{1,0:T(8,128)(2,1)S(1)} %get-tuple-element.389), channel_id=1, source_target_pairs={{0,12},{4,8},{8,4},{12,0},{1,13},{5,9},{9,5},{13,1},{2,14},{6,10},... | collective-permute-start | bytes 1376264 | tf_op jit(solution)/shard_map/ppermute | solution.py:46
  7.6 3.1 %pack_rows.10 = (s32[1,1]{1,0:T(1,128)}, bf16[64,2048]{1,0:T(8,128)(2,1)}, bf16[112,2048]{1,0:T(8,128)(2,1)S(1)}) custom-call(s32[3]{0:T(128)S(1)} %pad_add_fusion.1.where_ref, s32[1,256]{1,0:T(1,128)} %bitcast.22, s32[1,64]{1,0:T(1,128)} %bitcast.26, bf16[256,2048]{1,0:T(8,128)(2,1)} %act_ref.2), custom_call_target="tpu_custom_call" | custom-call | flops 184549 | bytes 1769 | tf_op jit(solution)/shard_map/pack_rows/pallas_call | solution.py:198
  11.3 2.5 %conditional.4 = (f32[256,128]{1,0:T(8,128)S(1)}, bf16[112,2048]{1,0:T(8,128)(2,1)S(1)}) conditional(s32[]{:T(128)} %bitcast.8, () %tuple.67, (s32[3]{0:T(128)S(1)}, s32[1,256]{1,0:T(1,128)}, s32[1,64]{1,0:T(1,128)}, bf16[256,2048]{1,0:T(8,128)(2,1)}) %tuple.107), branch_computations={%region_0.0_spmd, %region_1.0_spmd} | conditional | flops 117440 | bytes 589846 | solution.py:517
  11.4 2.4 %pack_rows.8 = (s32[1,1]{1,0:T(1,128)}, f32[256,128]{1,0:T(8,128)S(1)}, bf16[112,2048]{1,0:T(8,128)(2,1)S(1)}) custom-call(s32[3]{0:T(128)S(1)} %get-tuple-element.282.where_ref, s32[1,256]{1,0:T(1,128)} %get-tuple-element.283.tenant_ref, s32[1,64]{1,0:T(1,128)} %get-tuple-element.284.slot_ref, bf16[256,2048]{1,0:T(8,128)(2,1)} %get-tuple-element.285.act_ref), custom_call_target="tpu_custom_call" | custom-call | flops 117440 | bytes 1507 | tf_op jit(solution)/shard_map/cond/branch_1_fun/pack_rows/pallas_call | solution.py:198
  13.8 1.6 %collective-permute-start.15 = (bf16[256,2048]{1,0:T(8,128)(2,1)}, bf16[256,2048]{1,0:T(8,128)(2,1)}, u32[]{:S(2)}, u32[]{:S(2)}) collective-permute-start(bf16[256,2048]{1,0:T(8,128)(2,1)} %act_ref.2), channel_id=1, source_target_pairs={{0,2},{1,3},{2,0},{3,1},{4,6},{5,7},{6,4},{7,5},{8,10},{9,11},{10,... | collective-permute-start | bytes 3145736 | tf_op jit(solution)/shard_map/ppermute | solution.py:46
  16.1 7.8 %conditional.5 = (f32[256,512]{1,0:T(8,128)S(1)}, bf16[2048,2048]{1,0:T(8,128)(2,1)S(1)}, bf16[1024,512]{1,0:T(8,128)(2,1)S(1)}) conditional(s32[]{:T(128)} %bitcast.8, () %tuple.64, (bf16[256,2048]{1,0:T(8,128)(2,1)}, s32[3]{0:T(128)S(1)}, bf16[8192,512]{1,0:T(8,128)(2,1)}, bf16[16,2048,128]{2,1,0:T(8,128)(2,1)}, bf16[1024,512]{1,0:T(8,128)(2,1)}) %tuple.103), branch_computations={%region_2.0_spmd, %region_3.0_spmd} | conditional | flops 1073741 | bytes 9961504 | solution.py:517
  16.1 3.9 %stage_maps.4 = (bf16[2048,2048]{1,0:T(8,128)(2,1)S(1)}, bf16[1024,512]{1,0:T(8,128)(2,1)S(1)}) custom-call(bf16[16,2048,128]{2,1,0:T(8,128)(2,1)} %get-tuple-element.291.down_ref, bf16[1024,512]{1,0:T(8,128)(2,1)} %get-tuple-element.292.up_ref), custom_call_target="tpu_custom_call" | custom-call | tf_op jit(solution)/shard_map/cond/branch_1_fun/stage_maps/pallas_call | solution.py:232
  20.0 3.9 %shared_projection.3 = f32[256,512]{1,0:T(8,128)S(1)} custom-call(s32[3]{0:T(128)S(1)} %get-tuple-element.288.where_ref, bf16[256,2048]{1,0:T(8,128)(2,1)} %get-tuple-element.289.refs_0_, bf16[256,2048]{1,0:T(8,128)(2,1)S(1)} %collective-permute-done.refs_1_, bf16[8192,512]{1,0:T(8,128)(2,1)} %get-tuple-element.290.refs_2_), custom_call_target="tpu_custom_call" | custom-call | flops 1073741 | bytes 6291 | tf_op jit(solution)/shard_map/cond/branch_1_fun/shared_projection/pallas_call | solution.py:392
  23.9 5.7 %collective-permute-start.13 = (bf16[48,2048]{1,0:T(8,128)(2,1)S(1)}, bf16[48,2048]{1,0:T(8,128)(2,1)S(1)}, u32[]{:S(2)}, u32[]{:S(2)}) collective-permute-start(bf16[48,2048]{1,0:T(8,128)(2,1)S(1)} %slice.3), channel_id=1, source_target_pairs={{0,4},{4,0},{8,12},{12,8},{1,5},{5,1},{9,13},{13,9},{2,6},{6,2},{1... | collective-permute-start | bytes 589832 | tf_op jit(solution)/shard_map/ppermute | solution.py:46
  29.6 3.9 %down_maps.12 = (s32[1,1]{1,0:T(1,128)}, f32[336,128]{1,0:T(8,128)S(1)}, f32[336,128]{1,0:T(8,128)S(1)}) custom-call(s32[3]{0:T(128)S(1)} %pad_add_fusion.1.where_ref, bf16[2048,2048]{1,0:T(8,128)(2,1)S(1)} %get-tuple-element.402.weight_ref, bf16[112,2048]{1,0:T(8,128)(2,1)S(1)} %collective-permute-done.12.refs_0_.refs_1_, ...), custom_call_target="tpu_custom_call" | custom-call | flops 2818572 | bytes 9764 | tf_op jit(solution)/shard_map/down_maps/pallas_call | solution.py:315
  33.5 4.9 %collective-permute-done.11.refs_0_ = bf16[64,2048]{1,0:T(8,128)(2,1)} collective-permute-done((bf16[64,2048]{1,0:T(8,128)(2,1)}, bf16[64,2048]{1,0:T(8,128)(2,1)}, u32[]{:S(2)}, u32[]{:S(2)}) %collective-permute-start.11) | collective-permute-done | bytes 262176 | tf_op jit(solution)/shard_map/ppermute | solution.py:46
  38.5 3.5 %down_maps.13 = (s32[1,1]{1,0:T(1,128)}, f32[448,128]{1,0:T(8,128)S(1)}, f32[224,128]{1,0:T(8,128)S(1)}, bf16[224,128]{1,0:T(8,128)(2,1)S(1)}, bf16[224,128]{1,0...) custom-call(s32[3]{0:T(128)S(1)} %pad_add_fusion.1.where_ref, bf16[2048,2048]{1,0:T(8,128)(2,1)S(1)} %get-tuple-element.402.weight_ref, ...), custom_call_target="tpu_custom_call" | custom-call | flops 5637144576 | bytes 53084160 | tf_op jit(solution)/shard_map/down_maps/pallas_call | solution.py:315
  42.0 1.6 %collective-permute-start.17 = (bf16[224,128]{1,0:T(8,128)(2,1)S(1)}, bf16[224,128]{1,0:T(8,128)(2,1)S(1)}, u32[]{:S(2)}, u32[]{:S(2)}) collective-permute-start(bf16[224,128]{1,0:T(8,128)(2,1)S(1)} %get-tuple-element.416), channel_id=1, source_target_pairs={{0,2},{1,3},{2,0},{3,1},{4,6},{5,7},{6,4},{7,5},{8,10},{9,11},{10,... | collective-permute-start | bytes 172040 | tf_op jit(solution)/shard_map/ppermute | solution.py:46
  43.9 2.5 %collective-permute-done.17.refs_2_ = bf16[224,128]{1,0:T(8,128)(2,1)S(1)} collective-permute-done((bf16[224,128]{1,0:T(8,128)(2,1)S(1)}, bf16[224,128]{1,0:T(8,128)(2,1)S(1)}, u32[]{:S(2)}, u32[]{:S(2)}) %collective-permute-start.17) | collective-permute-done | bytes 57376 | tf_op jit(solution)/shard_map/ppermute | solution.py:46
  46.4 1.1 %collective-permute-done.18.refs_3_ = bf16[224,128]{1,0:T(8,128)(2,1)S(1)} collective-permute-done((bf16[224,128]{1,0:T(8,128)(2,1)S(1)}, bf16[224,128]{1,0:T(8,128)(2,1)S(1)}, u32[]{:S(2)}, u32[]{:S(2)}) %collective-permute-start.18) | collective-permute-done | bytes 57376 | tf_op jit(solution)/shard_map/ppermute | solution.py:46
  48.1 1.2 %collective-permute-start.19 = (bf16[112,512]{1,0:T(8,128)(2,1)S(1)}, bf16[112,512]{1,0:T(8,128)(2,1)S(1)}, u32[]{:S(2)}, u32[]{:S(2)}) collective-permute-start(bf16[112,512]{1,0:T(8,128)(2,1)S(1)} %get-tuple-element.419), channel_id=1, source_target_pairs={{0,8},{4,12},{8,0},{12,4},{1,9},{5,13},{9,1},{13,5},{2,10},{6,14},... | collective-permute-start | bytes 344072 | tf_op jit(solution)/shard_map/ppermute | solution.py:46
  49.3 2.5 %collective-permute-start.20 = (bf16[112,512]{1,0:T(8,128)(2,1)S(1)}, bf16[112,512]{1,0:T(8,128)(2,1)S(1)}, u32[]{:S(2)}, u32[]{:S(2)}) collective-permute-start(bf16[112,512]{1,0:T(8,128)(2,1)S(1)} %get-tuple-element.420), channel_id=1, source_target_pairs={{0,12},{4,8},{8,4},{12,0},{1,13},{5,9},{9,5},{13,1},{2,14},{6,10},... | collective-permute-start | bytes 344072 | tf_op jit(solution)/shard_map/ppermute | solution.py:46
  52.5 6.1 %conditional.6 = (f32[256,512]{1,0:T(8,128)S(1)}) conditional(s32[]{:T(128)} %bitcast.8, () %tuple.75, (bf16[256,2048]{1,0:T(8,128)(2,1)}, s32[3]{0:T(128)S(1)}, bf16[8192,512]{1,0:T(8,128)(2,1)}, f32[256,512]{1,0:T(8,128)S(1)}) %tuple.78), branch_computations={%region_4.0_spmd, %region_5.0_spmd} | conditional | flops 1073740 | bytes 4200642 | solution.py:517
  52.6 3.2 %shared_projection.4.refs_2_ = f32[256,512]{1,0:T(8,128)S(1)} custom-call(s32[3]{0:T(128)S(1)} %get-tuple-element.295.where_ref, bf16[256,2048]{1,0:T(8,128)(2,1)} %get-tuple-element.296.refs_0_, bf16[8192,512]{1,0:T(8,128)(2,1)} %get-tuple-element.297.refs_1_, f32[256,512]{1,0:T(8,128)S(1)} %get-tuple-element.298.refs_2_), custom_call_target="tpu_custom_call" | custom-call | flops 536870 | bytes 3145 | tf_op jit(solution)/shard_map/cond/branch_1_fun/shared_projection/pallas_call | solution.py:392
  55.8 2.8 %shared_projection.5 = f32[256,512]{1,0:T(8,128)S(1)} custom-call(s32[3]{0:T(128)S(1)} %get-tuple-element.295.where_ref, bf16[256,2048]{1,0:T(8,128)(2,1)S(1)} %collective-permute-done.1.refs_0_, bf16[8192,512]{1,0:T(8,128)(2,1)} %get-tuple-element.297.refs_1_, f32[256,512]{1,0:T(8,128)S(1)} %shared_projection.4.refs_2_), custom_call_target="tpu_custom_call" | custom-call | flops 536870 | bytes 3145 | tf_op jit(solution)/shard_map/cond/branch_1_fun/shared_projection/pallas_call | solution.py:392
  58.6 1.4 %collective-permute-done.19 = bf16[112,512]{1,0:T(8,128)(2,1)S(1)} collective-permute-done((bf16[112,512]{1,0:T(8,128)(2,1)S(1)}, bf16[112,512]{1,0:T(8,128)(2,1)S(1)}, u32[]{:S(2)}, u32[]{:S(2)}) %collective-permute-start.19) | collective-permute-done | bytes 114720 | tf_op jit(solution)/shard_map/ppermute | solution.py:46
  60.6 1.2 %conditional.7 = (bf16[256,512]{1,0:T(8,128)(2,1)}) conditional(s32[]{:T(128)} %bitcast.10, (f32[256,512]{1,0:T(8,128)S(1)}, f32[256,128]{1,0:T(8,128)S(1)}, bf16[112,512]{1,0:T(8,128)(2,1)S(1)}, bf16[112,512]{1,0:T(8,128)(2,1)S(1)}, bf16[112,512]{1,0:T(8,128)(2,1)S(1)}, /*index=5*/bf16[112,512]{1,0:T(8,128)(2,1)S(1)}) %tuple.79, ...), branch_computations={%region_6.0_spmd, %region_7.0_spmd} | conditional | flops 1624249 | bytes 73226744 | solution.py:597
  60.6 1.0 %join_corrections.7 = bf16[256,512]{1,0:T(8,128)(2,1)} custom-call(f32[256,512]{1,0:T(8,128)S(1)} %get-tuple-element.299.base_ref, f32[256,128]{1,0:T(8,128)S(1)} %get-tuple-element.300.place_ref, bf16[112,512]{1,0:T(8,128)(2,1)S(1)} %get-tuple-element.301.refs_0_, bf16[112,512]{1,0:T(8,128)(2,1)S(1)} %get-tuple-element.302.refs_1_, ...), custom_call_target="tpu_custom_call" | custom-call | flops 117440 | bytes 1245 | tf_op jit(solution)/shard_map/cond/branch_0_fun/join_corrections/pallas_call | solution.py:437
  (23 shorter events, 2.7 us)
Async XLA Ops:
  2.5 21.4 %collective-permute-start.12 = (bf16[112,2048]{1,0:T(8,128)(2,1)S(1)}, bf16[112,2048]{1,0:T(8,128)(2,1)S(1)}, u32[]{:S(2)}, u32[]{:S(2)}) collective-permute-start(bf16[112,2048]{1,0:T(8,128)(2,1)S(1)} %get-tuple-element.389), channel_id=1, source_target_pairs={{0,12},{4,8},{8,4},{12,0},{1,13},{5,9},{9,5},{13,1},{2,14},{6,10},... | collective-permute-start | bytes 1376264 | tf_op jit(solution)/shard_map/ppermute | solution.py:46
  10.7 18.9 %collective-permute-start.14 = (bf16[112,2048]{1,0:T(8,128)(2,1)S(1)}, bf16[112,2048]{1,0:T(8,128)(2,1)S(1)}, u32[]{:S(2)}, u32[]{:S(2)}) collective-permute-start(bf16[112,2048]{1,0:T(8,128)(2,1)S(1)} %get-tuple-element.392), channel_id=1, source_target_pairs={{0,4},{4,0},{8,12},{12,8},{1,5},{5,1},{9,13},{13,9},{2,6},{6,2},{1... | collective-permute-start | bytes 1376264 | tf_op jit(solution)/shard_map/ppermute | solution.py:46
  13.8 38.6 %collective-permute-start.15 = (bf16[256,2048]{1,0:T(8,128)(2,1)}, bf16[256,2048]{1,0:T(8,128)(2,1)}, u32[]{:S(2)}, u32[]{:S(2)}) collective-permute-start(bf16[256,2048]{1,0:T(8,128)(2,1)} %act_ref.2), channel_id=1, source_target_pairs={{0,2},{1,3},{2,0},{3,1},{4,6},{5,7},{6,4},{7,5},{8,10},{9,11},{10,... | collective-permute-start | bytes 3145736 | tf_op jit(solution)/shard_map/ppermute | solution.py:46
  15.4 23.1 %collective-permute-start.11 = (bf16[64,2048]{1,0:T(8,128)(2,1)}, bf16[64,2048]{1,0:T(8,128)(2,1)}, u32[]{:S(2)}, u32[]{:S(2)}) collective-permute-start(bf16[64,2048]{1,0:T(8,128)(2,1)} %get-tuple-element.391), channel_id=1, source_target_pairs={{0,8},{4,12},{8,0},{12,4},{1,9},{5,13},{9,1},{13,5},{2,10},{6,14},... | collective-permute-start | bytes 786440 | tf_op jit(solution)/shard_map/ppermute | solution.py:46
  16.1 3.9 %collective-permute-start = (bf16[256,2048]{1,0:T(8,128)(2,1)}, bf16[256,2048]{1,0:T(8,128)(2,1)S(1)}, u32[]{:S(2)}, u32[]{:S(2)}) collective-permute-start(bf16[256,2048]{1,0:T(8,128)(2,1)} %get-tuple-element.289.refs_0_), channel_id=1, source_target_pairs={{0,1},{1,0},{2,3},{3,2},{4,5},{5,4},{6,7},{7,6},{8,9},{9,8},{10,11... | collective-permute-start | bytes 3145736 | tf_op jit(solution)/shard_map/cond/branch_1_fun/ppermute | solution.py:46
  23.9 14.5 %collective-permute-start.13 = (bf16[48,2048]{1,0:T(8,128)(2,1)S(1)}, bf16[48,2048]{1,0:T(8,128)(2,1)S(1)}, u32[]{:S(2)}, u32[]{:S(2)}) collective-permute-start(bf16[48,2048]{1,0:T(8,128)(2,1)S(1)} %slice.3), channel_id=1, source_target_pairs={{0,4},{4,0},{8,12},{12,8},{1,5},{5,1},{9,13},{13,9},{2,6},{6,2},{1... | collective-permute-start | bytes 589832 | tf_op jit(solution)/shard_map/ppermute | solution.py:46
  41.9 1.9 %collective-permute-start.16 = (bf16[224,128]{1,0:T(8,128)(2,1)S(1)}, bf16[224,128]{1,0:T(8,128)(2,1)S(1)}, u32[]{:S(2)}, u32[]{:S(2)}) collective-permute-start(bf16[224,128]{1,0:T(8,128)(2,1)S(1)} %get-tuple-element.415), channel_id=1, source_target_pairs={{0,1},{1,0},{2,3},{3,2},{4,5},{5,4},{6,7},{7,6},{8,9},{9,8},{10,11... | collective-permute-start | bytes 172040 | tf_op jit(solution)/shard_map/ppermute | solution.py:46
  42.0 4.3 %collective-permute-start.17 = (bf16[224,128]{1,0:T(8,128)(2,1)S(1)}, bf16[224,128]{1,0:T(8,128)(2,1)S(1)}, u32[]{:S(2)}, u32[]{:S(2)}) collective-permute-start(bf16[224,128]{1,0:T(8,128)(2,1)S(1)} %get-tuple-element.416), channel_id=1, source_target_pairs={{0,2},{1,3},{2,0},{3,1},{4,6},{5,7},{6,4},{7,5},{8,10},{9,11},{10,... | collective-permute-start | bytes 172040 | tf_op jit(solution)/shard_map/ppermute | solution.py:46
  43.6 3.9 %collective-permute-start.18 = (bf16[224,128]{1,0:T(8,128)(2,1)S(1)}, bf16[224,128]{1,0:T(8,128)(2,1)S(1)}, u32[]{:S(2)}, u32[]{:S(2)}) collective-permute-start(bf16[224,128]{1,0:T(8,128)(2,1)S(1)} %get-tuple-element.417), channel_id=1, source_target_pairs={{0,3},{1,2},{2,1},{3,0},{4,7},{5,6},{6,5},{7,4},{8,11},{9,10},{10,... | collective-permute-start | bytes 172040 | tf_op jit(solution)/shard_map/ppermute | solution.py:46
  48.1 11.9 %collective-permute-start.19 = (bf16[112,512]{1,0:T(8,128)(2,1)S(1)}, bf16[112,512]{1,0:T(8,128)(2,1)S(1)}, u32[]{:S(2)}, u32[]{:S(2)}) collective-permute-start(bf16[112,512]{1,0:T(8,128)(2,1)S(1)} %get-tuple-element.419), channel_id=1, source_target_pairs={{0,8},{4,12},{8,0},{12,4},{1,9},{5,13},{9,1},{13,5},{2,10},{6,14},... | collective-permute-start | bytes 344072 | tf_op jit(solution)/shard_map/ppermute | solution.py:46
  49.3 10.7 %collective-permute-start.20 = (bf16[112,512]{1,0:T(8,128)(2,1)S(1)}, bf16[112,512]{1,0:T(8,128)(2,1)S(1)}, u32[]{:S(2)}, u32[]{:S(2)}) collective-permute-start(bf16[112,512]{1,0:T(8,128)(2,1)S(1)} %get-tuple-element.420), channel_id=1, source_target_pairs={{0,12},{4,8},{8,4},{12,0},{1,13},{5,9},{9,5},{13,1},{2,14},{6,10},... | collective-permute-start | bytes 344072 | tf_op jit(solution)/shard_map/ppermute | solution.py:46
  51.8 8.8 %collective-permute-start.21 = (bf16[112,512]{1,0:T(8,128)(2,1)S(1)}, bf16[112,512]{1,0:T(8,128)(2,1)S(1)}, u32[]{:S(2)}, u32[]{:S(2)}) collective-permute-start(bf16[112,512]{1,0:T(8,128)(2,1)S(1)} %get-tuple-element.422), channel_id=1, source_target_pairs={{0,4},{4,0},{8,12},{12,8},{1,5},{5,1},{9,13},{13,9},{2,6},{6,2},{1... | collective-permute-start | bytes 344072 | tf_op jit(solution)/shard_map/ppermute | solution.py:46
  52.5 8.2 %copy-start.3 = (s32[256,1]{0,1:T(1,128)S(1)}, s32[256,1]{0,1:T(1,128)}, u32[]{:S(2)}) copy-start(s32[256,1]{0,1:T(1,128)} %param.17) | copy-start | bytes 3076
  52.5 8.2 %copy-start.4 = (s32[64]{0:T(128)S(1)}, s32[64]{0:T(128)}, u32[]{:S(2)}) copy-start(s32[64]{0:T(128)} %param.18) | copy-start | bytes 772
  52.5 3.3 %collective-permute-start.1 = (bf16[256,2048]{1,0:T(8,128)(2,1)}, bf16[256,2048]{1,0:T(8,128)(2,1)S(1)}, u32[]{:S(2)}, u32[]{:S(2)}) collective-permute-start(bf16[256,2048]{1,0:T(8,128)(2,1)} %get-tuple-element.296.refs_0_), channel_id=1, source_target_pairs={{0,1},{1,0},{2,3},{3,2},{4,5},{5,4},{6,7},{7,6},{8,9},{9,8},{10,11... | collective-permute-start | bytes 3145736 | tf_op jit(solution)/shard_map/cond/branch_1_fun/ppermute | solution.py:46
